TPU v7x, 128 devices: a whole 4x4x4 slice. The times are simulated.
128 devices in a mesh: seq: 32 (over z, x, core), head: 4 (over y).
Axes of the slice: x: 4, y: 4, z: 4, core: 2. Of those that a mesh axis runs over, the one named last changes fastest.
Arguments:
- inputs: bfloat16 [8192, 2048], P('seq'), may hold values from -6 to 6
- gain_first: float32 [2048], replicated, may hold values from 0.5 to 1.5
- w_query: bfloat16 [2048, 2048], P(None, 'head'), may hold values from -0.125 to 0.125
- a_query: bfloat16 [2048, 8], replicated, may hold values from -0.125 to 0.125
- b_query: bfloat16 [8, 2048], P(None, 'head'), may hold values from -2 to 2
- key_projection_weight: bfloat16 [2048, 512], P(None, 'head'), may hold values from -0.125 to 0.125
- a_key: bfloat16 [2048, 8], replicated, may hold values from -0.125 to 0.125
- key_adapter_second: bfloat16 [8, 512], P(None, 'head'), may hold values from -2 to 2
- value_projection_weight: bfloat16 [2048, 512], P(None, 'head'), may hold values from -0.125 to 0.125
- a_value: bfloat16 [2048, 8], replicated, may hold values from -0.125 to 0.125
- value_adapter_second: bfloat16 [8, 512], P(None, 'head'), may hold values from -2 to 2
- feature_query: bfloat16 [32, 64, 64], P('head'), may hold values from -0.75 to 0.75
- key_hedgehog_map: bfloat16 [8, 64, 64], P('head'), may hold values from -0.75 to 0.75
- w_out: bfloat16 [2048, 2048], P('head'), may hold values from -1 to 1
- a_out: bfloat16 [2048, 8], P('head'), may hold values from -1 to 1
- b_out: bfloat16 [8, 2048], replicated, may hold values from -2 to 2
- gain_second: float32 [2048], replicated, may hold values from 0.5 to 1.5
- w_gate: bfloat16 [2048, 8192], P(None, 'head'), may hold values from -0.125 to 0.125
- w_up: bfloat16 [2048, 8192], P(None, 'head'), may hold values from -0.125 to 0.125
- w_down: bfloat16 [8192, 2048], P('head'), may hold values from -0.0625 to 0.0625
- lengths: int32 [3], replicated, may hold values from 1 to 7936, as said below
- cotangent: bfloat16 [8192, 2048], P('seq'), may hold values from -6 to 6
Outputs:
- block_out: bfloat16 [8192, 2048], P('seq', 'head')
- grad_inputs: float32 [8192, 2048], P('seq', 'head')
- grad_gain_first: float32 [2048], P('head')
- grad_w_query: float32 [2048, 2048], P('seq', 'head')
- grad_a_query: float32 [2048, 8], replicated
- grad_b_query: float32 [8, 2048], P(None, 'head')
- grad_w_key: float32 [2048, 512], P('seq', 'head')
- grad_a_key: float32 [2048, 8], replicated
- grad_b_key: float32 [8, 512], P(None, 'head')
- grad_w_value: float32 [2048, 512], P('seq', 'head')
- grad_a_value: float32 [2048, 8], replicated
- grad_b_value: float32 [8, 512], P(None, 'head')
- grad_feature_query: float32 [32, 64, 64], P('head')
- grad_feature_key: float32 [8, 64, 64], P('head')
- grad_w_out: float32 [2048, 2048], P('head', 'seq')
- grad_a_out: float32 [2048, 8], P('head')
- grad_b_out: float32 [8, 2048], replicated
- grad_gain_second: float32 [2048], P('head')
- grad_w_gate: float32 [2048, 8192], P('seq', 'head')
- grad_w_up: float32 [2048, 8192], P('seq', 'head')
- grad_w_down: float32 [8192, 2048], P('head', 'seq')
Inputs may be any that keep to these rules, and one draw needn't show every extreme that they name: Three documents in order whose lengths sum to 8192; the first and the last together hold 256 tokens, so the second starts on the first device of seq and ends on the last.
All inputs are finite; a program needn't handle non-finite values.
Results may differ from a plain program's by a relative error of at most 0.014.
The roundings to bfloat16 on the way count: a program that leaves them out, or rounds other values in their place, can miss the bound.
Values may be sent and summed in bfloat16 or wider, within the bound.
A program may use at most 256 MiB of HBM per device.

v0:
```python
import jax
import jax.numpy as jnp
from jax import lax
from jax.sharding import PartitionSpec as P

WINDOW = 64


EPS = 1e-05
NEG = -1e30
HIGH = lax.Precision.HIGHEST


def passed_along(value, axis, steps):
    count = lax.axis_size(axis)
    leading, last = (max(0, -steps), min(count, count - steps))
    return lax.ppermute(value, axis, [(source, source + steps) for source in range(leading, last)])


def entering(part, axis, combine, identity, reverse):
    count = lax.axis_size(axis)
    place = lax.axis_index(axis)
    ahead = count - 1 - place if reverse else place
    gathered = jax.tree.map(lambda a: lax.all_gather(a, axis), part)
    state = jax.tree.map(lambda a, e: jnp.zeros_like(a) + jnp.asarray(e, a.dtype), part, identity)

    def one(turn, state):
        source = count - 1 - turn if reverse else turn
        return combine(
            state, jax.tree.map(lambda a: lax.dynamic_index_in_dim(a, source, 0, False), gathered)
        )

    return lax.fori_loop(0, ahead, one, state)


def dot_plain(left_side, right_side):
    return jnp.dot(left_side, right_side, preferred_element_type=jnp.float32)


def by_transpose(left_side, right_side):
    return lax.dot_general(
        left_side, right_side, (((1,), (1,)), ((), ())), preferred_element_type=jnp.float32
    )


def by_transpose_exact(left_side, right_side):
    return lax.dot_general(
        left_side,
        right_side.astype(jnp.float32),
        (((1,), (1,)), ((), ())),
        precision=HIGH,
        preferred_element_type=jnp.float32,
    )


def transpose_by(left_side, right_side):
    return lax.dot_general(
        left_side, right_side, (((0,), (0,)), ((), ())), preferred_element_type=jnp.float32
    )


def transpose_by_exact(left_side, right_side):
    return lax.dot_general(
        left_side.astype(jnp.float32),
        right_side,
        (((0,), (0,)), ((), ())),
        precision=HIGH,
        preferred_element_type=jnp.float32,
    )


def rms_scale(values):
    return lax.rsqrt(jnp.mean(values * values, axis=-1, keepdims=True) + EPS)


def norm_back(grad_normed, values, factor, gain_vector):
    weighted = grad_normed * gain_vector
    return factor * weighted - values * factor * factor * factor * jnp.mean(
        weighted * values, axis=-1, keepdims=True
    )


def feature_map(inputs, feature_table):
    logits = jnp.einsum("hnd,hde->hne", inputs, feature_table, preferred_element_type=jnp.float32)
    return jnp.concatenate(
        [jax.nn.softmax(logits, axis=-1), jax.nn.softmax(-logits, axis=-1)], axis=-1
    ).astype(jnp.bfloat16)


def feature_back(inputs, feature_table, grad_phi):
    logits = jnp.einsum("hnd,hde->hne", inputs, feature_table, preferred_element_type=jnp.float32)
    half_width = logits.shape[-1]
    upper_soft = jax.nn.softmax(logits, axis=-1)
    lower_soft = jax.nn.softmax(-logits, axis=-1)
    grad_upper = grad_phi[..., :half_width]
    grad_lower = grad_phi[..., half_width:]
    grad_logits = upper_soft * (
        grad_upper - jnp.sum(upper_soft * grad_upper, axis=-1, keepdims=True)
    ) - lower_soft * (grad_lower - jnp.sum(lower_soft * grad_lower, axis=-1, keepdims=True))
    grad_inputs = jnp.einsum(
        "hne,hde->hnd", grad_logits, feature_table.astype(jnp.float32), precision=HIGH
    )
    grad_table = jnp.einsum("hnd,hne->hde", inputs.astype(jnp.float32), grad_logits, precision=HIGH)
    return (grad_inputs, grad_table)


def doc_of(positions, starts):
    return jnp.sum((starts[None, :] <= positions[:, None]).astype(jnp.int32), axis=1) - 1


def geometry(first_pos, row_count, starts):
    query_pos = first_pos + jnp.arange(row_count, dtype=jnp.int32)
    key_pos = first_pos - WINDOW + jnp.arange(row_count + WINDOW, dtype=jnp.int32)
    query_doc = doc_of(query_pos, starts)
    key_doc = doc_of(key_pos, starts)
    offset = query_pos[:, None] - key_pos[None, :]
    same_doc = query_doc[:, None] == key_doc[None, :]
    within = same_doc & (offset >= 0) & (offset < WINDOW)
    beyond = same_doc & (offset >= WINDOW)
    carry_on = (query_doc == doc_of(query_pos[:1] - WINDOW - 1, starts)[0]).astype(jnp.float32)
    keeping = (key_doc[:row_count] == key_doc[row_count - 1]).astype(jnp.float32)
    resets = jnp.any((starts >= key_pos[0]) & (starts <= key_pos[row_count - 1])).astype(
        jnp.float32
    )
    return (within, beyond, carry_on, keeping, resets)


def segment_join(earlier, later_part):
    passing = 1.0 - later_part[2]
    return (
        later_part[0] + passing * earlier[0],
        later_part[1] + passing * earlier[1],
        jnp.maximum(earlier[2], later_part[2]),
    )


def attend(query_group, phi_group, keys_all, phi_keys, values_all, prefix, layout):
    within, beyond, carry_on = layout
    factor = query_group.shape[-1] ** (-0.5)
    scores = (
        jnp.einsum("kgrd,kcd->kgrc", query_group, keys_all, preferred_element_type=jnp.float32)
        * factor
    )
    masked = jnp.where(within, scores, NEG)
    maxima = jnp.max(masked, axis=-1, keepdims=True)
    weights_near = jnp.exp(masked - maxima)
    damping = jnp.exp(-maxima)
    linear = jnp.einsum("kgrf,kcf->kgrc", phi_group, phi_keys, preferred_element_type=jnp.float32)
    weights_far = jnp.where(beyond, linear, 0.0) * damping
    gating = damping[..., 0] * carry_on
    phi_float = phi_group.astype(jnp.float32)
    numerator = (
        jnp.einsum(
            "kgrc,kcd->kgrd",
            weights_near.astype(jnp.bfloat16),
            values_all,
            preferred_element_type=jnp.float32,
        )
        + jnp.einsum("kgrc,kcd->kgrd", weights_far, values_all.astype(jnp.float32), precision=HIGH)
        + gating[..., None] * jnp.einsum("kgrf,kfd->kgrd", phi_float, prefix[0], precision=HIGH)
    )
    denominator = (
        jnp.sum(weights_near, axis=-1)
        + jnp.sum(weights_far, axis=-1)
        + gating * jnp.einsum("kgrf,kf->kgr", phi_float, prefix[1], precision=HIGH)
    )
    return (
        numerator / denominator[..., None],
        weights_near,
        weights_far,
        gating,
        denominator,
        damping,
    )


def body(
    inputs,
    gain_first,
    w_query,
    a_query,
    b_query,
    key_projection_weight,
    a_key,
    key_adapter_second,
    value_projection_weight,
    a_value,
    value_adapter_second,
    feature_query,
    key_hedgehog_map,
    w_out,
    a_out,
    b_out,
    gain_second,
    w_gate,
    w_up,
    w_down,
    lengths,
    cotangent,
):
    row_count = inputs.shape[0]
    model_width = inputs.shape[1]
    head_dim = feature_query.shape[-1]
    heads_of_queries = feature_query.shape[0]
    heads_of_keys = key_hedgehog_map.shape[0]
    group_count = heads_of_queries // heads_of_keys
    columns = model_width // lax.axis_size("head")
    column_at = lax.axis_index("head") * columns
    starts = jnp.cumsum(lengths) - lengths
    within, beyond, carry_on, keeping, resets = geometry(
        lax.axis_index("seq") * row_count, row_count, starts
    )
    layout = (within, beyond, carry_on)
    residual = inputs.astype(jnp.float32)
    scale_first = rms_scale(residual)
    normed = (residual * scale_first * gain_first).astype(jnp.bfloat16)
    low_query = dot_plain(normed, a_query).astype(jnp.bfloat16)
    low_key = dot_plain(normed, a_key).astype(jnp.bfloat16)
    low_value = dot_plain(normed, a_value).astype(jnp.bfloat16)
    queries = (dot_plain(normed, w_query) + dot_plain(low_query, b_query)).astype(jnp.bfloat16)
    keys_own = (
        dot_plain(normed, key_projection_weight) + dot_plain(low_key, key_adapter_second)
    ).astype(jnp.bfloat16)
    values_own = (
        dot_plain(normed, value_projection_weight) + dot_plain(low_value, value_adapter_second)
    ).astype(jnp.bfloat16)
    query_split = queries.reshape(row_count, heads_of_queries, head_dim).transpose(1, 0, 2)
    key_split = keys_own.reshape(row_count, heads_of_keys, head_dim).transpose(1, 0, 2)
    value_split = values_own.reshape(row_count, heads_of_keys, head_dim).transpose(1, 0, 2)
    tail_pair = passed_along(
        jnp.stack([key_split[:, row_count - WINDOW :], value_split[:, row_count - WINDOW :]]),
        "seq",
        1,
    )
    keys_all = jnp.concatenate([tail_pair[0], key_split], axis=1)
    values_all = jnp.concatenate([tail_pair[1], value_split], axis=1)
    query_features = feature_map(query_split, feature_query)
    phi_keys = feature_map(keys_all, key_hedgehog_map)
    query_group = query_split.reshape(heads_of_keys, group_count, row_count, head_dim)
    phi_group = query_features.reshape(heads_of_keys, group_count, row_count, 2 * head_dim)
    own_phi = phi_keys[:, :row_count].astype(jnp.float32) * keeping[None, :, None]
    own_values = values_all[:, :row_count].astype(jnp.float32)
    local_sum = (
        jnp.einsum("kcf,kcd->kfd", own_phi, own_values, precision=HIGH),
        jnp.sum(own_phi, axis=1),
        resets,
    )
    identity = (
        jnp.zeros_like(local_sum[0]),
        jnp.zeros_like(local_sum[1]),
        jnp.zeros((), jnp.float32),
    )
    prefix = entering(local_sum, "seq", segment_join, identity, False)
    attended = attend(query_group, phi_group, keys_all, phi_keys, values_all, prefix, layout)[0]
    mixed_heads = (
        attended.reshape(heads_of_queries, row_count, head_dim)
        .transpose(1, 0, 2)
        .reshape(row_count, heads_of_queries * head_dim)
        .astype(jnp.bfloat16)
    )
    branch, low_mix = lax.psum(
        (dot_plain(mixed_heads, w_out), dot_plain(mixed_heads, a_out)), "head"
    )
    low_mix = low_mix.astype(jnp.bfloat16)
    hidden_in = residual + branch + dot_plain(low_mix, b_out)
    scale_second = rms_scale(hidden_in)
    normed_second = (hidden_in * scale_second * gain_second).astype(jnp.bfloat16)
    gate_pre = dot_plain(normed_second, w_gate)
    up_pre = dot_plain(normed_second, w_up)
    sigmoid_gate = jax.nn.sigmoid(gate_pre)
    activated = gate_pre * sigmoid_gate
    hidden = (activated * up_pre).astype(jnp.bfloat16)
    ffn_part = lax.psum_scatter(dot_plain(hidden, w_down), "head", scatter_dimension=1, tiled=True)
    block_out = (lax.dynamic_slice_in_dim(hidden_in, column_at, columns, 1) + ffn_part).astype(
        jnp.bfloat16
    )
    grad_hidden = by_transpose(cotangent, w_down)
    grad_gate = (
        grad_hidden * up_pre * sigmoid_gate * (1.0 + gate_pre * (1.0 - sigmoid_gate))
    ).astype(jnp.bfloat16)
    grad_up = (grad_hidden * activated).astype(jnp.bfloat16)
    grad_w_down = transpose_by(hidden, cotangent)
    grad_w_gate = transpose_by(normed_second, grad_gate)
    grad_w_up = transpose_by(normed_second, grad_up)
    grad_second = lax.psum(by_transpose(grad_gate, w_gate) + by_transpose(grad_up, w_up), "head")
    grad_residual = cotangent.astype(jnp.float32) + norm_back(
        grad_second, hidden_in, scale_second, gain_second
    )
    grad_gain_second = jnp.sum(grad_second * hidden_in * scale_second, axis=0)
    grad_branch = grad_residual.astype(jnp.bfloat16)
    grad_low_mix = by_transpose(grad_branch, b_out)
    grad_mixed = by_transpose(grad_branch, w_out) + by_transpose_exact(grad_low_mix, a_out)
    grad_w_out = transpose_by(mixed_heads, grad_branch)
    grad_b_out = transpose_by(low_mix, grad_branch)
    grad_a_out = transpose_by_exact(mixed_heads, grad_low_mix)
    grad_heads = (
        grad_mixed.astype(jnp.bfloat16)
        .reshape(row_count, heads_of_queries, head_dim)
        .transpose(1, 0, 2)
        .reshape(heads_of_keys, group_count, row_count, head_dim)
    )
    attended, weights_near, weights_far, gating, denominator, damping = attend(
        query_group, phi_group, keys_all, phi_keys, values_all, prefix, layout
    )
    grad_float = grad_heads.astype(jnp.float32)
    grad_num = grad_float / denominator[..., None]
    grad_den = -jnp.sum(grad_float * attended, axis=-1) / denominator
    grad_weights = (
        jnp.einsum("kgrd,kcd->kgrc", grad_heads, values_all, preferred_element_type=jnp.float32)
        / denominator[..., None]
        + grad_den[..., None]
    )
    grad_scores = (weights_near * grad_weights).astype(jnp.bfloat16)
    grad_linear = jnp.where(beyond, grad_weights * damping, 0.0).astype(jnp.bfloat16)
    factor = head_dim ** (-0.5)
    grad_q_scores = (
        jnp.einsum("kgrc,kcd->kgrd", grad_scores, keys_all, preferred_element_type=jnp.float32)
        * factor
    )
    grad_keys = (
        jnp.einsum("kgrc,kgrd->kcd", grad_scores, query_group, preferred_element_type=jnp.float32)
        * factor
    )
    grad_phi_q = jnp.einsum(
        "kgrc,kcf->kgrf", grad_linear, phi_keys, preferred_element_type=jnp.float32
    )
    grad_phi_k = jnp.einsum(
        "kgrc,kgrf->kcf", grad_linear, phi_group, preferred_element_type=jnp.float32
    )
    mixed_weights = weights_near.astype(jnp.bfloat16).astype(jnp.float32) + weights_far
    grad_values = jnp.einsum("kgrc,kgrd->kcd", mixed_weights, grad_num, precision=HIGH)
    state_grad = gating[..., None] * grad_num
    phi_float = phi_group.astype(jnp.float32)
    grad_phi_q = (
        grad_phi_q
        + jnp.einsum("kgrd,kfd->kgrf", state_grad, prefix[0], precision=HIGH)
        + (gating * grad_den)[..., None] * prefix[1][:, None, None, :]
    )
    grad_state = jnp.einsum("kgrf,kgrd->kfd", phi_float, state_grad, precision=HIGH)
    grad_norms = jnp.einsum("kgrf,kgr->kf", phi_float, gating * grad_den, precision=HIGH)
    suffix = entering((grad_state, grad_norms, resets), "seq", segment_join, identity, True)
    padding = ((0, 0), (0, WINDOW), (0, 0))
    grad_phi_k = grad_phi_k + jnp.pad(
        (jnp.einsum("kfd,kcd->kcf", suffix[0], own_values, precision=HIGH) + suffix[1][:, None, :])
        * keeping[None, :, None],
        padding,
    )
    grad_values = grad_values + jnp.pad(
        jnp.einsum("kcf,kfd->kcd", own_phi, suffix[0], precision=HIGH), padding
    )
    grad_key_feature, grad_feature_key = feature_back(keys_all, key_hedgehog_map, grad_phi_k)
    grad_keys = grad_keys + grad_key_feature
    grad_query_feature, grad_feature_query = feature_back(
        query_split, feature_query, grad_phi_q.reshape(heads_of_queries, row_count, 2 * head_dim)
    )
    grad_query = grad_q_scores.reshape(heads_of_queries, row_count, head_dim) + grad_query_feature
    returned = passed_along(jnp.stack([grad_keys[:, :WINDOW], grad_values[:, :WINDOW]]), "seq", -1)
    tail_pad = ((0, 0), (row_count - WINDOW, 0), (0, 0))
    grad_keys_own = grad_keys[:, WINDOW:] + jnp.pad(returned[0], tail_pad)
    grad_values_own = grad_values[:, WINDOW:] + jnp.pad(returned[1], tail_pad)
    grad_q_rows = (
        grad_query.transpose(1, 0, 2)
        .reshape(row_count, heads_of_queries * head_dim)
        .astype(jnp.bfloat16)
    )
    grad_k_rows = (
        grad_keys_own.transpose(1, 0, 2)
        .reshape(row_count, heads_of_keys * head_dim)
        .astype(jnp.bfloat16)
    )
    grad_v_rows = (
        grad_values_own.transpose(1, 0, 2)
        .reshape(row_count, heads_of_keys * head_dim)
        .astype(jnp.bfloat16)
    )
    grad_low_query = by_transpose(grad_q_rows, b_query)
    grad_low_key = by_transpose(grad_k_rows, key_adapter_second)
    grad_low_value = by_transpose(grad_v_rows, value_adapter_second)
    grad_w_query = transpose_by(normed, grad_q_rows)
    grad_w_key = transpose_by(normed, grad_k_rows)
    grad_w_value = transpose_by(normed, grad_v_rows)
    grad_b_query = transpose_by(low_query, grad_q_rows)
    grad_b_key = transpose_by(low_key, grad_k_rows)
    grad_b_value = transpose_by(low_value, grad_v_rows)
    grad_a_query = transpose_by_exact(normed, grad_low_query)
    grad_a_key = transpose_by_exact(normed, grad_low_key)
    grad_a_value = transpose_by_exact(normed, grad_low_value)
    partial_first = (
        by_transpose(grad_q_rows, w_query)
        + by_transpose(grad_k_rows, key_projection_weight)
        + by_transpose(grad_v_rows, value_projection_weight)
        + by_transpose_exact(grad_low_query, a_query)
        + by_transpose_exact(grad_low_key, a_key)
        + by_transpose_exact(grad_low_value, a_value)
    )
    grad_first = lax.psum(partial_first, "head")
    grad_full = grad_residual + norm_back(grad_first, residual, scale_first, gain_first)
    grad_inputs = lax.dynamic_slice_in_dim(grad_full, column_at, columns, 1)
    grad_gain_first = jnp.sum(grad_first * residual * scale_first, axis=0)
    small_sums = lax.psum(
        (
            lax.dynamic_slice_in_dim(grad_gain_first, column_at, columns, 0),
            lax.dynamic_slice_in_dim(grad_gain_second, column_at, columns, 0),
            grad_b_query,
            grad_b_key,
            grad_b_value,
            grad_feature_query,
            grad_feature_key,
            grad_a_out,
            grad_b_out,
        ),
        "seq",
    )
    factor_sums = lax.psum((grad_a_query, grad_a_key, grad_a_value), ("seq", "head"))
    summed = (
        lax.psum_scatter(grad_w_query, "seq", scatter_dimension=0, tiled=True),
        lax.psum_scatter(grad_w_key, "seq", scatter_dimension=0, tiled=True),
        lax.psum_scatter(grad_w_value, "seq", scatter_dimension=0, tiled=True),
        lax.psum_scatter(grad_w_gate, "seq", scatter_dimension=0, tiled=True),
        lax.psum_scatter(grad_w_up, "seq", scatter_dimension=0, tiled=True),
        lax.psum_scatter(grad_w_out, "seq", scatter_dimension=1, tiled=True),
        lax.psum_scatter(grad_w_down, "seq", scatter_dimension=1, tiled=True),
    )
    return (
        block_out,
        grad_inputs,
        small_sums[0],
        summed[0],
        factor_sums[0],
        small_sums[2],
        summed[1],
        factor_sums[1],
        small_sums[3],
        summed[2],
        factor_sums[2],
        small_sums[4],
        small_sums[5],
        small_sums[6],
        summed[5],
        small_sums[7],
        small_sums[8],
        small_sums[1],
        summed[3],
        summed[4],
        summed[6],
    )


def solution(mesh):
    return jax.shard_map(
        body,
        mesh=mesh,
        in_specs=(
            P("seq", None),
            P(),
            P(None, "head"),
            P(),
            P(None, "head"),
            P(None, "head"),
            P(),
            P(None, "head"),
            P(None, "head"),
            P(),
            P(None, "head"),
            P("head", None, None),
            P("head", None, None),
            P("head", None),
            P("head", None),
            P(),
            P(),
            P(None, "head"),
            P(None, "head"),
            P("head", None),
            P(),
            P("seq", None),
        ),
        out_specs=(
            P("seq", "head"),
            P("seq", "head"),
            P("head"),
            P("seq", "head"),
            P(),
            P(None, "head"),
            P("seq", "head"),
            P(),
            P(None, "head"),
            P("seq", "head"),
            P(),
            P(None, "head"),
            P("head", None, None),
            P("head", None, None),
            P("head", "seq"),
            P("head", None),
            P(),
            P("head"),
            P("seq", "head"),
            P("seq", "head"),
            P("head", "seq"),
        ),
        check_vma=False,
    )
```

profile of v0, /device:TPU:1, one launch (start us, length us, event | category | flops | bytes accessed | tf_op | source)
XLA Modules:
  0.0 1770.6 jit_solution(17523593186454825437)
XLA Ops:
  15.0 4.5 collective-permute-start
  53.8 63.0 %all-reduce.4 = f32[32]{0:T(128)} all-reduce(f32[32]{0:T(128)S(1)} %dynamic-update-slice), channel_id=1, replica_groups=mesh['seq'=32,'head'=4] {'seq'}, use_global_device_ids=true, to_apply=%add.4 | all-reduce | flops 32 | bytes 256
  119.9 26.9 %all-gather.4 = f32[32,2,128]{2,1,0:T(2,128)} all-gather(f32[1,2,128]{2,1,0:T(2,128)} %bitcast.334), channel_id=3, replica_groups=mesh['seq'=32,'head'=4] {'seq'}, dimensions={0}, use_global_device_ids=true | all-gather | bytes 33792 | tf_op jit(solution)/shard_map/all_gather | solution.py:24
  155.6 4.1 while.30
  163.8 3.5 fusion.117
  171.9 9.3 psum.113
  181.3 170.6 %all-reduce.15.cloned.1.call-done = f32[256,2048]{1,0:T(8,128)} async-done(((f32[256,2048]{1,0:T(8,128)}), f32[256,2048]{1,0:T(8,128)}) %all-reduce.15.cloned.1.call-update) | async-done | bytes 2097168 | tf_op jit(solution)/shard_map/psum | solution.py:261
  356.1 7.6 fusion.128
  363.8 3.8 fusion.129
  367.6 8.8 multiply_convert_fusion.1
  378.8 7.2 convolution_add_fusion.5
  386.2 58.4 %all-reduce.17.cloned.1.call-done = f32[256,2048]{1,0:T(8,128)} async-done(((f32[256,2048]{1,0:T(8,128)}), f32[256,2048]{1,0:T(8,128)}) %all-reduce.17.cloned.1.call-update) | async-done | bytes 2097168 | tf_op jit(solution)/shard_map/psum | solution.py:285
  458.7 27.1 %all-gather.5 = f32[32,2,128]{2,1,0:T(2,128)} all-gather(f32[1,2,128]{2,1,0:T(2,128)S(1)} %bitcast.335), channel_id=5, replica_groups=mesh['seq'=32,'head'=4] {'seq'}, dimensions={0}, use_global_device_ids=true | all-gather | bytes 33792 | tf_op jit(solution)/shard_map/all_gather | solution.py:24
  494.1 7.5 all-gather.11.cloned.1.call-done
  501.7 87.7 %while.31 = (s32[]{:T(128)}, f32[2,128,64]{2,1,0:T(8,128)S(1)}, f32[2,128]{1,0:T(2,128)S(1)}, s32[]{:T(128)}, f32[32,2,128,64]{2,3,1,0:T(8,128)}, /*index=5*/f32...) while((s32[]{:T(128)}, f32[2,128,64]{2,1,0:T(8,128)S(1)}, ...), condition=%wide.region_30.31_spmd, body=%wide.region_29.30_spmd.sunk | while | flops 33287 | bytes 462035 | solution.py:33
  589.9 6.1 fusion.44
  597.7 5.2 collective-permute-start.1
  613.1 7.2 fusion.130
  638.5 28.1 %all-reduce.19.cloned.1.call-done = f32[256,2048]{1,0:T(8,128)} async-done(((f32[256,2048]{1,0:T(8,128)}), f32[256,2048]{1,0:T(8,128)}) %all-reduce.19.cloned.1.call-update) | async-done | bytes 2097168 | tf_op jit(solution)/shard_map/psum | solution.py:396
  678.8 8.2 fusion.151
  688.3 8.2 fusion.152
  698.0 8.2 fusion.153
  710.8 92.9 %all-reduce.25.cloned.1.call-done = (f32[8,64,64]{2,1,0:T(8,128)}, f32[8,2048]{1,0:T(8,128)}) async-done(((f32[8,64,64]{2,1,0:T(8,128)}, f32[8,2048]{1,0:T(8,128)}), (f32[8,64,64]{2,1,0:T(8,128)}, f32[8,2048]{1,0:T(8,128)})) %all-reduce.25.cloned.1.call-update) | async-done | bytes 196624 | tf_op jit(solution)/shard_map/psum | solution.py:400
  803.7 148.5 %all-reduce.21.cloned.1.call-done = (f32[2048,8]{0,1:T(8,128)}, f32[2048,8]{0,1:T(8,128)}, f32[2048,8]{0,1:T(8,128)}) async-done(((f32[2048,8]{0,1:T(8,128)}, f32[2048,8]{0,1:T(8,128)}, f32[2048,8]{0,1:T(8,128)}), (f32[2048,8]{0,1:T(8,128)}, f32[2048,8]{0,1:T(8,128)}, f32[2048,8]{0,1:T(8,128)})) %all-reduce.21.cloned.1.call-update) | async-done | bytes 196624 | tf_op jit(solution)/shard_map/psum | solution.py:414
  952.2 79.2 %reduce-scatter.13.cloned.1.call-done = f32[64,128]{1,0:T(8,128)} async-done(((f32[2048,128]{1,0:T(8,128)}), f32[64,128]{1,0:T(8,128)}) %reduce-scatter.13.cloned.1.call-update) | async-done | bytes 32784 | tf_op jit(solution)/shard_map/reduce_scatter | solution.py:417
  1031.3 80.9 %reduce-scatter.15.cloned.1.call-done = f32[64,128]{1,0:T(8,128)} async-done(((f32[2048,128]{1,0:T(8,128)}), f32[64,128]{1,0:T(8,128)}) %reduce-scatter.15.cloned.1.call-update) | async-done | bytes 32784 | tf_op jit(solution)/shard_map/reduce_scatter | solution.py:418
  1112.2 108.0 %all-reduce.23.cloned.1.call-done = (f32[512]{0:T(512)}, f32[8,512]{1,0:T(8,128)}, f32[8,128]{1,0:T(8,128)}, f32[8,128]{1,0:T(8,128)}, f32[2,64,64]{2,1,0:T(8,128)}, /*index=5*/f32[512,8]{0,1:T(8,128)}, f32[512]{0:T(512)}) async-done(((f32[512]{0:T(512)}, f32[8,512]{1,0:T(8,128)}, f32[8,128]{1,0:T(8,128)}, f32[8,128]{1,0:T(8,128)}, f32[2,64,64]{2,1,0:T(8,128)}, /*index=5*/f32[512,8]{0,1:T(8,128)}, ...) | async-done | bytes 77840 | tf_op jit(solution)/shard_map/psum | solution.py:400
  1220.2 83.6 %reduce-scatter.11.cloned.1.call-done = f32[64,512]{1,0:T(8,128)} async-done(((f32[2048,512]{1,0:T(8,128)}), f32[64,512]{1,0:T(8,128)}) %reduce-scatter.11.cloned.1.call-update) | async-done | bytes 131088 | tf_op jit(solution)/shard_map/reduce_scatter | solution.py:416
  1303.8 85.9 %reduce-scatter.17.cloned.1.call-done = f32[512,64]{0,1:T(8,128)} async-done(((f32[512,2048]{0,1:T(8,128)}), f32[512,64]{0,1:T(8,128)}) %reduce-scatter.17.cloned.1.call-update) | async-done | bytes 131088 | tf_op jit(solution)/shard_map/reduce_scatter | solution.py:421
  1389.8 119.3 %reduce-scatter.19.cloned.1.call-done = f32[64,2048]{1,0:T(8,128)} async-done(((f32[2048,2048]{1,0:T(8,128)}), f32[64,2048]{1,0:T(8,128)}) %reduce-scatter.19.cloned.1.call-update) | async-done | bytes 524304 | tf_op jit(solution)/shard_map/reduce_scatter | solution.py:419
  1509.1 118.9 %reduce-scatter.21.cloned.1.call-done = f32[64,2048]{1,0:T(8,128)} async-done(((f32[2048,2048]{1,0:T(8,128)}), f32[64,2048]{1,0:T(8,128)}) %reduce-scatter.21.cloned.1.call-update) | async-done | bytes 524304 | tf_op jit(solution)/shard_map/reduce_scatter | solution.py:420
  1628.0 119.0 %reduce-scatter.23.cloned.1.call-done = f32[2048,64]{0,1:T(8,128)} async-done(((f32[2048,2048]{0,1:T(8,128)}), f32[2048,64]{0,1:T(8,128)}) %reduce-scatter.23.cloned.1.call-update) | async-done | bytes 524304 | tf_op jit(solution)/shard_map/reduce_scatter | solution.py:422
  (598 shorter events, 226.4 us)
Async XLA Ops:
  7.2 160.8 %copy-start = (bf16[512,2048]{1,0:T(8,128)(2,1)S(1)}, bf16[512,2048]{1,0:T(8,128)(2,1)}, u32[]{:S(2)}) copy-start(bf16[512,2048]{1,0:T(8,128)(2,1)} %param.39) | copy-start | bytes 6291460
  7.2 147.8 %all-gather.9.cloned.1.call-start = ((), (), s32[]{:S(2)}) async-start(), calls=%async_computation.19 | async-start | bytes 2162688 | tf_op jit(solution)/shard_map/all_gather | solution.py:24
  15.0 10.1 collective-permute-start
  33.1 318.9 %all-reduce.15.cloned.1.call-start = ((), (), s32[]{:S(2)}) async-start(), calls=%async_computation.8 | async-start | bytes 4194304 | tf_op jit(solution)/shard_map/psum | solution.py:261
  37.5 109.3 %copy-start.18 = (bf16[256,512]{0,1:T(8,128)(2,1)}, bf16[256,512]{0,1:T(8,128)(2,1)S(1)}, u32[]{:S(2)}) copy-start(bf16[256,512]{0,1:T(8,128)(2,1)S(1)} %copy.97) | copy-start | bytes 786436
  43.5 103.4 %copy-start.49 = (bf16[256,128]{0,1:T(8,128)(2,1)S(1)}, bf16[256,128]{0,1:T(8,128)(2,1)}, u32[]{:S(2)}) copy-start(bf16[256,128]{0,1:T(8,128)(2,1)} %copy-done.48) | copy-start | bytes 196612
  162.0 293.1 %copy-start.92 = (f32[2,4,256]{2,1,0:T(4,128)}, f32[2,4,256]{2,1,0:T(4,128)S(1)}, u32[]{:S(2)}) copy-start(f32[2,4,256]{2,1,0:T(4,128)S(1)} %get-tuple-element.307) | copy-start | bytes 24580
  162.0 293.1 %copy-start.109 = (f32[2,4,256]{2,1,0:T(4,128)}, f32[2,4,256]{2,1,0:T(4,128)S(1)}, u32[]{:S(2)}) copy-start(f32[2,4,256]{2,1,0:T(4,128)S(1)} %get-tuple-element.306) | copy-start | bytes 24580
  170.2 181.8 %copy-start.76 = (bf16[8,2048]{1,0:T(8,128)(2,1)S(1)}, bf16[8,2048]{1,0:T(8,128)(2,1)}, u32[]{:S(2)}) copy-start(bf16[8,2048]{1,0:T(8,128)(2,1)} %param.41) | copy-start | bytes 98308
  170.2 274.4 %all-reduce.17.cloned.1.call-start = ((), (), s32[]{:S(2)}) async-start(), calls=%async_computation.10 | async-start | bytes 4194304 | tf_op jit(solution)/shard_map/psum | solution.py:285
  181.3 173.1 %copy-start.99 = (bf16[256,8]{0,1:T(8,128)(2,1)}, bf16[256,8]{0,1:T(8,128)(2,1)S(1)}, u32[]{:S(2)}) copy-start(bf16[256,8]{0,1:T(8,128)(2,1)S(1)} %psum.113) | copy-start | bytes 12292
  181.3 174.5 %copy-start.95 = (f32[2048]{0:T(1024)S(1)}, f32[2048]{0:T(1024)}, u32[]{:S(2)}) copy-start(f32[2048]{0:T(1024)} %param.42) | copy-start | bytes 24580
  386.0 115.7 %all-gather.11.cloned.1.call-start = ((), (), s32[]{:S(2)}) async-start(), calls=%async_computation.20 | async-start | bytes 2162688 | tf_op jit(solution)/shard_map/all_gather | solution.py:24
  457.3 209.2 %all-reduce.19.cloned.1.call-start = ((), (), s32[]{:S(2)}) async-start(), calls=%async_computation.11 | async-start | bytes 4194304 | tf_op jit(solution)/shard_map/psum | solution.py:396
  492.9 110.0 %copy-start.20 = (bf16[8,256,64]{1,2,0:T(8,128)(2,1)}, bf16[8,256,64]{1,2,0:T(8,128)(2,1)S(1)}, u32[]{:S(2)}) copy-start(bf16[8,256,64]{1,2,0:T(8,128)(2,1)S(1)} %fusion.33) | copy-start | bytes 786436
  494.1 95.3 %copy-start.68 = (bf16[2,256,128]{1,2,0:T(8,128)(2,1)S(1)}, bf16[2,256,128]{1,2,0:T(8,128)(2,1)}, u32[]{:S(2)}) copy-start(bf16[2,256,128]{1,2,0:T(8,128)(2,1)} %copy-done.67) | copy-start | bytes 393220
  494.1 95.3 %copy-start.118 = (f32[256]{0:T(256)S(1)}, f32[256]{0:T(256)}, u32[]{:S(2)}) copy-start(f32[256]{0:T(256)} %compare_convert_fusion) | copy-start | bytes 3076
  501.7 88.1 %copy-start.56 = (bf16[256,512]{0,1:T(8,128)(2,1)S(1)}, bf16[256,512]{0,1:T(8,128)(2,1)}, u32[]{:S(2)}) copy-start(bf16[256,512]{0,1:T(8,128)(2,1)} %copy-done.55) | copy-start | bytes 786436
  501.7 88.1 %copy-start.64 = (pred[256,320]{0,1:T(8,128)(4,1)S(1)}, pred[256,320]{0,1:T(8,128)(4,1)}, u32[]{:S(2)}) copy-start(pred[256,320]{0,1:T(8,128)(4,1)} %copy-done.62) | copy-start | bytes 245764
  597.7 6.4 collective-permute-start.1
  611.9 94.4 %reduce-scatter.9.cloned.1.call-start = ((), (), s32[]{:S(2)}) async-start(), calls=%async_computation.9 | async-start | bytes 2621440 | tf_op jit(solution)/shard_map/reduce_scatter | solution.py:273
  620.4 183.3 %all-reduce.25.cloned.1.call-start = ((), (), s32[]{:S(2)}) async-start(), calls=%async_computation.23 | async-start | bytes 655360 | tf_op jit(solution)/shard_map/psum | solution.py:400
  624.5 327.6 %all-reduce.21.cloned.1.call-start = ((), (), s32[]{:S(2)}) async-start(), calls=%async_computation.21 | async-start | bytes 393216 | tf_op jit(solution)/shard_map/psum | solution.py:414
  627.2 404.2 %reduce-scatter.13.cloned.1.call-start = ((), (), s32[]{:S(2)}) async-start(), calls=%async_computation.13 | async-start | bytes 1081344 | tf_op jit(solution)/shard_map/reduce_scatter | solution.py:417
  628.7 483.4 %reduce-scatter.15.cloned.1.call-start = ((), (), s32[]{:S(2)}) async-start(), calls=%async_computation.14 | async-start | bytes 1081344 | tf_op jit(solution)/shard_map/reduce_scatter | solution.py:418
  630.3 589.9 %all-reduce.23.cloned.1.call-start = ((), (), s32[]{:S(2)}) async-start(), calls=%async_computation.22 | async-start | bytes 221184 | tf_op jit(solution)/shard_map/psum | solution.py:400
  670.6 633.3 %reduce-scatter.11.cloned.1.call-start = ((), (), s32[]{:S(2)}) async-start(), calls=%async_computation.12 | async-start | bytes 4325376 | tf_op jit(solution)/shard_map/reduce_scatter | solution.py:416
  673.4 716.4 %reduce-scatter.17.cloned.1.call-start = ((), (), s32[]{:S(2)}) async-start(), calls=%async_computation.15 | async-start | bytes 4325376 | tf_op jit(solution)/shard_map/reduce_scatter | solution.py:421
  677.1 832.0 %reduce-scatter.19.cloned.1.call-start = ((), (), s32[]{:S(2)}) async-start(), calls=%async_computation.16 | async-start | bytes 17301504 | tf_op jit(solution)/shard_map/reduce_scatter | solution.py:419
  687.1 940.9 %reduce-scatter.21.cloned.1.call-start = ((), (), s32[]{:S(2)}) async-start(), calls=%async_computation.17 | async-start | bytes 17301504 | tf_op jit(solution)/shard_map/reduce_scatter | solution.py:420
  696.5 1050.4 %reduce-scatter.23.cloned.1.call-start = ((), (), s32[]{:S(2)}) async-start(), calls=%async_computation.18 | async-start | bytes 17301504 | tf_op jit(solution)/shard_map/reduce_scatter | solution.py:422
  706.3 1057.3 %copy-start.1 = (bf16[512,2048]{1,0:T(8,128)(2,1)S(1)}, bf16[512,2048]{1,0:T(8,128)(2,1)}, u32[]{:S(2)}) copy-start(bf16[512,2048]{1,0:T(8,128)(2,1)} %param.39) | copy-start | bytes 6291460
  (120 other events, 1013.9 us)
Sparse Core Ops, SparseCore 0:
  33.2 45.9 all-gather.8
  170.3 181.5 all-reduce.14
  386.1 58.4 all-reduce.16
  457.4 44.1 all-gather.10
  612.0 54.4 all-reduce.18
  668.9 29.4 reduce-scatter.8
  701.8 101.8 all-reduce.24
  809.9 142.2 all-reduce.20
  956.6 74.6 reduce-scatter.12
  1035.2 76.9 reduce-scatter.14
  1118.7 101.4 all-reduce.22
  1224.3 79.4 reduce-scatter.10
  1308.5 81.2 reduce-scatter.16
  1394.1 114.8 reduce-scatter.18
  1513.4 114.5 reduce-scatter.20
  1632.3 114.5 reduce-scatter.22
where the time goes:
time: 1780 us; the launch traced here: 1770 us
  waiting for transfers between devices  1300 us (73%)
  matrix products  138 us (8%)
  blocking collectives  126 us (7%)
  local copies, waits for them, and re-layouts  95.8 us (5%)
  other arithmetic  59 us (3%)
  loops' own time  20.7 us (1%)
  between operations  17.9 us (1%)
    psum x2, waiting for transfers between devices, body(): lax.psum((lax.dynamic_slice_in_dim(grad_gain_first, column_at, columns, 0...  201 us
    psum x1, waiting for transfers between devices, body(): lax.psum((dot_plain(mixed_heads, w_out), dot_plain(mixed_heads, a_out)),...  171 us
    psum x1, waiting for transfers between devices, body(): lax.psum((grad_a_query, grad_a_key, grad_a_value), ('seq', 'head'))  148 us
    reduce_scatter x1, waiting for transfers between devices, body(): lax.psum_scatter(grad_w_gate, 'seq', scatter_dimension=0, tiled=True)  119 us
    reduce_scatter x1, waiting for transfers between devices, body(): lax.psum_scatter(grad_w_down, 'seq', scatter_dimension=1, tiled=True)  119 us
    reduce_scatter x1, waiting for transfers between devices, body(): lax.psum_scatter(grad_w_up, 'seq', scatter_dimension=0, tiled=True)  119 us
    reduce_scatter x1, waiting for transfers between devices, body(): lax.psum_scatter(grad_w_out, 'seq', scatter_dimension=1, tiled=True)  85.9 us
    reduce_scatter x1, waiting for transfers between devices, body(): lax.psum_scatter(grad_w_query, 'seq', scatter_dimension=0, tiled=True)  83.6 us
  transfers between devices with their start and end apart: 18, of which 15 were waited for; matrix products, arithmetic and copies ran while one was open for 6% of the time, Pallas kernels for 0%

commit v1 on v0

--- a/solution.py
+++ b/solution.py
@@ -1,6 +1,8 @@
 import jax
 import jax.numpy as jnp
 from jax import lax
+from jax.experimental import pallas as pl
+from jax.experimental.pallas import tpu as pltpu
 from jax.sharding import PartitionSpec as P
 
 WINDOW = 64
@@ -9,6 +11,383 @@
 EPS = 1e-05
 NEG = -1e30
 HIGH = lax.Precision.HIGHEST
+
+MESH = pl.DeviceIdType.MESH
+F32 = jnp.float32
+BF16 = jnp.bfloat16
+
+
+def spot():
+    s = lax.axis_index("seq")
+    y = lax.axis_index("head")
+    return lax.div(s, 8), lax.rem(lax.div(s, 2), 4), lax.rem(s, 2), y
+
+
+def at(z, x, c, y):
+    return ((z * 4 + x) * 2 + c, y)
+
+
+def turned(p, steps):
+    return lax.rem(p + steps, 4)
+
+
+def greet(partners):
+    barrier = pltpu.get_barrier_semaphore()
+    for partner in partners:
+        pl.semaphore_signal(barrier, inc=1, device_id=partner, device_id_type=MESH)
+    pl.semaphore_wait(barrier, len(partners))
+
+
+def send(src, dst, ss, rs, device):
+    return pltpu.make_async_remote_copy(
+        src_ref=src, dst_ref=dst, send_sem=ss, recv_sem=rs, device_id=device, device_id_type=MESH
+    )
+
+
+class Ring:
+    def __init__(self, refs, rows, term, finish):
+        self.sb, self.ra, self.rf, self.tb, self.ra3, self.rf3, self.ss, self.rs = refs
+        self.rows, self.term, self.finish = rows, term, finish
+        z, x, c, y = spot()
+        self.axes = (
+            (x, at(z, turned(x, 1), c, y), at(z, turned(x, 3), c, y)),
+            (z, at(turned(z, 1), x, c, y), at(turned(z, 3), x, c, y)),
+        )
+
+    @staticmethod
+    def scratch(count, rows, width):
+        return [
+            pltpu.VMEM((count, 3, 4 * rows, width), BF16),
+            pltpu.VMEM((count, 2, 2 * rows, width), BF16),
+            pltpu.VMEM((count, 2, 4 * rows, width), BF16),
+            pltpu.VMEM((count, 4, rows, width), BF16),
+            pltpu.VMEM((count, 2, rows // 2, width), BF16),
+            pltpu.VMEM((count, 2, rows, width), BF16),
+            pltpu.SemaphoreType.DMA((count, 12)),
+            pltpu.SemaphoreType.DMA((count, 12)),
+        ]
+
+    def copy(self, t, k, i):
+        p, ahead, behind = self.axes[k]
+        q, ahead3, behind3 = self.axes[1 - k]
+        h, g = 2 * self.rows, self.rows // 2
+        lo, hi, lo3, hi3 = pl.ds(0, h), pl.ds(h, h), pl.ds(0, g), pl.ds(g, g)
+        sb, ra, rf, tb, ra3, rf3 = self.sb, self.ra, self.rf, self.tb, self.ra3, self.rf3
+        src, dst, device = (
+            lambda: (sb.at[t, 0, lo], ra.at[t, 0], ahead),
+            lambda: (sb.at[t, 0, hi], ra.at[t, 1], behind),
+            lambda: (sb.at[t, 1, hi], rf.at[t, 0, hi], ahead),
+            lambda: (sb.at[t, 2, lo], rf.at[t, 1, lo], behind),
+            lambda: (sb.at[t, 1, lo], rf.at[t, 0, lo], ahead),
+            lambda: (sb.at[t, 2, hi], rf.at[t, 1, hi], behind),
+            lambda: (tb.at[t, turned(q, 2), lo3], ra3.at[t, 0], ahead3),
+            lambda: (tb.at[t, turned(q, 2), hi3], ra3.at[t, 1], behind3),
+            lambda: (tb.at[t, turned(q, 1), hi3], rf3.at[t, 0, hi3], ahead3),
+            lambda: (tb.at[t, turned(q, 3), lo3], rf3.at[t, 1, lo3], behind3),
+            lambda: (tb.at[t, turned(q, 1), lo3], rf3.at[t, 0, lo3], ahead3),
+            lambda: (tb.at[t, turned(q, 3), hi3], rf3.at[t, 1, hi3], behind3),
+        )[i]()
+        return send(src, dst, self.ss.at[t, i], self.rs.at[t, i], device)
+
+    def start(self, t, k):
+        p = self.axes[k][0]
+        h = 2 * self.rows
+        self.sb[t, 0] = self.term(t, k, turned(p, 2), 0, 4).astype(BF16)
+        self.copy(t, k, 0).start()
+        self.copy(t, k, 1).start()
+        self.sb[t, 1, h:] = self.term(t, k, turned(p, 1), 2, 4).astype(BF16)
+        self.copy(t, k, 2).start()
+        self.sb[t, 2, :h] = self.term(t, k, turned(p, 3), 0, 2).astype(BF16)
+        self.copy(t, k, 3).start()
+
+    def merge(self, t, k):
+        p = self.axes[k][0]
+        h = 2 * self.rows
+        self.copy(t, k, 0).wait_recv()
+        self.sb[t, 1, :h] = (self.term(t, k, turned(p, 1), 0, 2) + self.ra[t, 0].astype(F32)).astype(BF16)
+        self.copy(t, k, 4).start()
+        self.copy(t, k, 1).wait_recv()
+        self.sb[t, 2, h:] = (self.term(t, k, turned(p, 3), 2, 4) + self.ra[t, 1].astype(F32)).astype(BF16)
+        self.copy(t, k, 5).start()
+
+    def cross(self, t, k):
+        p = self.axes[k][0]
+        own = self.term(t, k, p, 0, 4)
+        for i in (2, 3, 4, 5):
+            self.copy(t, k, i).wait_recv()
+        own = own + self.rf[t, 0].astype(F32) + self.rf[t, 1].astype(F32)
+        self.tb[t] = own.astype(BF16).reshape(self.tb.shape[1:])
+        for i in (6, 7, 8, 9):
+            self.copy(t, k, i).start()
+
+    def merge_cross(self, t, k):
+        q = self.axes[1 - k][0]
+        g = self.rows // 2
+        self.copy(t, k, 6).wait_recv()
+        ahead, behind = turned(q, 1), turned(q, 3)
+        self.tb[t, ahead, :g] = (self.tb[t, ahead, :g].astype(F32) + self.ra3[t, 0].astype(F32)).astype(BF16)
+        self.copy(t, k, 10).start()
+        self.copy(t, k, 7).wait_recv()
+        self.tb[t, behind, g:] = (self.tb[t, behind, g:].astype(F32) + self.ra3[t, 1].astype(F32)).astype(BF16)
+        self.copy(t, k, 11).start()
+
+    def end(self, t, k):
+        q = self.axes[1 - k][0]
+        for i in (8, 9, 10, 11):
+            self.copy(t, k, i).wait_recv()
+        self.finish(
+            t, k, self.tb[t, q].astype(F32) + self.rf3[t, 0].astype(F32) + self.rf3[t, 1].astype(F32)
+        )
+
+    def drain(self, t, k):
+        for i in range(12):
+            self.copy(t, k, i).wait_send()
+
+
+def over_pairs(count, step):
+    def both(u, carry):
+        step(2 * u, 0)
+        step(2 * u + 1, 1)
+        return carry
+
+    lax.fori_loop(0, count // 2, both, 0)
+
+
+FFN_TILES, FFN_WIDTH = 12, 512
+ATT_TILES, ATT_WIDTH = 5, 256
+PACK = 32
+
+
+def sums_kernel(
+    xt_ffn, y_ffn, xt_att, y_att, pack,
+    out_ffn, out_att, out_pack,
+    xf, yf, xa, ya, pk, sem_ffn, sem_att, sem_pack,
+    *rest,
+):
+    ring_ffn, ring_att, ring_pack = rest[0:8], rest[8:16], rest[16:24]
+    ysum, sem_y, sem_zx = rest[24:27]
+    z, x, c, y = spot()
+    sibling = at(z, x, 1 - c, y)
+    others = (1, 2, 3)
+    z_mates = [at(turned(z, i), x, c, y) for i in others]
+    x_mates = [at(z, turned(x, i), c, y) for i in others]
+    y_mates = [at(z, x, c, turned(y, i)) for i in others]
+    greet([sibling] + z_mates + x_mates + y_mates)
+
+    own_rows, far_rows = pl.ds(0, 256), pl.ds(256, 256)
+
+    def factors(xt, yt, xd, yd, sem, m, t):
+        copies = []
+        if m is not None:
+            copies.append(pltpu.make_async_copy(xt.at[m, c], xd.at[m, :, :, :, own_rows], sem.at[0, m]))
+            copies.append(
+                send(xt.at[m, 1 - c], xd.at[m, :, :, :, far_rows], sem.at[1, m], sem.at[2, m], sibling)
+            )
+        if t is not None:
+            copies.append(pltpu.make_async_copy(yt.at[t], yd.at[t, own_rows], sem.at[0, 2 + t]))
+            copies.append(send(yt.at[t], yd.at[t, far_rows], sem.at[1, 2 + t], sem.at[2, 2 + t], sibling))
+        return copies
+
+    ffn = (xt_ffn, y_ffn, xf, yf, sem_ffn)
+    att = (xt_att, y_att, xa, ya, sem_att)
+    pack_own = pltpu.make_async_copy(pack.at[c], pk.at[0], sem_pack.at[0])
+    pack_far = send(pack.at[1 - c], pk.at[1], sem_pack.at[1], sem_pack.at[2], sibling)
+    for m in range(2):
+        for copy in factors(*ffn, m, None):
+            copy.start()
+
+    def open_ffn(t, carry):
+        for copy in factors(*ffn, None, t):
+            copy.start()
+        return carry
+
+    lax.fori_loop(0, FFN_TILES, open_ffn, 0)
+    for m in range(2):
+        for copy in factors(*att, m, None):
+            copy.start()
+    for t in range(ATT_TILES):
+        for copy in factors(*att, None, t):
+            copy.start()
+    pack_own.start()
+    pack_far.start()
+
+    def product(xd, yd, kind):
+        def term(t, k, dest, first, last):
+            m = kind(t)
+            if k == 0:
+                rows = xd[m, first:last, dest]
+            else:
+                rows = xd[m, dest, first:last]
+            rows = rows.reshape((last - first) * 64, 512)
+            return jnp.dot(rows, yd[t], preferred_element_type=F32)
+
+        return term
+
+    def finish_ffn(t, k, value):
+        out_ffn[t] = value
+
+    def finish_att(t, k, value):
+        out_att[t] = value
+
+    def term_pack(t, k, dest, first, last):
+        both = (pk[0, first:last, dest], pk[1, first:last, dest])
+        return (both[0] + both[1]).reshape((last - first) * PACK, 128)
+
+    def finish_pack(t, k, value):
+        out_pack[c, z, x] = value
+
+    big = Ring(ring_ffn, 64, product(xf, yf, lambda t: lax.div(t, 8)), finish_ffn)
+    mid = Ring(ring_att, 64, product(xa, ya, lambda t: t // 3), finish_att)
+    low = Ring(ring_pack, PACK, term_pack, finish_pack)
+
+    for m in range(2):
+        for copy in factors(*ffn, m, None):
+            copy.wait()
+
+    def first_ffn(t, k):
+        for copy in factors(*ffn, None, t):
+            copy.wait()
+        big.start(t, k)
+
+    over_pairs(FFN_TILES, first_ffn)
+    for m in range(2):
+        for copy in factors(*att, m, None):
+            copy.wait()
+    for t in range(ATT_TILES):
+        for copy in factors(*att, None, t):
+            copy.wait()
+        mid.start(t, t % 2)
+    pack_own.wait()
+    pack_far.wait()
+    low.start(0, 0)
+    over_pairs(FFN_TILES, big.merge)
+    for t in range(ATT_TILES):
+        mid.merge(t, t % 2)
+    low.merge(0, 0)
+    over_pairs(FFN_TILES, big.cross)
+    for t in range(ATT_TILES):
+        mid.cross(t, t % 2)
+    low.cross(0, 0)
+    over_pairs(FFN_TILES, big.merge_cross)
+    for t in range(ATT_TILES):
+        mid.merge_cross(t, t % 2)
+    low.merge_cross(0, 0)
+    over_pairs(FFN_TILES, big.end)
+    for t in range(ATT_TILES):
+        mid.end(t, t % 2)
+    low.end(0, 0)
+    top = pl.ds(0, 16)
+    turns = [
+        send(out_pack.at[c, z, x, top], ysum.at[i], sem_y.at[0, i], sem_y.at[1, i], y_mates[i]) for i in range(3)
+    ]
+    for copy in turns:
+        copy.start()
+    for copy in turns:
+        copy.wait()
+    out_pack[c, z, x, top] = out_pack[c, z, x, top] + ysum[0] + ysum[1] + ysum[2]
+    turns = [
+        send(out_pack.at[c, z, x], out_pack.at[c, z, x], sem_zx.at[0, i], sem_zx.at[1, i], z_mates[i])
+        for i in range(3)
+    ]
+    for copy in turns:
+        copy.start()
+    for i in range(3):
+        came = out_pack.at[c, turned(z, 3 - i), x]
+        send(came, came, sem_zx.at[0, i], sem_zx.at[1, i], z_mates[i]).wait()
+    turns = [
+        send(out_pack.at[c, :, x], out_pack.at[c, :, x], sem_zx.at[0, 3 + i], sem_zx.at[1, 3 + i], x_mates[i])
+        for i in range(3)
+    ]
+    for copy in turns:
+        copy.start()
+    for i in range(3):
+        came = out_pack.at[c, :, turned(x, 3 - i)]
+        send(came, came, sem_zx.at[0, 3 + i], sem_zx.at[1, 3 + i], x_mates[i]).wait()
+    last = send(out_pack.at[c], out_pack.at[c], sem_zx.at[0, 6], sem_zx.at[1, 6], sibling)
+    last.start()
+    came = out_pack.at[1 - c]
+    send(came, came, sem_zx.at[0, 6], sem_zx.at[1, 6], sibling).wait()
+    over_pairs(FFN_TILES, big.drain)
+    for t in range(ATT_TILES):
+        mid.drain(t, t % 2)
+    low.drain(0, 0)
+
+
+def seq_sums(xt_ffn, y_ffn, xt_att, y_att, pack):
+    anywhere = pl.BlockSpec(memory_space=pl.ANY)
+    vmem = pl.BlockSpec(memory_space=pltpu.VMEM)
+    return pl.pallas_call(
+        sums_kernel,
+        out_shape=(
+            jax.ShapeDtypeStruct((FFN_TILES, 64, FFN_WIDTH), F32),
+            jax.ShapeDtypeStruct((ATT_TILES, 64, ATT_WIDTH), F32),
+            jax.ShapeDtypeStruct((2, 4, 4, PACK, 128), F32),
+        ),
+        in_specs=[anywhere] * 5,
+        out_specs=(vmem,) * 3,
+        scratch_shapes=[
+            pltpu.VMEM((2, 4, 4, 64, 512), BF16),
+            pltpu.VMEM((FFN_TILES, 512, FFN_WIDTH), BF16),
+            pltpu.VMEM((2, 4, 4, 64, 512), BF16),
+            pltpu.VMEM((ATT_TILES, 512, ATT_WIDTH), BF16),
+            pltpu.VMEM((2, 4, 4, PACK, 128), F32),
+            pltpu.SemaphoreType.DMA((3, 2 + FFN_TILES)),
+            pltpu.SemaphoreType.DMA((3, 2 + ATT_TILES)),
+            pltpu.SemaphoreType.DMA((3,)),
+            *Ring.scratch(FFN_TILES, 64, FFN_WIDTH),
+            *Ring.scratch(ATT_TILES, 64, ATT_WIDTH),
+            *Ring.scratch(1, PACK, 128),
+            pltpu.VMEM((3, 16, 128), F32),
+            pltpu.SemaphoreType.DMA((2, 3)),
+            pltpu.SemaphoreType.DMA((2, 7)),
+        ],
+        compiler_params=pltpu.CompilerParams(
+            collective_id=0, has_side_effects=True, vmem_limit_bytes=60 * 2**20
+        ),
+        name="seq_sums",
+    )(xt_ffn, y_ffn, xt_att, y_att, pack)
+
+
+def by_owner(rows):
+    return rows.reshape(rows.shape[0], 4, 4, 2, 64).transpose(3, 1, 2, 4, 0)
+
+
+def tiles_of(rows, width):
+    return rows.reshape(rows.shape[0], -1, width).transpose(1, 0, 2)
+
+
+def untile(tiles):
+    return tiles.transpose(1, 0, 2).reshape(tiles.shape[1], -1)
+
+
+def pack_small(a_rows, b_out, f_query, f_key, b_rows, a_out, gain_one, gain_two):
+    top = jnp.concatenate([a_rows[:12], b_out[:4], a_rows[12:], b_out[4:]], axis=0)
+    top = top.reshape(2, 16, 16, 128).transpose(2, 0, 1, 3).reshape(32, 16, 128)
+    bottom = jnp.concatenate(
+        [
+            f_query.reshape(4, 2, 64, 64).transpose(0, 2, 1, 3).reshape(16, 16, 128),
+            f_key.transpose(1, 0, 2).reshape(4, 16, 128),
+            b_rows.reshape(8, 6, 128).transpose(1, 0, 2).reshape(3, 16, 128),
+            a_out.reshape(8, 4, 128).transpose(1, 0, 2).reshape(2, 16, 128),
+            jnp.concatenate([gain_one.reshape(4, 128), gain_two.reshape(4, 128), jnp.zeros((8, 128), F32)])[None],
+            jnp.zeros((6, 16, 128), F32),
+        ]
+    )
+    return jnp.concatenate([top, bottom], axis=1).reshape(2, 4, 4, 32, 128)
+
+
+def unpack_small(packed):
+    flat = packed.reshape(32, 32, 128)
+    top = flat[:, :16].reshape(16, 2, 16, 128).transpose(1, 2, 0, 3).reshape(2, 16, 2048)
+    a_rows = jnp.concatenate([top[0, :12], top[1, :12]])
+    b_out = jnp.concatenate([top[0, 12:], top[1, 12:]])
+    bottom = flat[:, 16:]
+    f_query = bottom[:16].reshape(4, 64, 2, 64).transpose(0, 2, 1, 3).reshape(8, 64, 64)
+    f_key = bottom[16:20].reshape(64, 2, 64).transpose(1, 0, 2)
+    b_rows = bottom[20:23].reshape(6, 8, 128).transpose(1, 0, 2).reshape(8, 768)
+    a_out = bottom[23:25].reshape(4, 8, 128).transpose(1, 0, 2).reshape(8, 512)
+    gains = bottom[25]
+    return a_rows, b_out, f_query, f_key, b_rows, a_out, gains[:4].reshape(512), gains[4:8].reshape(512)
 
 
 def passed_along(value, axis, steps):
@@ -279,9 +658,6 @@
         grad_hidden * up_pre * sigmoid_gate * (1.0 + gate_pre * (1.0 - sigmoid_gate))
     ).astype(jnp.bfloat16)
     grad_up = (grad_hidden * activated).astype(jnp.bfloat16)
-    grad_w_down = transpose_by(hidden, cotangent)
-    grad_w_gate = transpose_by(normed_second, grad_gate)
-    grad_w_up = transpose_by(normed_second, grad_up)
     grad_second = lax.psum(by_transpose(grad_gate, w_gate) + by_transpose(grad_up, w_up), "head")
     grad_residual = cotangent.astype(jnp.float32) + norm_back(
         grad_second, hidden_in, scale_second, gain_second
@@ -290,9 +666,8 @@
     grad_branch = grad_residual.astype(jnp.bfloat16)
     grad_low_mix = by_transpose(grad_branch, b_out)
     grad_mixed = by_transpose(grad_branch, w_out) + by_transpose_exact(grad_low_mix, a_out)
-    grad_w_out = transpose_by(mixed_heads, grad_branch)
     grad_b_out = transpose_by(low_mix, grad_branch)
-    grad_a_out = transpose_by_exact(mixed_heads, grad_low_mix)
+    grad_a_out = transpose_by_exact(mixed_heads, grad_low_mix).T
     grad_heads = (
         grad_mixed.astype(jnp.bfloat16)
         .reshape(row_count, heads_of_queries, head_dim)
@@ -376,9 +751,6 @@
     grad_low_query = by_transpose(grad_q_rows, b_query)
     grad_low_key = by_transpose(grad_k_rows, key_adapter_second)
     grad_low_value = by_transpose(grad_v_rows, value_adapter_second)
-    grad_w_query = transpose_by(normed, grad_q_rows)
-    grad_w_key = transpose_by(normed, grad_k_rows)
-    grad_w_value = transpose_by(normed, grad_v_rows)
     grad_b_query = transpose_by(low_query, grad_q_rows)
     grad_b_key = transpose_by(low_key, grad_k_rows)
     grad_b_value = transpose_by(low_value, grad_v_rows)
@@ -397,52 +769,49 @@
     grad_full = grad_residual + norm_back(grad_first, residual, scale_first, gain_first)
     grad_inputs = lax.dynamic_slice_in_dim(grad_full, column_at, columns, 1)
     grad_gain_first = jnp.sum(grad_first * residual * scale_first, axis=0)
-    small_sums = lax.psum(
-        (
-            lax.dynamic_slice_in_dim(grad_gain_first, column_at, columns, 0),
-            lax.dynamic_slice_in_dim(grad_gain_second, column_at, columns, 0),
-            grad_b_query,
-            grad_b_key,
-            grad_b_value,
-            grad_feature_query,
-            grad_feature_key,
-            grad_a_out,
-            grad_b_out,
+    packed = pack_small(
+        jnp.concatenate([grad_a_query, grad_a_key, grad_a_value], axis=1).T,
+        0.25 * grad_b_out,
+        grad_feature_query,
+        grad_feature_key,
+        jnp.concatenate([grad_b_query, grad_b_key, grad_b_value], axis=1),
+        grad_a_out,
+        lax.dynamic_slice_in_dim(grad_gain_first, column_at, columns, 0),
+        lax.dynamic_slice_in_dim(grad_gain_second, column_at, columns, 0),
+    )
+    out_ffn, out_att, out_pack = seq_sums(
+        jnp.stack([by_owner(normed_second), by_owner(cotangent)]),
+        jnp.concatenate([tiles_of(a, FFN_WIDTH) for a in (grad_gate, grad_up, hidden)]),
+        jnp.stack([by_owner(normed), by_owner(grad_branch)]),
+        jnp.concatenate(
+            [tiles_of(a, ATT_WIDTH) for a in (grad_q_rows, jnp.concatenate([grad_k_rows, grad_v_rows], axis=1), mixed_heads)]
         ),
-        "seq",
-    )
-    factor_sums = lax.psum((grad_a_query, grad_a_key, grad_a_value), ("seq", "head"))
-    summed = (
-        lax.psum_scatter(grad_w_query, "seq", scatter_dimension=0, tiled=True),
-        lax.psum_scatter(grad_w_key, "seq", scatter_dimension=0, tiled=True),
-        lax.psum_scatter(grad_w_value, "seq", scatter_dimension=0, tiled=True),
-        lax.psum_scatter(grad_w_gate, "seq", scatter_dimension=0, tiled=True),
-        lax.psum_scatter(grad_w_up, "seq", scatter_dimension=0, tiled=True),
-        lax.psum_scatter(grad_w_out, "seq", scatter_dimension=1, tiled=True),
-        lax.psum_scatter(grad_w_down, "seq", scatter_dimension=1, tiled=True),
-    )
+        packed,
+    )
+    a_rows, b_out_sum, f_query, f_key, b_rows, a_out_sum, gain_one, gain_two = unpack_small(out_pack)
+    a_rows = a_rows.T
     return (
         block_out,
         grad_inputs,
-        small_sums[0],
-        summed[0],
-        factor_sums[0],
-        small_sums[2],
-        summed[1],
-        factor_sums[1],
-        small_sums[3],
-        summed[2],
-        factor_sums[2],
-        small_sums[4],
-        small_sums[5],
-        small_sums[6],
-        summed[5],
-        small_sums[7],
-        small_sums[8],
-        small_sums[1],
-        summed[3],
-        summed[4],
-        summed[6],
+        gain_one,
+        untile(out_att[:2]),
+        a_rows[:, :8],
+        b_rows[:, :512],
+        out_att[2, :, :128],
+        a_rows[:, 8:16],
+        b_rows[:, 512:640],
+        out_att[2, :, 128:],
+        a_rows[:, 16:],
+        b_rows[:, 640:],
+        f_query,
+        f_key,
+        untile(out_att[3:]).T,
+        a_out_sum.T,
+        b_out_sum,
+        gain_two,
+        untile(out_ffn[:4]),
+        untile(out_ffn[4:8]),
+        untile(out_ffn[8:]).T,
     )
 
 

time: 1780 us -> 886 us (0.50)
  waiting for transfers between devices: 1300 us -> 235 us
  Pallas kernels: 0 us -> 109 us
  local copies, waits for them, and re-layouts: 95.8 us -> 152 us
  other arithmetic: 59 us -> 88 us
  matrix products: 138 us -> 112 us
    reduce_scatter x7 -> x0, waiting for transfers between devices: 687 us -> none  [the longest x1 119 us: body(): lax.psum_scatter(grad_w_gate, 'seq', scatter_dimension=0, tiled=True)]
    psum x3 -> x0, waiting for transfers between devices: 349 us -> none  [the longest x2 201 us: body(): lax.psum((lax.dynamic_slice_in_dim(grad_gain_first, column_at, columns, 0...]
    pallas_call x0 -> x1, Pallas kernels: none -> 109 us  [seq_sums(): pl.pallas_call(sums_kernel, out_shape=(jax.ShapeDtypeStruct((FFN_TILES, 6...]
    psum x1, waiting for transfers between devices: 58.4 us -> 17.9 us  [body(): lax.psum(by_transpose(grad_gate, w_gate) + by_transpose(grad_up, w_up), '...]
    dot_general x11 -> x4, matrix products: 36.9 us -> 2.96 us  [transpose_by(): lax.dot_general(left_side, right_side, (((0,), (0,)), ((), ())), preferre...]
    reshape x0 -> x23, local copies, waits for them, and re-layouts: none -> 24.8 us  [the longest x4 8.2 us: by_owner(): return rows.reshape(rows.shape[0], 4, 4, 2, 64).transpose(3, 1, 2, 4, 0)]
    dynamic_slice x93, local copies, waits for them, and re-layouts: 48.1 us -> 66.8 us  [one(): lax.dynamic_index_in_dim(a, source, 0, False)]
    psum x1, waiting for transfers between devices: 28.1 us -> 45.9 us  [body(): grad_first = lax.psum(partial_first, 'head')]
  transfers between devices with their start and end apart: 18 -> 8, of which waited for: 15 -> 4; matrix products, arithmetic and copies ran while one was open for 6% -> 16% of each run, Pallas kernels for 0% -> 0%
where the time goes in v1:
time: 886 us; the launch traced here: 873 us
  waiting for transfers between devices  235 us (27%)
  local copies, waits for them, and re-layouts  152 us (17%)
  blocking collectives  126 us (14%)
  matrix products  112 us (13%)
  Pallas kernels  109 us (12%)
  other arithmetic  88 us (10%)
  loops' own time  20.5 us (2%)
  between operations  17.8 us (2%)
  starting transfers between devices  11.7 us (1%)
    psum x1, waiting for transfers between devices, body(): lax.psum((dot_plain(mixed_heads, w_out), dot_plain(mixed_heads, a_out)),...  171 us
    pallas_call x1, Pallas kernels, seq_sums(): pl.pallas_call(sums_kernel, out_shape=(jax.ShapeDtypeStruct((FFN_TILES, 6...  109 us
    dynamic_slice x93, local copies, waits for them, and re-layouts, one(): lax.dynamic_index_in_dim(a, source, 0, False)  66.8 us
    unnamed x1, blocking collectives  62.9 us
    all_gather x2, blocking collectives, entering(): gathered = jax.tree.map(lambda a: lax.all_gather(a, axis), part)  53.9 us
    psum x1, waiting for transfers between devices, body(): grad_first = lax.psum(partial_first, 'head')  45.9 us
    add x31, other arithmetic, segment_join(): later_part[1] + passing * earlier[1]  39 us
    dot_general x15, matrix products, dot_plain(): return jnp.dot(left_side, right_side, preferred_element_type=jnp.float32)  30.1 us
  transfers between devices with their start and end apart: 8, of which 4 were waited for; matrix products, arithmetic and copies ran while one was open for 16% of the time, Pallas kernels for 0%

profile of v1, /device:TPU:1, one launch (start us, length us, event | category | flops | bytes accessed | tf_op | source)
XLA Modules:
  0.0 872.6 jit_solution(11724417818488895063)
XLA Ops:
  8.9 2.9 convert_multiply_fusion.2
  15.1 4.5 collective-permute-start
  33.3 3.0 fusion.31
  53.5 62.9 %all-reduce.4 = f32[32]{0:T(128)} all-reduce(f32[32]{0:T(128)S(1)} %dynamic-update-slice), channel_id=1, replica_groups=mesh['seq'=32,'head'=4] {'seq'}, use_global_device_ids=true, to_apply=%add.4 | all-reduce | flops 32 | bytes 256
  119.5 26.9 %all-gather.4 = f32[32,2,128]{2,1,0:T(2,128)} all-gather(f32[1,2,128]{2,1,0:T(2,128)} %bitcast.500), channel_id=3, replica_groups=mesh['seq'=32,'head'=4] {'seq'}, dimensions={0}, use_global_device_ids=true | all-gather | bytes 33792 | tf_op jit(solution)/shard_map/all_gather | solution.py:403
  155.2 4.1 while.30
  163.4 3.5 fusion.121
  171.5 8.9 %psum.29 = bf16[256,8]{0,1:T(8,128)(2,1)S(1)} all-reduce(f32[256,8]{0,1:T(8,128)S(1)} %fusion.131), channel_id=1, replica_groups=mesh['seq'=32,'head'=4] {'head'}, use_global_device_ids=true, to_apply=%region_21.22 | all-reduce | flops 2048 | bytes 12288 | tf_op jit(solution)/shard_map/psum | solution.py:640
  180.4 171.0 %all-reduce.9.cloned.1.call-done = f32[256,2048]{1,0:T(8,128)} async-done(((f32[256,2048]{1,0:T(8,128)}), f32[256,2048]{1,0:T(8,128)}) %all-reduce.9.cloned.1.call-update) | async-done | bytes 2097168 | tf_op jit(solution)/shard_map/psum | solution.py:640
  351.4 2.5 multiply_reduce_fusion.2
  355.5 7.6 fusion.132
  363.1 3.7 fusion.133
  366.8 8.8 %multiply_convert_fusion.1 = (bf16[256,2048]{1,0:T(8,128)(2,1)S(1)}, bf16[256,2048]{1,0:T(8,128)(2,1)S(1)}, bf16[256,2048]{1,0:T(8,128)(2,1)}) fusion(f32[256,2048]{1,0:T(8,128)} %fusion.132, f32[256,2048]{1,0:T(8,128)} %fusion.133, bf16[256,2048]{1,0:T(8,128)(2,1)S(1)} %copy-done.28, bf16[2048,2048]{1,0:T(8,128)(2,1)} %param.45), kind=kOutput, calls=%fused_computation.43 | convolution fusion | flops 2155347968 | bytes 16777216 | tf_op jit(solution)/shard_map/dot_general | solution.py:420
  378.0 7.1 convolution_add_fusion.5
  385.4 7.4 fusion.134
  420.7 3.3 pad_maximum_fusion.1.xt_ffn
  425.8 17.9 %all-reduce.11.cloned.1.call-done = f32[256,2048]{1,0:T(8,128)} async-done(((f32[256,2048]{1,0:T(8,128)}), f32[256,2048]{1,0:T(8,128)}) %all-reduce.11.cloned.1.call-update) | async-done | bytes 2097168 | tf_op jit(solution)/shard_map/psum | solution.py:661
  443.7 3.5 multiply_reduce_fusion
  447.3 3.8 fusion.110
  455.4 2.7 fusion.32
  459.9 2.4 copy.254
  464.1 3.0 fusion.54
  467.1 4.9 multiply_convert_fusion
  472.5 2.6 fusion.18
  486.2 27.1 %all-gather.5 = f32[32,2,128]{2,1,0:T(2,128)} all-gather(f32[1,2,128]{2,1,0:T(2,128)S(1)} %bitcast.501), channel_id=5, replica_groups=mesh['seq'=32,'head'=4] {'seq'}, dimensions={0}, use_global_device_ids=true | all-gather | bytes 33792 | tf_op jit(solution)/shard_map/all_gather | solution.py:403
  516.3 3.2 pad_maximum_fusion.2.xt_att
  527.2 123.5 %while.31 = (s32[]{:T(128)}, f32[2,128,64]{2,1,0:T(8,128)S(1)}, f32[2,128]{1,0:T(2,128)}, s32[]{:T(128)}, f32[32,2,128,64]{2,3,1,0:T(8,128)}, /*index=5*/f32[32]...) while((s32[]{:T(128)}, f32[2,128,64]{2,1,0:T(8,128)S(1)}, ...), condition=%wide.region_30.31_spmd, body=%wide.region_29.30_spmd.sunk | while | flops 33287 | bytes 462035 | solution.py:412
  652.1 6.1 fusion.44
  660.9 6.3 collective-permute-start.1
  685.6 45.9 %all-reduce.13.cloned.1.call-done = f32[256,2048]{1,0:T(8,128)} async-done(((f32[256,2048]{1,0:T(8,128)}), f32[256,2048]{1,0:T(8,128)}) %all-reduce.13.cloned.1.call-update) | async-done | bytes 2097168 | tf_op jit(solution)/shard_map/psum | solution.py:768
  731.4 3.4 fusion.12
  735.8 109.0 %seq_sums.1 = (f32[12,64,512]{2,1,0:T(8,128)}, f32[5,64,256]{2,1,0:T(8,128)}, f32[2,4,4,32,128]{4,3,2,1,0:T(8,128)}) custom-call(bf16[2,2,4,4,64,256]{5,4,3,2,1,0:T(8,128)(2,1)} %pad_maximum_fusion.1.xt_ffn, bf16[12,256,512]{2,1,0:T(8,128)(2,1)} %pad_maximum_fusion.y_ffn, bf16[2,2,4,4,64,256]{5,4,3,2,1,0:T(8,128)(2,1)} %pad_maximum_fusion.2.xt_att, ...), custom_call_target="tpu_custom_call" | custom-call | tf_op jit(solution)/shard_map/seq_sums/pallas_call | solution.py:319
  (618 shorter events, 268.6 us)
Async XLA Ops:
  7.2 160.5 %copy-start = (bf16[512,2048]{1,0:T(8,128)(2,1)S(1)}, bf16[512,2048]{1,0:T(8,128)(2,1)}, u32[]{:S(2)}) copy-start(bf16[512,2048]{1,0:T(8,128)(2,1)} %param.39) | copy-start | bytes 6291460
  7.2 147.4 %all-gather.9.cloned.1.call-start = ((), (), s32[]{:S(2)}) async-start(), calls=%async_computation.5 | async-start | bytes 2162688 | tf_op jit(solution)/shard_map/all_gather | solution.py:403
  12.9 13.3 %copy-start.107 = (bf16[2,64,64]{2,1,0:T(8,128)(2,1)S(1)}, bf16[2,64,64]{2,1,0:T(8,128)(2,1)}, u32[]{:S(2)}) copy-start(bf16[2,64,64]{2,1,0:T(8,128)(2,1)} %param.38) | copy-start | bytes 49156
  13.8 19.2 %copy-start.105 = (bf16[8,512]{1,0:T(8,128)(2,1)S(1)}, bf16[8,512]{1,0:T(8,128)(2,1)}, u32[]{:S(2)}) copy-start(bf16[8,512]{1,0:T(8,128)(2,1)} %param.30) | copy-start | bytes 24580
  14.1 11.6 %copy-start.43 = (bf16[256,128]{0,1:T(8,128)(2,1)}, bf16[256,128]{0,1:T(8,128)(2,1)S(1)}, u32[]{:S(2)}) copy-start(bf16[256,128]{0,1:T(8,128)(2,1)S(1)} %fusion.47) | copy-start | bytes 196612
  15.1 10.0 %collective-permute-start = (bf16[2,2,64,64]{2,3,1,0:T(8,128)(2,1)S(1)}, bf16[2,2,64,64]{2,3,1,0:T(8,128)(2,1)S(1)}, u32[]{:S(2)}, u32[]{:S(2)}) collective-permute-start(bf16[2,2,64,64]{2,3,1,0:T(8,128)(2,1)S(1)} %pad_maximum_fusion.10), channel_id=1, source_target_pairs={{0,4},{4,8},{8,12},{12,16},{16,20},{20,24},{24,28},{28,32},{32,36}... | collective-permute-start | bytes 98312 | tf_op jit(solution)/shard_map/ppermute | solution.py:396
  20.0 16.4 %copy-start.97 = (bf16[256,8]{0,1:T(8,128)(2,1)}, bf16[256,8]{0,1:T(8,128)(2,1)S(1)}, u32[]{:S(2)}) copy-start(bf16[256,8]{0,1:T(8,128)(2,1)S(1)} %convolution_convert_fusion.2) | copy-start | bytes 12292
  26.6 9.7 %copy-start.110 = (f32[2,320]{1,0:T(2,128)}, f32[2,320]{1,0:T(2,128)S(1)}, u32[]{:S(2)}) copy-start(f32[2,320]{1,0:T(2,128)S(1)} %get-tuple-element.408) | copy-start | bytes 7684
  33.0 318.5 %all-reduce.9.cloned.1.call-start = ((), (), s32[]{:S(2)}) async-start(), calls=%async_computation.1 | async-start | bytes 4194304 | tf_op jit(solution)/shard_map/psum | solution.py:640
  37.4 109.0 %copy-start.13 = (bf16[256,512]{0,1:T(8,128)(2,1)}, bf16[256,512]{0,1:T(8,128)(2,1)S(1)}, u32[]{:S(2)}) copy-start(bf16[256,512]{0,1:T(8,128)(2,1)S(1)} %copy.161) | copy-start | bytes 786436
  39.6 10.8 %copy-start.128 = (u32[128]{0:T(128)S(1)}, u32[128]{0:T(128)}, u32[]{:S(2)}) copy-start(u32[128]{0:T(128)} %constant.149) | copy-start | bytes 1540
  39.6 12.0 %copy-start.124 = (s32[3]{0:T(128)S(1)}, s32[3]{0:T(128)}, u32[]{:S(2)}) copy-start(s32[3]{0:T(128)} %copy-done.123) | copy-start | bytes 40
  43.3 103.1 %copy-start.44 = (bf16[256,128]{0,1:T(8,128)(2,1)S(1)}, bf16[256,128]{0,1:T(8,128)(2,1)}, u32[]{:S(2)}) copy-start(bf16[256,128]{0,1:T(8,128)(2,1)} %copy-done.43) | copy-start | bytes 196612
  45.4 72.5 %copy-start.85 = (f32[8,256]{1,0:T(8,128)}, f32[8,256]{1,0:T(8,128)S(1)}, u32[]{:S(2)}) copy-start(f32[8,256]{1,0:T(8,128)S(1)} %get-tuple-element.406) | copy-start | bytes 24580
  49.8 68.1 %copy-start.125 = (s32[256]{0:T(256)}, s32[256]{0:T(256)S(1)}, u32[]{:S(2)}) copy-start(s32[256]{0:T(256)S(1)} %iota_add_fusion.1) | copy-start | bytes 3076
  117.9 31.7 %copy-start.3 = (bf16[2,4,256,128]{3,2,1,0:T(8,128)(2,1)}, bf16[2,4,256,128]{3,2,1,0:T(8,128)(2,1)S(1)}, u32[]{:S(2)}) copy-start(bf16[2,4,256,128]{3,2,1,0:T(8,128)(2,1)S(1)} %pad_maximum_fusion.4) | copy-start | bytes 1572868
  119.5 30.0 %copy-start.57 = (pred[256,320]{0,1:T(8,128)(4,1)}, pred[256,320]{0,1:T(8,128)(4,1)S(1)}, u32[]{:S(2)}) copy-start(pred[256,320]{0,1:T(8,128)(4,1)S(1)} %get-tuple-element.401) | copy-start | bytes 245764
  161.7 302.4 %copy-start.109 = (f32[2,4,256]{2,1,0:T(4,128)}, f32[2,4,256]{2,1,0:T(4,128)S(1)}, u32[]{:S(2)}) copy-start(f32[2,4,256]{2,1,0:T(4,128)S(1)} %get-tuple-element.363) | copy-start | bytes 24580
  169.7 181.7 %copy-start.75 = (bf16[8,2048]{1,0:T(8,128)(2,1)S(1)}, bf16[8,2048]{1,0:T(8,128)(2,1)}, u32[]{:S(2)}) copy-start(bf16[8,2048]{1,0:T(8,128)(2,1)} %param.41) | copy-start | bytes 98308
  169.7 274.0 %all-reduce.11.cloned.1.call-start = ((), (), s32[]{:S(2)}) async-start(), calls=%async_computation.3 | async-start | bytes 4194304 | tf_op jit(solution)/shard_map/psum | solution.py:661
  180.4 173.5 %copy-start.99 = (bf16[256,8]{0,1:T(8,128)(2,1)}, bf16[256,8]{0,1:T(8,128)(2,1)S(1)}, u32[]{:S(2)}) copy-start(bf16[256,8]{0,1:T(8,128)(2,1)S(1)} %psum.29) | copy-start | bytes 12292
  180.4 174.8 %copy-start.94 = (f32[2048]{0:T(1024)S(1)}, f32[2048]{0:T(1024)}, u32[]{:S(2)}) copy-start(f32[2048]{0:T(1024)} %param.42) | copy-start | bytes 24580
  363.1 12.5 %slice-start = ((s8[8388608]{0:T(1024)(128)(4,1)}), s8[4194304]{0:T(1024)(128)(4,1)S(1)}, s32[]{:S(2)}) async-start(s8[8388608]{0:T(1024)(128)(4,1)} %bitcast.503), calls=%async_computation.7 | async-start | bytes 8388608
  366.8 8.8 %slice-start.1 = ((s8[8388608]{0:T(1024)(128)(4,1)}), s8[4194304]{0:T(1024)(128)(4,1)S(1)}, s32[]{:S(2)}) async-start(s8[8388608]{0:T(1024)(128)(4,1)} %bitcast.503), calls=%async_computation.8 | async-start | bytes 8388608
  385.1 139.5 %reduce-scatter.2.cloned.1.call-start = ((), (), s32[]{:S(2)}) async-start(), calls=%async_computation.2 | async-start | bytes 2621440 | tf_op jit(solution)/shard_map/reduce_scatter | solution.py:652
  392.8 133.8 %all-gather.11.cloned.1.call-start = ((), (), s32[]{:S(2)}) async-start(), calls=%async_computation.6 | async-start | bytes 2162688 | tf_op jit(solution)/shard_map/all_gather | solution.py:403
  471.9 259.5 %all-reduce.13.cloned.1.call-start = ((), (), s32[]{:S(2)}) async-start(), calls=%async_computation.4 | async-start | bytes 4194304 | tf_op jit(solution)/shard_map/psum | solution.py:768
  660.2 10.7 %copy-start.119 = (bf16[8,128]{1,0:T(8,128)(2,1)S(1)}, bf16[8,128]{1,0:T(8,128)(2,1)}, u32[]{:S(2)}) copy-start(bf16[8,128]{1,0:T(8,128)(2,1)} %param.33) | copy-start | bytes 6148
  660.9 7.5 collective-permute-start.1
  680.4 51.0 %copy-start.6 = (bf16[256,2048]{1,0:T(8,128)(2,1)S(1)}, bf16[256,2048]{1,0:T(8,128)(2,1)}, u32[]{:S(2)}) copy-start(bf16[256,2048]{1,0:T(8,128)(2,1)} %param.26) | copy-start | bytes 3145732
  685.5 49.3 %copy-start.122 = (f32[4,128]{1,0:T(4,128)S(1)}, f32[4,128]{1,0:T(4,128)}, u32[]{:S(2)}) copy-start(f32[4,128]{1,0:T(4,128)} %dynamic-slice_bitcast_fusion) | copy-start | bytes 6148
  685.5 49.3 %copy-start.126 = (f32[16]{0:T(128)S(1)}, f32[16]{0:T(128)}, u32[]{:S(2)}) copy-start(f32[16]{0:T(128)} %pad.27.clone) | copy-start | bytes 196
  (109 other events, 334.8 us)
Sparse Core Ops, SparseCore 0:
  33.1 45.9 all-gather.8
  169.8 181.5 all-reduce.8
  385.2 58.4 all-reduce.10
  446.0 29.5 reduce-scatter.1
  478.5 44.0 all-gather.10
  678.0 53.3 all-reduce.12

commit v2 on v0

v2 whole, which is shorter than its diff:
```python
import jax
import jax.numpy as jnp
from jax import lax
from jax.experimental import pallas as pl
from jax.experimental.pallas import tpu as pltpu
from jax.sharding import PartitionSpec as P

MESH = pl.DeviceIdType.MESH
F32 = jnp.float32
BF16 = jnp.bfloat16


def spot():
    s = lax.axis_index("seq")
    y = lax.axis_index("head")
    return lax.div(s, 8), lax.rem(lax.div(s, 2), 4), lax.rem(s, 2), y


def at(z, x, c, y):
    return ((z * 4 + x) * 2 + c, y)


def turned(p, steps):
    return lax.rem(p + steps, 4)


def greet(partners):
    barrier = pltpu.get_barrier_semaphore()
    for partner in partners:
        pl.semaphore_signal(barrier, inc=1, device_id=partner, device_id_type=MESH)
    pl.semaphore_wait(barrier, len(partners))


def send(src, dst, ss, rs, device):
    return pltpu.make_async_remote_copy(
        src_ref=src, dst_ref=dst, send_sem=ss, recv_sem=rs, device_id=device, device_id_type=MESH
    )


class Ring:
    def __init__(self, refs, rows, term, finish):
        self.sb, self.ra, self.rf, self.ra3, self.rf3, self.ss, self.rs = refs
        self.rows, self.term, self.finish = rows, term, finish
        z, x, c, y = spot()
        self.axes = (
            (x, at(z, turned(x, 1), c, y), at(z, turned(x, 3), c, y)),
            (z, at(turned(z, 1), x, c, y), at(turned(z, 3), x, c, y)),
        )

    @staticmethod
    def scratch(count, rows, width):
        return [
            pltpu.VMEM((count, 2, 4 * rows, width), BF16),
            pltpu.VMEM((count, 2, 2 * rows, width), BF16),
            pltpu.VMEM((count, 2, 4 * rows, width), BF16),
            pltpu.VMEM((count, 2, rows // 2, width), BF16),
            pltpu.VMEM((count, 2, rows, width), BF16),
            pltpu.SemaphoreType.DMA((count, 12)),
            pltpu.SemaphoreType.DMA((count, 12)),
        ]

    def block(self, b, part):
        g = self.rows // 2
        if part is None:
            return pl.ds(pl.multiple_of(b * self.rows, self.rows), self.rows)
        return pl.ds(pl.multiple_of(b * self.rows + part * g, g), g)

    def copy(self, t, k, i):
        p, ahead, behind = self.axes[k]
        q, ahead3, behind3 = self.axes[1 - k]
        h, g = 2 * self.rows, self.rows // 2
        lo, hi, lo3, hi3 = pl.ds(0, h), pl.ds(h, h), pl.ds(0, g), pl.ds(g, g)
        sb, ra, rf, ra3, rf3, block = self.sb, self.ra, self.rf, self.ra3, self.rf3, self.block
        src, dst, device = (
            lambda: (sb.at[t, 0, lo], ra.at[t, 0], ahead),
            lambda: (sb.at[t, 0, hi], ra.at[t, 1], behind),
            lambda: (sb.at[t, 1, hi], rf.at[t, 0, hi], ahead),
            lambda: (sb.at[t, 1, lo], rf.at[t, 1, lo], behind),
            lambda: (ra.at[t, 0], rf.at[t, 0, lo], ahead),
            lambda: (ra.at[t, 1], rf.at[t, 1, hi], behind),
            lambda: (sb.at[t, 0, block(turned(q, 2), 0)], ra3.at[t, 0], ahead3),
            lambda: (sb.at[t, 0, block(turned(q, 2), 1)], ra3.at[t, 1], behind3),
            lambda: (sb.at[t, 0, block(turned(q, 1), 1)], rf3.at[t, 0, hi3], ahead3),
            lambda: (sb.at[t, 0, block(turned(q, 3), 0)], rf3.at[t, 1, lo3], behind3),
            lambda: (ra3.at[t, 0], rf3.at[t, 0, lo3], ahead3),
            lambda: (ra3.at[t, 1], rf3.at[t, 1, hi3], behind3),
        )[i]()
        return send(src, dst, self.ss.at[t, i], self.rs.at[t, i], device)

    def start(self, t, k):
        p = self.axes[k][0]
        h = 2 * self.rows
        self.sb[t, 0] = self.term(t, k, turned(p, 2), 0, 4).astype(BF16)
        self.copy(t, k, 0).start()
        self.copy(t, k, 1).start()
        self.sb[t, 1, h:] = self.term(t, k, turned(p, 1), 2, 4).astype(BF16)
        self.copy(t, k, 2).start()
        self.sb[t, 1, :h] = self.term(t, k, turned(p, 3), 0, 2).astype(BF16)
        self.copy(t, k, 3).start()

    def merge(self, t, k):
        p = self.axes[k][0]
        for way, dest, first in ((0, turned(p, 1), 0), (1, turned(p, 3), 2)):
            self.copy(t, k, way).wait_recv()
            self.ra[t, way] = (self.term(t, k, dest, first, first + 2) + self.ra[t, way].astype(F32)).astype(BF16)
            self.copy(t, k, 4 + way).start()

    def cross(self, t, k):
        p = self.axes[k][0]
        own = self.term(t, k, p, 0, 4)
        for i in (0, 1):
            self.copy(t, k, i).wait_send()
        for i in (2, 3, 4, 5):
            self.copy(t, k, i).wait_recv()
        self.sb[t, 0] = (own + self.rf[t, 0].astype(F32) + self.rf[t, 1].astype(F32)).astype(BF16)
        for i in (6, 7, 8, 9):
            self.copy(t, k, i).start()

    def merge_cross(self, t, k):
        q = self.axes[1 - k][0]
        for way, dest in ((0, turned(q, 1)), (1, turned(q, 3))):
            self.copy(t, k, 6 + way).wait_recv()
            mine = self.sb[t, 0, self.block(dest, way), :]
            self.ra3[t, way] = (mine.astype(F32) + self.ra3[t, way].astype(F32)).astype(BF16)
            self.copy(t, k, 10 + way).start()

    def end(self, t, k):
        q = self.axes[1 - k][0]
        for i in (8, 9, 10, 11):
            self.copy(t, k, i).wait_recv()
        mine = self.sb[t, 0, self.block(q, None), :].astype(F32)
        self.finish(t, k, mine + self.rf3[t, 0].astype(F32) + self.rf3[t, 1].astype(F32))

    def drain(self, t, k):
        for i in range(2, 12):
            self.copy(t, k, i).wait_send()


def over_pairs(first, last, step):
    def both(u, carry):
        step(2 * u, 0)
        step(2 * u + 1, 1)
        return carry

    lax.fori_loop(first, last, both, 0)


FFN_TILES, FFN_WIDTH = 12, 512
ATT_TILES, ATT_WIDTH = 5, 256
PACK = 32


def untile(tiles):
    return tiles.transpose(1, 0, 2).reshape(tiles.shape[1], -1)


def unpack_small(packed):
    flat = packed.reshape(32, 32, 128)
    top = flat[:, :16].reshape(16, 2, 16, 128).transpose(1, 2, 0, 3).reshape(2, 16, 2048)
    a_rows = jnp.concatenate([top[0, :12], top[1, :12]])
    b_out = jnp.concatenate([top[0, 12:], top[1, 12:]])
    bottom = flat[:, 16:]
    f_query = bottom[:16].reshape(4, 64, 2, 64).transpose(0, 2, 1, 3).reshape(8, 64, 64)
    f_key = bottom[16:20].reshape(64, 2, 64).transpose(1, 0, 2)
    b_rows = bottom[20:23].reshape(6, 8, 128).transpose(1, 0, 2).reshape(8, 768)
    a_out = bottom[23:25].reshape(4, 8, 128).transpose(1, 0, 2).reshape(8, 512)
    gains = bottom[25]
    return a_rows, b_out, f_query, f_key, b_rows, a_out, gains[:4].reshape(512), gains[4:8].reshape(512)


EPS = 1e-05
NEG = -1e30
HIGH = lax.Precision.HIGHEST
ROWS = 256
WINDOW = 64
SPAN = ROWS + WINDOW
COLS = 512
HEADS, KEY_HEADS, DIM = 8, 2, 64
STATE = 72


def mm(a, b):
    return jnp.dot(a, b, preferred_element_type=F32)


def mm_nt(a, b, precision=None):
    return lax.dot_general(a, b, (((1,), (1,)), ((), ())), precision=precision, preferred_element_type=F32)


def mm_tn(a, b, precision=None):
    return lax.dot_general(a, b, (((0,), (0,)), ((), ())), precision=precision, preferred_element_type=F32)


def halves(value):
    top = value.astype(BF16)
    return top, (value - top.astype(F32)).astype(BF16)


def soft_pair(rows, table):
    both = mm(rows, jnp.concatenate([table, -table], axis=1))
    left = lax.broadcasted_iota(jnp.int32, both.shape, 1) < DIM
    upper = jnp.max(jnp.where(left, both, NEG), axis=1, keepdims=True)
    lower = jnp.max(jnp.where(left, NEG, both), axis=1, keepdims=True)
    grown = jnp.exp(both - jnp.where(left, upper, lower))
    sum_left = jnp.sum(jnp.where(left, grown, 0.0), axis=1, keepdims=True)
    sum_right = jnp.sum(jnp.where(left, 0.0, grown), axis=1, keepdims=True)
    return grown / jnp.where(left, sum_left, sum_right)


def doc_at(positions, lengths):
    first = lengths[0]
    second = first + lengths[1]
    return (
        (positions >= 0).astype(jnp.int32)
        + (positions >= first).astype(jnp.int32)
        + (positions >= second).astype(jnp.int32)
    )


def write_masks(near, far, lengths):
    base = lax.axis_index("seq") * ROWS
    row = lax.broadcasted_iota(jnp.int32, (ROWS, SPAN), 0) + base
    column = lax.broadcasted_iota(jnp.int32, (ROWS, SPAN), 1) + base - WINDOW
    same = doc_at(row, lengths) == doc_at(column, lengths)
    offset = row - column
    near[...] = jnp.where(same & (offset >= 0) & (offset < WINDOW), 0.0, NEG)
    far[...] = jnp.where(same & (offset >= WINDOW), 1.0, 0.0)


def middle(count, first, lengths):
    base = lax.axis_index("seq") * ROWS + first
    position = lax.broadcasted_iota(jnp.int32, (count, 1), 0) + base
    return (doc_at(position, lengths) == 2).astype(F32)


def value_columns(kv):
    lane = lax.broadcasted_iota(jnp.int32, kv.shape, 1)
    v = jnp.concatenate([kv[:, DIM:], kv[:, :DIM]], axis=1)
    return jnp.where(lane < DIM, v, jnp.where(lane == DIM, 1.0, 0.0).astype(kv.dtype))


class Scan:
    def __init__(self, refs, reverse):
        self.own, self.pair, self.line, self.plane, self.sem = refs
        self.reverse = reverse
        z, x, c, y = spot()
        self.z, self.x, self.c = z, x, c
        self.sibling = at(z, x, 1 - c, y)
        self.x_mates = [at(z, turned(x, i), c, y) for i in (1, 2, 3)]
        self.z_mates = [at(turned(z, i), x, c, y) for i in (1, 2, 3)]

    @staticmethod
    def scratch(shape):
        return [
            pltpu.VMEM((3, *shape), F32),
            pltpu.VMEM(shape, F32),
            pltpu.VMEM((3, *shape), F32),
            pltpu.VMEM((3, *shape), F32),
            pltpu.SemaphoreType.DMA((2, 7)),
        ]

    def pair_copy(self):
        return send(self.own.at[0], self.pair, self.sem.at[0, 0], self.sem.at[1, 0], self.sibling)

    def line_copy(self, i):
        return send(self.own.at[1], self.line.at[i], self.sem.at[0, 1 + i], self.sem.at[1, 1 + i], self.x_mates[i])

    def plane_copy(self, i):
        return send(self.own.at[2], self.plane.at[i], self.sem.at[0, 4 + i], self.sem.at[1, 4 + i], self.z_mates[i])

    def counts(self, me, other):
        return ((other > me) if self.reverse else (other < me)).astype(F32)

    def open(self):
        self.pair_copy().start()

    def along_x(self):
        self.pair_copy().wait()
        self.own[1] = self.own[0] + self.pair[...]
        for i in range(3):
            self.line_copy(i).start()

    def along_z(self):
        for i in range(3):
            self.line_copy(i).wait()
        self.own[2] = self.own[1] + self.line[0] + self.line[1] + self.line[2]
        for i in range(3):
            self.plane_copy(i).start()

    def close(self):
        for i in range(3):
            self.plane_copy(i).wait()
        total = self.pair[...] * self.counts(self.c, 1 - self.c)
        for i in range(3):
            total = total + self.line[i] * self.counts(self.x, turned(self.x, 3 - i))
        for i in range(3):
            total = total + self.plane[i] * self.counts(self.z, turned(self.z, 3 - i))
        return total


def front_kernel(
    x_ref, gain_one, gain_two, a_in, b_q, b_k, b_v, f_q, f_k, a_out, b_out, lengths, w_q, w_k, w_v, w_o,
    normed_out, low_out, q_out, kv_out, state_out, att_out, stat_out, mixed_out, lowmix_out, hidden_out, ns_out, r2_out, r1_out,
    wq, wk, wv, wo, w_sem, qh, phq, phk, num, near, far, tail_sem,
    part, came, y_sem, low_part, low_came, square, square_came,
    *scan_refs,
):
    z, x, c, y = spot()
    s = lax.axis_index("seq")
    following, leading = (lax.rem(s + 1, 32), y), (lax.rem(s + 31, 32), y)
    y_mates = [at(z, x, c, turned(y, i)) for i in (1, 2, 3)]
    scan = Scan(scan_refs, False)
    greet([following, leading, scan.sibling] + scan.x_mates + scan.z_mates + y_mates)
    loads = [
        pltpu.make_async_copy(src, dst, w_sem.at[i])
        for i, (src, dst) in enumerate(((w_q, wq), (w_k, wk), (w_v, wv), (w_o, wo)))
    ]
    for load in loads:
        load.start()
    for i in range(4):
        rows = pl.ds(64 * i, 64)
        value = x_ref[rows, :].astype(F32)
        scale = lax.rsqrt(jnp.mean(value * value, axis=1, keepdims=True) + EPS)
        r1_out[rows, :] = scale
        normed_out[rows, :] = (value * scale * gain_one[...]).astype(BF16)
    write_masks(near, far, lengths)
    low_out[...] = mm(normed_out[...], a_in[...]).astype(BF16)
    low = low_out[...]
    loads[1].wait()
    loads[2].wait()
    k = (mm(normed_out[...], wk[...]) + mm(low[:, 8:16], b_k[...])).astype(BF16)
    v = (mm(normed_out[...], wv[...]) + mm(low[:, 16:24], b_v[...])).astype(BF16)
    for j in range(KEY_HEADS):
        cut = slice(j * DIM, (j + 1) * DIM)
        kv_out[j, WINDOW:] = jnp.concatenate([k[:, cut], v[:, cut]], axis=1)
    tail = send(
        kv_out.at[:, pl.ds(ROWS, WINDOW)], kv_out.at[:, pl.ds(0, WINDOW)], tail_sem.at[0], tail_sem.at[1], following
    )
    tail.start()
    loads[0].wait()
    for i in range(2):
        cut = slice(i * 256, (i + 1) * 256)
        q_out[:, cut] = (mm(normed_out[...], wq[:, cut]) + mm(low[:, :8], b_q[:, cut])).astype(BF16)
    for h in range(HEADS):
        qh[h] = q_out[:, h * DIM : (h + 1) * DIM]
    tail.wait()
    inside = middle(ROWS, -WINDOW, lengths)
    for j in range(KEY_HEADS):
        phk[j] = soft_pair(kv_out[j][:, :DIM], f_k[j]).astype(BF16)
        counted = (phk[j, :ROWS].astype(F32) * inside).astype(BF16)
        scan.own[0, j] = mm_tn(value_columns(kv_out[j, :ROWS]), counted)[:STATE]
    scan.open()

    def features(h, carry):
        phq[h] = soft_pair(qh[h], f_q[h]).astype(BF16)
        return carry

    lax.fori_loop(0, HEADS, features, 0)
    scan.along_x()

    def inner(h, carry):
        j = lax.div(h, 4)
        kv = kv_out[j]
        scores = mm_nt(qh[h], kv[:, :DIM]) * (DIM**-0.5) + near[...]
        top = jnp.max(scores, axis=1, keepdims=True)
        weights = jnp.exp(scores - top)
        distant = mm_nt(phq[h], phk[j]) * far[...] * jnp.exp(-top)
        total = weights + distant
        high = total.astype(BF16)
        rest = ((total - high.astype(F32)) * far[...]).astype(BF16)
        v = kv[:, DIM:]
        num[h] = mm(high, v) + mm(rest, v)
        stat_out[h, :, 0:1] = top
        stat_out[h, :, 1:2] = jnp.sum(total, axis=1, keepdims=True)
        return carry

    lax.fori_loop(0, 4, inner, 0)
    scan.along_z()
    lax.fori_loop(4, HEADS, inner, 0)
    state_out[...] = scan.close()
    mine = middle(ROWS, 0, lengths)
    for h in range(HEADS):
        top, rest = halves(state_out[h // 4])
        carried = mm_nt(phq[h], top) + mm_nt(phq[h], rest)
        gate = jnp.exp(-stat_out[h, :, 0:1]) * mine
        total = stat_out[h, :, 1:2] + gate * carried[:, DIM : DIM + 1]
        stat_out[h, :, 1:2] = total
        stat_out[h, :, 2:3] = gate
        cut = slice(h * DIM, (h + 1) * DIM)
        attended = (num[h] + gate * carried[:, :DIM]) / total
        att_out[:, cut] = attended
        mixed_out[:, cut] = attended.astype(BF16)
    mixed = mixed_out[...]
    low_part[0] = mm_nt(a_out[...], mixed)
    low_turns = [send(low_part.at[0], low_came.at[i], y_sem.at[0, i], y_sem.at[1, i], y_mates[i]) for i in range(3)]
    for turn in low_turns:
        turn.start()
    loads[3].wait()

    def columns(ref, d):
        return ref[:, pl.ds(pl.multiple_of(d * COLS, COLS), COLS)]

    turns = [send(part.at[i], came.at[i], y_sem.at[0, 3 + i], y_sem.at[1, 3 + i], y_mates[i]) for i in range(3)]
    for i in (1, 0, 2):
        part[i] = mm(mixed, columns(wo, turned(y, 1 + i))).astype(BF16)
        turns[i].start()
    value = mm(mixed, columns(wo, y)) + columns(x_ref, y).astype(F32)
    for turn in low_turns:
        turn.wait()
    low_sum = low_part[0] + low_came[0] + low_came[1] + low_came[2]
    lowmix_out[...] = low_sum.T.astype(BF16)
    value = value + mm(lowmix_out[...], columns(b_out, y))
    for turn in turns:
        turn.wait()
    value = value + came[0].astype(F32) + came[1].astype(F32) + came[2].astype(F32)
    hidden_out[...] = value
    square[...] = mm_nt(jnp.ones((8, COLS), F32), value * value, HIGH)
    turns = [send(square, square_came.at[i], y_sem.at[0, 6 + i], y_sem.at[1, 6 + i], y_mates[i]) for i in range(3)]
    for turn in turns:
        turn.start()
    for turn in turns:
        turn.wait()
    mean = (square[...] + square_came[0] + square_came[1] + square_came[2]) * (1.0 / 2048)
    scale = lax.rsqrt(mean + EPS).T[:, 0:1]
    r2_out[...] = scale
    ns_out[y] = (hidden_out[...] * scale * columns(gain_two, y)).astype(BF16)
    turns = [send(ns_out.at[y], ns_out.at[y], y_sem.at[0, 9 + i], y_sem.at[1, 9 + i], y_mates[i]) for i in range(3)]
    for turn in turns:
        turn.start()
    for i in range(3):
        here = ns_out.at[turned(y, 3 - i)]
        send(here, here, y_sem.at[0, 9 + i], y_sem.at[1, 9 + i], y_mates[i]).wait_recv()
    for turn in turns:
        turn.wait_send()


def front(x, gain_one, gain_two, a_in, b_q, b_k, b_v, f_q, f_k, a_out, b_out, lengths, w_q, w_k, w_v, w_o):
    anywhere = pl.BlockSpec(memory_space=pl.ANY)
    vmem = pl.BlockSpec(memory_space=pltpu.VMEM)
    shapes = (
        ((ROWS, 2048), BF16),
        ((ROWS, 24), BF16),
        ((ROWS, 512), BF16),
        ((KEY_HEADS, SPAN, 128), BF16),
        ((KEY_HEADS, STATE, 128), F32),
        ((ROWS, 512), F32),
        ((HEADS, ROWS, 8), F32),
        ((ROWS, 512), BF16),
        ((ROWS, 8), BF16),
        ((ROWS, COLS), F32),
        ((4, ROWS, COLS), BF16),
        ((ROWS, 1), F32),
        ((ROWS, 1), F32),
    )
    return pl.pallas_call(
        front_kernel,
        out_shape=tuple(jax.ShapeDtypeStruct(*shape) for shape in shapes),
        in_specs=[vmem] * 11 + [pl.BlockSpec(memory_space=pltpu.SMEM)] + [anywhere] * 4,
        out_specs=(vmem,) * len(shapes),
        scratch_shapes=[
            pltpu.VMEM((2048, 512), BF16),
            pltpu.VMEM((2048, 128), BF16),
            pltpu.VMEM((2048, 128), BF16),
            pltpu.VMEM((512, 2048), BF16),
            pltpu.SemaphoreType.DMA((4,)),
            pltpu.VMEM((HEADS, ROWS, DIM), BF16),
            pltpu.VMEM((HEADS, ROWS, 128), BF16),
            pltpu.VMEM((KEY_HEADS, SPAN, 128), BF16),
            pltpu.VMEM((HEADS, ROWS, DIM), F32),
            pltpu.VMEM((ROWS, SPAN), F32),
            pltpu.VMEM((ROWS, SPAN), F32),
            pltpu.SemaphoreType.DMA((2,)),
            pltpu.VMEM((3, ROWS, COLS), BF16),
            pltpu.VMEM((3, ROWS, COLS), BF16),
            pltpu.SemaphoreType.DMA((2, 12)),
            pltpu.VMEM((1, 8, ROWS), F32),
            pltpu.VMEM((3, 8, ROWS), F32),
            pltpu.VMEM((8, ROWS), F32),
            pltpu.VMEM((3, 8, ROWS), F32),
            *Scan.scratch((KEY_HEADS, STATE, 128)),
        ],
        compiler_params=pltpu.CompilerParams(
            collective_id=1, has_side_effects=True, vmem_limit_bytes=60 * 2**20
        ),
        name="front",
    )(x, gain_one, gain_two, a_in, b_q, b_k, b_v, f_q, f_k, a_out, b_out, lengths, w_q, w_k, w_v, w_o)


def ffn_kernel(ns, cot, normed, wg, wu, wd, y_out, gs_out, ffn_out, xt_out, gs_sum, ffn_sum):
    j = pl.program_id(0)
    gate = jnp.zeros((ROWS, COLS), F32)
    up = jnp.zeros((ROWS, COLS), F32)
    for k in range(4):
        cut = slice(k * COLS, (k + 1) * COLS)
        gate = gate + mm(ns[k], wg[cut])
        up = up + mm(ns[k], wu[cut])
    grad = mm_nt(cot[...], wd[...])
    sigmoid = jax.nn.sigmoid(gate)
    active = gate * sigmoid
    hidden = (active * up).astype(BF16)
    grad_gate = (grad * up * sigmoid * (1.0 + gate * (1.0 - sigmoid))).astype(BF16)
    grad_up = (grad * active).astype(BF16)
    y_out[0, 0] = grad_gate
    y_out[1, 0] = grad_up
    y_out[2, 0] = hidden
    for k in range(4):
        cut = slice(k * COLS, (k + 1) * COLS)
        back = mm_nt(grad_gate, wg[cut]) + mm_nt(grad_up, wu[cut])
        forth = mm(hidden, wd[:, cut])

        @pl.when(j == 0)
        def _():
            gs_sum[k] = back
            ffn_sum[k] = forth

        @pl.when((j > 0) & (j < 3))
        def _():
            gs_sum[k] = gs_sum[k] + back
            ffn_sum[k] = ffn_sum[k] + forth

        @pl.when(j == 3)
        def _():
            gs_out[k] = (gs_sum[k] + back).astype(BF16)
            ffn_out[k] = (ffn_sum[k] + forth).astype(BF16)

    def turn(m, block_of):
        for i in range(16):
            block = block_of(i).T
            xt_out[m, 0, i // 4, i % 4] = block[:64]
            xt_out[m, 1, i // 4, i % 4] = block[64:]

    @pl.when(j == 0)
    def _():
        turn(0, lambda i: ns[i // 4, :, (i % 4) * 128 : (i % 4 + 1) * 128])

    @pl.when(j == 1)
    def _():
        turn(1, lambda i: cot[:, i * 128 : (i + 1) * 128])

    @pl.when(j == 2)
    def _():
        turn(2, lambda i: normed[:, i * 128 : (i + 1) * 128])


def ffn(ns, cot, normed, w_gate, w_up, w_down):
    def whole(*shape):
        return pl.BlockSpec(shape, lambda j: (0,) * len(shape))

    return pl.pallas_call(
        ffn_kernel,
        grid=(4,),
        out_shape=(
            jax.ShapeDtypeStruct((3, 4, ROWS, COLS), BF16),
            jax.ShapeDtypeStruct((4, ROWS, COLS), BF16),
            jax.ShapeDtypeStruct((4, ROWS, COLS), BF16),
            jax.ShapeDtypeStruct((3, 2, 4, 4, 64, ROWS), BF16),
        ),
        in_specs=[
            whole(4, ROWS, COLS),
            whole(ROWS, 2048),
            whole(ROWS, 2048),
            pl.BlockSpec((2048, COLS), lambda j: (0, j)),
            pl.BlockSpec((2048, COLS), lambda j: (0, j)),
            pl.BlockSpec((COLS, 2048), lambda j: (j, 0)),
        ],
        out_specs=(
            pl.BlockSpec((3, 1, ROWS, COLS), lambda j: (0, j, 0, 0)),
            whole(4, ROWS, COLS),
            whole(4, ROWS, COLS),
            whole(3, 2, 4, 4, 64, ROWS),
        ),
        scratch_shapes=[pltpu.VMEM((4, ROWS, COLS), F32), pltpu.VMEM((4, ROWS, COLS), F32)],
        compiler_params=pltpu.CompilerParams(vmem_limit_bytes=60 * 2**20),
        name="ffn",
    )(ns, cot, normed, w_gate, w_up, w_down)


def soft_back(soft, grad):
    left = lax.broadcasted_iota(jnp.int32, soft.shape, 1) < DIM
    part = soft * grad
    sum_left = jnp.sum(jnp.where(left, part, 0.0), axis=1, keepdims=True)
    sum_right = jnp.sum(jnp.where(left, 0.0, part), axis=1, keepdims=True)
    both = part - soft * jnp.where(left, sum_left, sum_right)
    return both[:, :DIM] - both[:, DIM:]


def back_kernel(
    hidden_in, r1, r2, gain_one, gain_two, mixed, low_mix, att, stat, state, q_in, kv, low,
    f_q, f_k, a_in, a_out, b_out, b_q, b_k, b_v, lengths,
    gs_hbm, ffn_hbm, normed_hbm, x_hbm, cot_hbm, xt_hbm, y_hbm, w_q, w_k, w_v, w_o,
    out_block, out_inputs, out_ffn, out_att, out_pack,
    wide_w, wk, wv, x_own, cot_own, gs_own, ffn_own, w_sem,
    gs_came, ffn_came, gf_part, dot_part, dot_came, gb, gres, gsum, y_sem,
    xf, yf, sem_ffn, xa, ya, xgb, sem_att, pk, sem_pack,
    near, far, qh, gh, pq, pkey, dext, dk, dv, gfq, gfk, ret, ret_came, ret_sem, glow, gkv, wide, gao, gbo,
    ysum, sem_zx,
    *rest,
):
    scan = Scan(rest[0:5], True)
    refs_big, refs_mid, refs_low = rest[5:12], rest[12:19], rest[19:26]
    z, x, c, y = spot()
    s = lax.axis_index("seq")
    following, leading = (lax.rem(s + 1, 32), y), (lax.rem(s + 31, 32), y)
    y_mates = [at(z, x, c, turned(y, i)) for i in (1, 2, 3)]
    sibling = scan.sibling
    greet([following, leading, sibling] + scan.x_mates + scan.z_mates + y_mates)

    def columns(ref, d):
        return ref[:, pl.ds(pl.multiple_of(d * COLS, COLS), COLS)]

    def to_mates(base, pieces, slots):
        return [
            send(pieces(i), slots.at[i], y_sem.at[0, base + i], y_sem.at[1, base + i], y_mates[i]) for i in range(3)
        ]

    own_columns = pl.ds(pl.multiple_of(y * COLS, COLS), COLS)
    gs_turns = to_mates(0, lambda i: gs_hbm.at[turned(y, 1 + i)], gs_came)
    for turn in gs_turns:
        turn.start()
    early = [
        pltpu.make_async_copy(src, dst, w_sem.at[i])
        for i, (src, dst) in enumerate(
            (
                (gs_hbm.at[y], gs_own),
                (cot_hbm.at[:, own_columns], cot_own),
                (x_hbm.at[:, own_columns], x_own),
                (ffn_hbm.at[y], ffn_own),
                (w_k, wk),
                (w_v, wv),
            )
        )
    ]

    def quarter(k):
        return pl.ds(k * COLS, COLS)

    load_o = [pltpu.make_async_copy(w_o.at[:, quarter(k)], wide_w.at[k], w_sem.at[6 + k]) for k in range(4)]
    load_q = [pltpu.make_async_copy(w_q.at[quarter(k)], wide_w.at[k], w_sem.at[10 + k]) for k in range(4)]
    load_n = [pltpu.make_async_copy(normed_hbm.at[:, quarter(k)], gb.at[k], w_sem.at[14 + k]) for k in range(4)]
    own_rows, far_rows = pl.ds(0, ROWS), pl.ds(ROWS, ROWS)

    def left_ffn(m):
        return [
            pltpu.make_async_copy(xt_hbm.at[m, c], xf.at[m, :, :, :, own_rows], sem_ffn.at[0, m]),
            send(xt_hbm.at[m, 1 - c], xf.at[m, :, :, :, far_rows], sem_ffn.at[1, m], sem_ffn.at[2, m], sibling),
        ]

    def right_ffn(t):
        return [
            pltpu.make_async_copy(y_hbm.at[t], yf.at[t, own_rows], sem_ffn.at[0, 2 + t]),
            send(y_hbm.at[t], yf.at[t, far_rows], sem_ffn.at[1, 2 + t], sem_ffn.at[2, 2 + t], sibling),
        ]

    left_att = [
        pltpu.make_async_copy(xt_hbm.at[2, c], xa.at[0, :, :, :, own_rows], sem_att.at[0, 0]),
        send(xt_hbm.at[2, 1 - c], xa.at[0, :, :, :, far_rows], sem_att.at[1, 0], sem_att.at[2, 0], sibling),
    ]

    def right_att(t):
        return send(ya.at[t, own_rows], ya.at[t, far_rows], sem_att.at[1, 2 + t], sem_att.at[2, 2 + t], sibling)

    for m in range(2):
        for copy in left_ffn(m):
            copy.start()

    def open_ffn(t, carry):
        for copy in right_ffn(t):
            copy.start()
        return carry

    lax.fori_loop(0, FFN_TILES, open_ffn, 0)
    for load in early + load_o:
        load.start()
    for copy in left_att:
        copy.start()

    def product(xd, yd, kind):
        def term(t, k, dest, first, last):
            m = kind(t)
            rows = xd[m, first:last, dest] if k == 0 else xd[m, dest, first:last]
            return mm(rows.reshape((last - first) * 64, 2 * ROWS), yd[t])

        return term

    def finish_ffn(t, k, value):
        out_ffn[t] = value

    def finish_att(t, k, value):
        out_att[t] = value

    def term_pack(t, k, dest, first, last):
        return (pk[c, first:last, dest] + pk[2, first:last, dest]).reshape((last - first) * PACK, 128)

    def finish_pack(t, k, value):
        out_pack[c, z, x] = value

    big = Ring(refs_big, 64, product(xf, yf, lambda t: lax.div(t, 8)), finish_ffn)
    mid = Ring(refs_mid, 64, product(xa, ya, lambda t: t // 3), finish_att)
    low_ring = Ring(refs_low, PACK, term_pack, finish_pack)

    for m in range(2):
        for copy in left_ffn(m):
            copy.wait()

    def first_ffn(t, k):
        for copy in right_ffn(t):
            copy.wait()
        big.start(t, k)

    over_pairs(0, 6, first_ffn)

    for load in early:
        load.wait()
    for turn in gs_turns:
        turn.wait()
    total = gs_own[...].astype(F32) + gs_came[0].astype(F32) + gs_came[1].astype(F32) + gs_came[2].astype(F32)
    gsum[...] = total
    ones = jnp.ones((8, COLS), F32)

    def mean_over(base, value):
        dot_part[...] = mm_nt(ones, value, HIGH)
        turns = to_mates(base, lambda i: dot_part, dot_came)
        for turn in turns:
            turn.start()
        return turns

    dot_turns = mean_over(3, total * columns(gain_two, y) * hidden_in[...])
    write_masks(near, far, lengths)
    for h in range(HEADS):
        qh[h] = q_in[:, h * DIM : (h + 1) * DIM]
    gain_rows_two = jnp.sum(total * hidden_in[...] * r2[...], axis=0, keepdims=True)
    for turn in dot_turns:
        turn.wait()

    def mean_column():
        return ((dot_part[...] + dot_came[0] + dot_came[1] + dot_came[2]) * (1.0 / 2048)).T[:, 0:1]

    scale = r2[...]
    residual = (
        cot_own[...].astype(F32)
        + scale * (gsum[...] * columns(gain_two, y))
        - hidden_in[...] * (scale * scale * scale * mean_column())
    )
    gres[...] = residual
    gb[y] = residual.astype(BF16)
    gb_turns = [
        send(gb.at[y], gb.at[y], y_sem.at[0, 6 + i], y_sem.at[1, 6 + i], y_mates[i]) for i in range(3)
    ]
    for turn in gb_turns:
        turn.start()
    ffn_turns = to_mates(9, lambda i: ffn_hbm.at[turned(y, 1 + i)], ffn_came)
    for turn in ffn_turns:
        turn.start()

    def features(h, carry):
        pq[h] = soft_pair(qh[h], f_q[h])
        return carry

    lax.fori_loop(0, HEADS, features, 0)
    for j in range(KEY_HEADS):
        pkey[j] = soft_pair(kv[j][:, :DIM], f_k[j])
    dk[...] = jnp.zeros(dk.shape, F32)
    dv[...] = jnp.zeros(dv.shape, F32)
    pk[...] = jnp.zeros(pk.shape, F32)
    over_pairs(0, 1, big.merge)

    for i in range(3):
        here = gb.at[turned(y, 3 - i)]
        send(here, here, y_sem.at[0, 6 + i], y_sem.at[1, 6 + i], y_mates[i]).wait_recv()
    for load in load_o:
        load.wait()
    grad_low = jnp.zeros((ROWS, 8), F32)
    grad_mixed = jnp.zeros((ROWS, COLS), F32)
    for k in range(4):
        cut = slice(k * COLS, (k + 1) * COLS)
        grad_low = grad_low + mm_nt(gb[k], b_out[:, cut])
        grad_mixed = grad_mixed + mm_nt(gb[k], wide_w[k])
    grad_mixed = grad_mixed + jnp.dot(
        grad_low, a_out[...].astype(F32), precision=HIGH, preferred_element_type=F32
    )
    rounded = grad_mixed.astype(BF16)
    for load in load_q:
        load.start()
    for h in range(HEADS):
        gh[h] = rounded[:, h * DIM : (h + 1) * DIM]
    top, bottom = halves(grad_low)
    gao[...] = mm_tn(top, mixed[...]) + mm_tn(bottom, mixed[...])
    gbo[...] = mm_tn(low_mix[...], gb[y])

    lane = lax.broadcasted_iota(jnp.int32, (ROWS, DIM), 1)
    for h in range(HEADS):
        j = h // 4
        grad = gh[h].astype(F32)
        den = stat[h, :, 1:2]
        inner = -jnp.sum(grad * att[:, h * DIM : (h + 1) * DIM], axis=1, keepdims=True) / den
        ext = jnp.concatenate([grad / den, jnp.where(lane == 0, inner, 0.0)], axis=1)
        dext[h] = ext
        top, bottom = halves(ext * stat[h, :, 2:3])
        phi = pq[h].astype(BF16)
        piece = (mm_tn(top, phi) + mm_tn(bottom, phi))[:STATE]
        scan.own[0, j] = piece if h % 4 == 0 else scan.own[0, j] + piece
    scan.open()

    for i in range(16):
        block = gb[i // 4, :, (i % 4) * 128 : (i % 4 + 1) * 128].T
        xa[1, i // 4, i % 4, :, 0:ROWS] = jnp.where(c == 0, block[:64], block[64:])
        xgb[i // 4, i % 4] = jnp.where(c == 0, block[64:], block[:64])
    for turn in gb_turns:
        turn.wait_send()
    for load in load_n:
        load.start()
    left_gb = send(xgb, xa.at[1, :, :, :, far_rows], sem_att.at[1, 1], sem_att.at[2, 1], sibling)
    left_gb.start()
    for t in (3, 4):
        ya[t, 0:ROWS] = mixed[:, (t - 3) * ATT_WIDTH : (t - 2) * ATT_WIDTH]
        right_att(t).start()
    scan.along_x()
    left_gb.wait()
    for t in (3, 4):
        right_att(t).wait()
        mid.start(t, t % 2)

    def backward(h, carry):
        j = lax.div(h, 4)
        keys, values = kv[j][:, :DIM], kv[j][:, DIM:]
        q, grad, ext = qh[h], gh[h], dext[h]
        top, den, gate = stat[h, :, 0:1], stat[h, :, 1:2], stat[h, :, 2:3]
        soft = pq[h]
        phi, phi_key = soft.astype(BF16), pkey[j].astype(BF16)
        damping = far[...] * jnp.exp(-top)
        weights = jnp.exp(mm_nt(q, keys) * (DIM**-0.5) + near[...] - top)
        grad_weights = mm_nt(grad, values) / den + ext[:, DIM : DIM + 1]
        grad_scores = (weights * grad_weights).astype(BF16)
        grad_linear = (damping * grad_weights).astype(BF16)
        both = weights.astype(BF16).astype(F32) + mm_nt(phi, phi_key) * damping
        high, rest = halves(both / den)
        grad_q = mm(grad_scores, keys) * (DIM**-0.5)
        dk[j] = dk[j] + mm_tn(grad_scores, q) * (DIM**-0.5)
        dv[j] = dv[j] + mm_tn(high, grad) + mm_tn(rest, grad)
        pkey[KEY_HEADS + j] = pkey[KEY_HEADS + j] + mm_tn(grad_linear, phi)
        carried = jnp.dot(
            (ext * gate)[:, :STATE], state[j], precision=HIGH, preferred_element_type=F32
        )
        grad_soft = mm(grad_linear, phi_key) + carried
        high, rest = halves(soft_back(soft, grad_soft))
        qh[h] = (grad_q + mm_nt(high, f_q[h]) + mm_nt(rest, f_q[h])).astype(BF16)
        gfq[h] = mm_tn(q, high) + mm_tn(q, rest)

        @pl.when(h == 1)
        def _():
            scan.along_z()

        @pl.when(h < 5)
        def _():
            big.merge(2 * h + 2, 0)
            big.merge(2 * h + 3, 1)

        @pl.when(h >= 5)
        def _():
            big.cross(2 * h - 10, 0)
            big.cross(2 * h - 9, 1)

        return carry

    for j in range(KEY_HEADS):
        pkey[KEY_HEADS + j] = jnp.zeros((SPAN, 128), F32)
    lax.fori_loop(0, HEADS, backward, 0)

    inside = middle(ROWS, -WINDOW, lengths)
    suffix = scan.close()
    for j in range(KEY_HEADS):
        soft = pkey[j]
        high, rest = halves(suffix[j])
        rows = value_columns(kv[j, :ROWS])[:, :STATE]
        grad_phi = pkey[KEY_HEADS + j]
        carried = (mm(rows, high) + mm(rows, rest)) * inside
        grad_phi = jnp.concatenate([grad_phi[:ROWS] + carried, grad_phi[ROWS:]], axis=0)
        phi = soft[:ROWS].astype(BF16)
        dv[j, :ROWS] = dv[j, :ROWS] + ((mm_nt(phi, high) + mm_nt(phi, rest)) * inside)[:, :DIM]
        high, rest = halves(soft_back(soft, grad_phi))
        dk[j] = dk[j] + mm_nt(high, f_k[j]) + mm_nt(rest, f_k[j])
        keys = kv[j][:, :DIM]
        gfk[j] = mm_tn(keys, high) + mm_tn(keys, rest)
        ret[j] = jnp.concatenate([dk[j, :WINDOW], dv[j, :WINDOW]], axis=1)
    back = send(ret, ret_came, ret_sem.at[0], ret_sem.at[1], leading)
    back.start()
    gq = jnp.concatenate([qh[h] for h in range(HEADS)], axis=1)
    for i in range(2):
        ya[i, 0:ROWS] = gq[:, i * ATT_WIDTH : (i + 1) * ATT_WIDTH]
        right_att(i).start()
    for turn in ffn_turns:
        turn.wait()
    out_block[...] = (
        hidden_in[...]
        + ffn_own[...].astype(F32)
        + ffn_came[0].astype(F32)
        + ffn_came[1].astype(F32)
        + ffn_came[2].astype(F32)
    ).astype(BF16)
    back.wait()
    for j in range(KEY_HEADS):
        dk[j, ROWS:] = dk[j, ROWS:] + ret_came[j][:, :DIM]
        dv[j, ROWS:] = dv[j, ROWS:] + ret_came[j][:, DIM:]
    gk = jnp.concatenate([dk[j, WINDOW:] for j in range(KEY_HEADS)], axis=1).astype(BF16)
    gv = jnp.concatenate([dv[j, WINDOW:] for j in range(KEY_HEADS)], axis=1).astype(BF16)
    gkv[...] = jnp.concatenate([gk, gv], axis=1)
    ya[2, 0:ROWS] = gkv[...]
    right_att(2).start()

    for load in load_q + load_n:
        load.wait()
    glow[...] = jnp.concatenate([mm_nt(gq, b_q[...]), mm_nt(gk, b_k[...]), mm_nt(gv, b_v[...])], axis=1)
    glow_high, glow_rest = halves(glow[...])

    def partial_first(d):
        rows = pl.ds(pl.multiple_of(d * COLS, COLS), COLS)
        down = a_in[rows, :]
        return (
            mm_nt(gq, wide_w[d])
            + mm_nt(gkv[:, :128], wk[rows, :])
            + mm_nt(gkv[:, 128:], wv[rows, :])
            + mm_nt(glow_high, down)
            + mm_nt(glow_rest, down)
        )

    gf_turns = to_mates(12, lambda i: gf_part.at[i], gs_came)
    for i in (1, 0, 2):
        gf_part[i] = partial_first(turned(y, 1 + i)).astype(BF16)
        gf_turns[i].start()
    gsum[...] = partial_first(y)
    for copy in left_att:
        copy.wait()
    for t in range(3):
        right_att(t).wait()
        mid.start(t, t % 2)

    for k in range(4):
        wide[:, k * COLS : (k + 1) * COLS] = mm_tn(glow_high, gb[k]) + mm_tn(glow_rest, gb[k])
    for i in range(16):
        for half in range(2):
            d = 2 * i + half
            pk[d // 16, d // 4 % 4, d % 4, 0:12] = wide[12 * half : 12 * half + 12, i * 128 : (i + 1) * 128]
    for i in range(4):
        for half in range(2):
            d = 2 * i + half
            pk[lax.div(y, 2), lax.rem(y, 2) * 2 + d // 4, d % 4, 12:16] = gbo[
                4 * half : 4 * half + 4, i * 128 : (i + 1) * 128
            ]

    def low_half(d, value):
        pk[d // 16, d // 4 % 4, d % 4, 16 : 16 + value.shape[0]] = value

    for i in range(4):
        pair = jnp.concatenate([gfq[2 * i], gfq[2 * i + 1]], axis=1)
        for part in range(4):
            low_half(4 * i + part, pair[16 * part : 16 * part + 16])
    pair = jnp.concatenate([gfk[0], gfk[1]], axis=1)
    for part in range(4):
        low_half(16 + part, pair[16 * part : 16 * part + 16])
    grad_b = jnp.concatenate(
        [mm_tn(low[:, :8], gq), mm_tn(low[:, 8:16], gkv[:, :128]), mm_tn(low[:, 16:24], gkv[:, 128:])], axis=1
    )
    for i in range(3):
        low_half(20 + i, jnp.concatenate([grad_b[:, 256 * i : 256 * i + 128], grad_b[:, 256 * i + 128 : 256 * i + 256]]))
    for i in range(2):
        low_half(
            23 + i, jnp.concatenate([gao[:, 256 * i : 256 * i + 128], gao[:, 256 * i + 128 : 256 * i + 256]])
        )
    for turn in gf_turns:
        turn.wait()
    total = gsum[...] + gs_came[0].astype(F32) + gs_came[1].astype(F32) + gs_came[2].astype(F32)
    gsum[...] = total
    inputs = x_own[...].astype(F32)
    gain_rows_one = jnp.sum(total * inputs * r1[...], axis=0, keepdims=True)
    low_half(
        25,
        jnp.concatenate([rows[:, i * 128 : (i + 1) * 128] for rows in (gain_rows_one, gain_rows_two) for i in range(4)]),
    )
    pack_far = send(pk.at[1 - c], pk.at[2], sem_pack.at[0], sem_pack.at[1], sibling)
    pack_far.start()
    dot_turns = mean_over(15, total * columns(gain_one, y) * inputs)
    pack_far.wait()
    low_ring.start(0, 0)
    for turn in dot_turns:
        turn.wait()
    scale = r1[...]
    out_inputs[...] = (
        gres[...]
        + scale * (gsum[...] * columns(gain_one, y))
        - x_own[...].astype(F32) * (scale * scale * scale * mean_column())
    )
    for t in (3, 4, 0, 1, 2):
        mid.merge(t, t % 2)
    low_ring.merge(0, 0)
    over_pairs(3, 6, big.cross)
    for t in (3, 4, 0, 1, 2):
        mid.cross(t, t % 2)
    low_ring.cross(0, 0)
    over_pairs(0, 6, big.merge_cross)
    for t in (3, 4, 0, 1, 2):
        mid.merge_cross(t, t % 2)
    low_ring.merge_cross(0, 0)
    low_ring.end(0, 0)
    crown = pl.ds(0, 16)
    turns = to_mates(18, lambda i: out_pack.at[c, z, x, crown], ysum)
    for turn in turns:
        turn.start()
    for turn in turns:
        turn.wait()
    out_pack[c, z, x, crown] = out_pack[c, z, x, crown] + ysum[0] + ysum[1] + ysum[2]

    def spread(base, piece, mates, back_piece):
        turns = [
            send(piece, piece, sem_zx.at[0, base + i], sem_zx.at[1, base + i], mate) for i, mate in enumerate(mates)
        ]
        for turn in turns:
            turn.start()
        return [
            send(back_piece(i), back_piece(i), sem_zx.at[0, base + i], sem_zx.at[1, base + i], mate)
            for i, mate in enumerate(mates)
        ]

    turns = spread(0, out_pack.at[c, z, x], scan.z_mates, lambda i: out_pack.at[c, turned(z, 3 - i), x])
    over_pairs(0, 6, big.end)
    for turn in turns:
        turn.wait()
    turns = spread(3, out_pack.at[c, :, x], scan.x_mates, lambda i: out_pack.at[c, :, turned(x, 3 - i)])
    for t in (3, 4, 0, 1, 2):
        mid.end(t, t % 2)
    for turn in turns:
        turn.wait()
    turns = spread(6, out_pack.at[c], [sibling], lambda i: out_pack.at[1 - c])
    over_pairs(0, 6, big.drain)
    for t in range(ATT_TILES):
        mid.drain(t, t % 2)
    low_ring.drain(0, 0)
    for turn in turns:
        turn.wait()


def back(args, weights):
    anywhere = pl.BlockSpec(memory_space=pl.ANY)
    vmem = pl.BlockSpec(memory_space=pltpu.VMEM)
    shapes = (
        ((ROWS, COLS), BF16),
        ((ROWS, COLS), F32),
        ((FFN_TILES, 64, FFN_WIDTH), F32),
        ((ATT_TILES, 64, ATT_WIDTH), F32),
        ((2, 4, 4, PACK, 128), F32),
    )
    block = (ROWS, COLS)
    return pl.pallas_call(
        back_kernel,
        out_shape=tuple(jax.ShapeDtypeStruct(*shape) for shape in shapes),
        in_specs=[vmem] * 21 + [pl.BlockSpec(memory_space=pltpu.SMEM)] + [anywhere] * 11,
        out_specs=(vmem,) * len(shapes),
        scratch_shapes=[
            pltpu.VMEM((4, 512, 512), BF16),
            pltpu.VMEM((2048, 128), BF16),
            pltpu.VMEM((2048, 128), BF16),
            pltpu.VMEM(block, BF16),
            pltpu.VMEM(block, BF16),
            pltpu.VMEM(block, BF16),
            pltpu.VMEM(block, BF16),
            pltpu.SemaphoreType.DMA((18,)),
            pltpu.VMEM((3, *block), BF16),
            pltpu.VMEM((3, *block), BF16),
            pltpu.VMEM((3, *block), BF16),
            pltpu.VMEM((8, ROWS), F32),
            pltpu.VMEM((3, 8, ROWS), F32),
            pltpu.VMEM((4, *block), BF16),
            pltpu.VMEM(block, F32),
            pltpu.VMEM(block, F32),
            pltpu.SemaphoreType.DMA((2, 21)),
            pltpu.VMEM((2, 4, 4, 64, 512), BF16),
            pltpu.VMEM((FFN_TILES, 512, FFN_WIDTH), BF16),
            pltpu.SemaphoreType.DMA((3, 2 + FFN_TILES)),
            pltpu.VMEM((2, 4, 4, 64, 512), BF16),
            pltpu.VMEM((ATT_TILES, 512, ATT_WIDTH), BF16),
            pltpu.VMEM((4, 4, 64, ROWS), BF16),
            pltpu.SemaphoreType.DMA((3, 2 + ATT_TILES)),
            pltpu.VMEM((3, 4, 4, PACK, 128), F32),
            pltpu.SemaphoreType.DMA((2,)),
            pltpu.VMEM((ROWS, SPAN), F32),
            pltpu.VMEM((ROWS, SPAN), F32),
            pltpu.VMEM((HEADS, ROWS, DIM), BF16),
            pltpu.VMEM((HEADS, ROWS, DIM), BF16),
            pltpu.VMEM((HEADS, ROWS, 128), F32),
            pltpu.VMEM((2 * KEY_HEADS, SPAN, 128), F32),
            pltpu.VMEM((HEADS, ROWS, 128), F32),
            pltpu.VMEM((KEY_HEADS, SPAN, DIM), F32),
            pltpu.VMEM((KEY_HEADS, SPAN, DIM), F32),
            pltpu.VMEM((HEADS, DIM, DIM), F32),
            pltpu.VMEM((KEY_HEADS, DIM, DIM), F32),
            pltpu.VMEM((KEY_HEADS, WINDOW, 128), F32),
            pltpu.VMEM((KEY_HEADS, WINDOW, 128), F32),
            pltpu.SemaphoreType.DMA((2,)),
            pltpu.VMEM((ROWS, 24), F32),
            pltpu.VMEM((ROWS, 256), BF16),
            pltpu.VMEM((24, 2048), F32),
            pltpu.VMEM((8, COLS), F32),
            pltpu.VMEM((8, COLS), F32),
            pltpu.VMEM((3, 16, 128), F32),
            pltpu.SemaphoreType.DMA((2, 7)),
            *Scan.scratch((KEY_HEADS, STATE, 128)),
            *Ring.scratch(FFN_TILES, 64, FFN_WIDTH),
            *Ring.scratch(ATT_TILES, 64, ATT_WIDTH),
            *Ring.scratch(1, PACK, 128),
        ],
        compiler_params=pltpu.CompilerParams(
            collective_id=2, has_side_effects=True, vmem_limit_bytes=63 * 2**20
        ),
        name="back",
    )(*args, *weights)


def body(
    inputs,
    gain_first,
    w_query,
    a_query,
    b_query,
    key_projection_weight,
    a_key,
    key_adapter_second,
    value_projection_weight,
    a_value,
    value_adapter_second,
    feature_query,
    key_hedgehog_map,
    w_out,
    a_out,
    b_out,
    gain_second,
    w_gate,
    w_up,
    w_down,
    lengths,
    cotangent,
):
    gain_one, gain_two = gain_first[None], gain_second[None]
    a_in = jnp.concatenate([a_query, a_key, a_value], axis=1)
    a_out = a_out.T
    projections = (w_query, key_projection_weight, value_projection_weight, w_out)
    normed, low, queries, kv, state, att, stat, mixed, low_mix, hidden_in, ns, r2, r1 = front(
        inputs, gain_one, gain_two, a_in, b_query, key_adapter_second, value_adapter_second,
        feature_query, key_hedgehog_map, a_out, b_out, lengths, *projections,
    )
    y_ffn, gs, ffn_sum, xt = ffn(ns, cotangent, normed, w_gate, w_up, w_down)
    block_out, grad_inputs, out_ffn, out_att, out_pack = back(
        (
            hidden_in, r1, r2, gain_one, gain_two, mixed, low_mix, att, stat, state, queries, kv, low,
            feature_query, key_hedgehog_map, a_in, a_out, b_out, b_query, key_adapter_second,
            value_adapter_second, lengths,
        ),
        (gs, ffn_sum, normed, inputs, cotangent, xt, y_ffn.reshape(FFN_TILES, ROWS, FFN_WIDTH), *projections),
    )
    a_rows, b_out_sum, f_query, f_key, b_rows, a_out_sum, gain_one, gain_two = unpack_small(out_pack)
    a_rows = a_rows.T
    return (
        block_out,
        grad_inputs,
        gain_one,
        untile(out_att[:2]),
        a_rows[:, :8],
        b_rows[:, :512],
        out_att[2, :, :128],
        a_rows[:, 8:16],
        b_rows[:, 512:640],
        out_att[2, :, 128:],
        a_rows[:, 16:],
        b_rows[:, 640:],
        f_query,
        f_key,
        untile(out_att[3:]).T,
        a_out_sum.T,
        b_out_sum,
        gain_two,
        untile(out_ffn[:4]),
        untile(out_ffn[4:8]),
        untile(out_ffn[8:]).T,
    )


def solution(mesh):
    return jax.shard_map(
        body,
        mesh=mesh,
        in_specs=(
            P("seq", None),
            P(),
            P(None, "head"),
            P(),
            P(None, "head"),
            P(None, "head"),
            P(),
            P(None, "head"),
            P(None, "head"),
            P(),
            P(None, "head"),
            P("head", None, None),
            P("head", None, None),
            P("head", None),
            P("head", None),
            P(),
            P(),
            P(None, "head"),
            P(None, "head"),
            P("head", None),
            P(),
            P("seq", None),
        ),
        out_specs=(
            P("seq", "head"),
            P("seq", "head"),
            P("head"),
            P("seq", "head"),
            P(),
            P(None, "head"),
            P("seq", "head"),
            P(),
            P(None, "head"),
            P("seq", "head"),
            P(),
            P(None, "head"),
            P("head", None, None),
            P("head", None, None),
            P("head", "seq"),
            P("head", None),
            P(),
            P("head"),
            P("seq", "head"),
            P("seq", "head"),
            P("head", "seq"),
        ),
        check_vma=False,
    )
```

time: 1780 us -> 240 us (0.13)
  waiting for transfers between devices: 1300 us -> 0 us
  Pallas kernels: 0 us -> 218 us
  matrix products: 138 us -> 0 us
  blocking collectives: 126 us -> 0 us
  local copies, waits for them, and re-layouts: 95.8 us -> 18.7 us
  other arithmetic: 59 us -> 1.47 us
  loops' own time: 20.7 us -> 0 us
    reduce_scatter x8 -> x0, waiting for transfers between devices: 687 us -> none  [the longest x1 119 us: body(): lax.psum_scatter(grad_w_gate, 'seq', scatter_dimension=0, tiled=True)]
    psum x6 -> x0, waiting for transfers between devices: 606 us -> none  [the longest x2 201 us: body(): lax.psum((lax.dynamic_slice_in_dim(grad_gain_first, column_at, columns, 0...]
    pallas_call x0 -> x3, Pallas kernels: none -> 218 us  [the longest x1 129 us: back(): pl.pallas_call(back_kernel, out_shape=tuple((jax.ShapeDtypeStruct(*shape)...]
    dot_general x67 -> x0, matrix products: 132 us -> none  [the longest x11 36.9 us: transpose_by(): lax.dot_general(left_side, right_side, (((0,), (0,)), ((), ())), preferre...]
    unnamed x1 -> x0, blocking collectives: 63 us -> none
    all_gather x2 -> x0, blocking collectives: 53.9 us -> none  [entering(): gathered = jax.tree.map(lambda a: lax.all_gather(a, axis), part)]
    dynamic_slice x95 -> x0, local copies, waits for them, and re-layouts: 50.1 us -> none  [the longest x93 48.1 us: one(): lax.dynamic_index_in_dim(a, source, 0, False)]
    unnamed x283 -> x11, local copies, waits for them, and re-layouts: 36.6 us -> 3.25 us
  transfers between devices with their start and end apart: 18 -> 0, of which waited for: 15 -> 0; matrix products, arithmetic and copies ran while one was open for 6% -> 0% of each run, Pallas kernels for 0% -> 0%
where the time goes in v2:
time: 240 us; the launch traced here: 239 us
  Pallas kernels  218 us (91%)
  local copies, waits for them, and re-layouts  18.7 us (8%)
    pallas_call x1, Pallas kernels, back(): pl.pallas_call(back_kernel, out_shape=tuple((jax.ShapeDtypeStruct(*shape)...  129 us
    pallas_call x1, Pallas kernels, front(): pl.pallas_call(front_kernel, out_shape=tuple((jax.ShapeDtypeStruct(*shape...  63 us
    pallas_call x1, Pallas kernels, ffn(): pl.pallas_call(ffn_kernel, grid=(4,), out_shape=(jax.ShapeDtypeStruct((3,...  26.1 us

profile of v2, /device:TPU:1, one launch (start us, length us, event | category | flops | bytes accessed | tf_op | source)
XLA Modules:
  0.0 239.0 jit_solution(775399373967028319)
XLA Ops:
  0.7 0.8 pad_maximum_fusion
  1.5 1.0 copy.59.a_in
  2.5 63.0 %front.1 = (bf16[256,2048]{1,0:T(8,128)(2,1)}, bf16[256,24]{1,0:T(8,128)(2,1)}, bf16[256,512]{1,0:T(8,128)(2,1)}, bf16[2,320,128]{2,1,0:T(8,128)(2,1)}, f32[2,72...) custom-call(bf16[256,2048]{1,0:T(8,128)(2,1)} %x_hbm.1, ...), custom_call_target="tpu_custom_call" | custom-call | tf_op jit(solution)/shard_map/front/pallas_call | solution.py:455
  65.5 26.1 %ffn.1 = (bf16[3,4,256,512]{3,2,1,0:T(8,128)(2,1)}, bf16[4,256,512]{2,1,0:T(8,128)(2,1)}, bf16[4,256,512]{2,1,0:T(8,128)(2,1)}, bf16[3,2,4,4,64,256]{5,4,3,2,1,0:T(8,128)(2,1)}) custom-call(bf16[4,256,512]{2,1,0:T(8,128)(2,1)} %get-tuple-element.54.ns, bf16[256,2048]{1,0:T(8,128)(2,1)} %cot_hbm.1, bf16[256,2048]{1,0:T(8,128)(2,1)} %get-tuple-element.55.normed.normed_hbm, ...), custom_call_target="tpu_custom_call" | custom-call | tf_op jit(solution)/shard_map/ffn/pallas_call | solution.py:549
  91.6 128.9 %back.1 = (bf16[256,512]{1,0:T(8,128)(2,1)}, f32[256,512]{1,0:T(8,128)}, f32[12,64,512]{2,1,0:T(8,128)}, f32[5,64,256]{2,1,0:T(8,128)}, f32[2,4,4,32,128]{4,3,2,1,0:T(8,128)}) custom-call(f32[256,512]{1,0:T(8,128)} %get-tuple-element.43.hidden_in, f32[256,1]{1,0:T(8,128)} %get-tuple-element.44.r1, f32[256,1]{1,0:T(8,128)} %get-tuple-element.45.r2, ...), custom_call_target="tpu_custom_call" | custom-call | tf_op jit(solution)/shard_map/back/pallas_call | solution.py:1052
  220.5 0.0 copy-start
  220.5 1.4 slice_bitcast_fusion.11
  221.9 1.3 slice.120
  223.2 0.7 slice.112
  224.0 0.6 fusion.1
  224.6 0.6 slice.113
  225.2 0.8 slice.119
  225.9 0.1 reshape.110
  226.0 0.6 copy.68
  226.7 1.4 slice_bitcast_fusion.9
  228.1 1.0 slice_bitcast_fusion.5
  229.1 0.7 copy.70
  229.7 0.7 copy.69
  230.4 0.9 slice.118
  231.3 1.0 slice.108
  232.3 0.2 copy.75
  232.5 0.6 pad_maximum_fusion.1
  233.2 0.7 fusion
  233.9 0.2 reshape.108
  234.1 0.7 copy.63
  234.8 0.0 copy-done
  234.8 0.1 slice_bitcast_fusion
  235.0 0.8 copy.73
  235.8 0.8 copy.72
  236.6 0.8 copy.71
  237.5 0.7 copy.78
  238.2 0.8 copy.79
  (8 shorter events, 0.1 us)
Async XLA Ops:
  220.5 14.3 %copy-start = (f32[12,64,512]{2,1,0:T(8,128)S(1)}, f32[12,64,512]{2,1,0:T(8,128)}, u32[]{:S(2)}) copy-start(f32[12,64,512]{2,1,0:T(8,128)} %get-tuple-element.64) | copy-start | bytes 4718596
  234.8 2.6 %copy-start.2 = (bf16[256,512]{1,0:T(8,128)(2,1)S(1)}, bf16[256,512]{1,0:T(8,128)(2,1)}, u32[]{:S(2)}) copy-start(bf16[256,512]{1,0:T(8,128)(2,1)} %get-tuple-element.146) | copy-start | bytes 786436
  234.8 3.3 %copy-start.1 = (f32[256,512]{1,0:T(8,128)S(1)}, f32[256,512]{1,0:T(8,128)}, u32[]{:S(2)}) copy-start(f32[256,512]{1,0:T(8,128)} %get-tuple-element.147) | copy-start | bytes 1572868

commit v3 on v2

--- a/solution.py
+++ b/solution.py
@@ -150,24 +150,6 @@
 PACK = 32
 
 
-def untile(tiles):
-    return tiles.transpose(1, 0, 2).reshape(tiles.shape[1], -1)
-
-
-def unpack_small(packed):
-    flat = packed.reshape(32, 32, 128)
-    top = flat[:, :16].reshape(16, 2, 16, 128).transpose(1, 2, 0, 3).reshape(2, 16, 2048)
-    a_rows = jnp.concatenate([top[0, :12], top[1, :12]])
-    b_out = jnp.concatenate([top[0, 12:], top[1, 12:]])
-    bottom = flat[:, 16:]
-    f_query = bottom[:16].reshape(4, 64, 2, 64).transpose(0, 2, 1, 3).reshape(8, 64, 64)
-    f_key = bottom[16:20].reshape(64, 2, 64).transpose(1, 0, 2)
-    b_rows = bottom[20:23].reshape(6, 8, 128).transpose(1, 0, 2).reshape(8, 768)
-    a_out = bottom[23:25].reshape(4, 8, 128).transpose(1, 0, 2).reshape(8, 512)
-    gains = bottom[25]
-    return a_rows, b_out, f_query, f_key, b_rows, a_out, gains[:4].reshape(512), gains[4:8].reshape(512)
-
-
 EPS = 1e-05
 NEG = -1e30
 HIGH = lax.Precision.HIGHEST
@@ -196,6 +178,10 @@
     return top, (value - top.astype(F32)).astype(BF16)
 
 
+def down_rows(a_q, a_k, a_v):
+    return jnp.concatenate([a[...].astype(F32) for a in (a_q, a_k, a_v)], axis=0).astype(BF16)
+
+
 def soft_pair(rows, table):
     both = mm(rows, jnp.concatenate([table, -table], axis=1))
     left = lax.broadcasted_iota(jnp.int32, both.shape, 1) < DIM
@@ -287,10 +273,9 @@
         for i in range(3):
             self.plane_copy(i).start()
 
-    def close(self):
+    def close(self, total):
         for i in range(3):
             self.plane_copy(i).wait()
-        total = self.pair[...] * self.counts(self.c, 1 - self.c)
         for i in range(3):
             total = total + self.line[i] * self.counts(self.x, turned(self.x, 3 - i))
         for i in range(3):
@@ -299,10 +284,10 @@
 
 
 def front_kernel(
-    x_ref, gain_one, gain_two, a_in, b_q, b_k, b_v, f_q, f_k, a_out, b_out, lengths, w_q, w_k, w_v, w_o,
-    normed_out, low_out, q_out, kv_out, state_out, att_out, stat_out, mixed_out, lowmix_out, hidden_out, ns_out, r2_out, r1_out,
-    wq, wk, wv, wo, w_sem, qh, phq, phk, num, near, far, tail_sem,
-    part, came, y_sem, low_part, low_came, square, square_came,
+    x_ref, gain_one, gain_two, a_q, a_k, a_v, b_q, b_k, b_v, f_q, f_k, a_out, b_out, lengths, w_q, w_k, w_v, w_o,
+    normed_out, low_out, q_out, kv_out, state_out, att_out, stat_out, mixed_out, lowmix_out, hidden_out, g_out, r2_out, r1_out,
+    wq, wk, wv, wo, w_sem, qh, phq, phk, num, near, far, brief, tail_sem,
+    part, came, y_sem, low_part, square, square_came,
     *scan_refs,
 ):
     z, x, c, y = spot()
@@ -324,7 +309,7 @@
         r1_out[rows, :] = scale
         normed_out[rows, :] = (value * scale * gain_one[...]).astype(BF16)
     write_masks(near, far, lengths)
-    low_out[...] = mm(normed_out[...], a_in[...]).astype(BF16)
+    low_out[...] = mm_nt(normed_out[...], down_rows(a_q, a_k, a_v)).astype(BF16)
     low = low_out[...]
     loads[1].wait()
     loads[2].wait()
@@ -343,20 +328,32 @@
         q_out[:, cut] = (mm(normed_out[...], wq[:, cut]) + mm(low[:, :8], b_q[:, cut])).astype(BF16)
     for h in range(HEADS):
         qh[h] = q_out[:, h * DIM : (h + 1) * DIM]
-    tail.wait()
-    inside = middle(ROWS, -WINDOW, lengths)
+    inside = middle(ROWS, 0, lengths)
     for j in range(KEY_HEADS):
-        phk[j] = soft_pair(kv_out[j][:, :DIM], f_k[j]).astype(BF16)
-        counted = (phk[j, :ROWS].astype(F32) * inside).astype(BF16)
-        scan.own[0, j] = mm_tn(value_columns(kv_out[j, :ROWS]), counted)[:STATE]
+        phk[j, WINDOW:] = soft_pair(kv_out[j, WINDOW:][:, :DIM], f_k[j]).astype(BF16)
+        counted = (phk[j, WINDOW:].astype(F32) * inside).astype(BF16)
+        rows = value_columns(kv_out[j, WINDOW:])
+        settled = mm_tn(rows[: ROWS - WINDOW], counted[: ROWS - WINDOW])[:STATE]
+        brief[0, j] = settled
+        scan.own[0, j] = settled + mm_tn(rows[ROWS - WINDOW :], counted[ROWS - WINDOW :])[:STATE]
+    brief_turn = send(brief.at[0], brief.at[1], tail_sem.at[2], tail_sem.at[3], scan.sibling)
+    brief_turn.start()
     scan.open()
 
     def features(h, carry):
         phq[h] = soft_pair(qh[h], f_q[h]).astype(BF16)
         return carry
 
-    lax.fori_loop(0, HEADS, features, 0)
+    lax.fori_loop(0, 4, features, 0)
     scan.along_x()
+    lax.fori_loop(4, HEADS, features, 0)
+    tail.wait()
+    inside = middle(WINDOW, -WINDOW, lengths)
+    for j in range(KEY_HEADS):
+        phk[j, :WINDOW] = soft_pair(kv_out[j, :WINDOW][:, :DIM], f_k[j]).astype(BF16)
+        counted = (phk[j, :WINDOW].astype(F32) * inside).astype(BF16)
+        brief[2, j] = mm_tn(value_columns(kv_out[j, :WINDOW]), counted)[:STATE]
+    brief_turn.wait()
 
     def inner(h, carry):
         j = lax.div(h, 4)
@@ -377,7 +374,8 @@
     lax.fori_loop(0, 4, inner, 0)
     scan.along_z()
     lax.fori_loop(4, HEADS, inner, 0)
-    state_out[...] = scan.close()
+    second = c.astype(F32)
+    state_out[...] = scan.close(brief[1] * second - brief[2] * (1.0 - second))
     mine = middle(ROWS, 0, lengths)
     for h in range(HEADS):
         top, rest = halves(state_out[h // 4])
@@ -391,8 +389,8 @@
         att_out[:, cut] = attended
         mixed_out[:, cut] = attended.astype(BF16)
     mixed = mixed_out[...]
-    low_part[0] = mm_nt(a_out[...], mixed)
-    low_turns = [send(low_part.at[0], low_came.at[i], y_sem.at[0, i], y_sem.at[1, i], y_mates[i]) for i in range(3)]
+    low_part[y] = mm_nt(a_out[...], mixed)
+    low_turns = [send(low_part.at[y], low_part.at[y], y_sem.at[0, i], y_sem.at[1, i], y_mates[i]) for i in range(3)]
     for turn in low_turns:
         turn.start()
     loads[3].wait()
@@ -405,36 +403,36 @@
         part[i] = mm(mixed, columns(wo, turned(y, 1 + i))).astype(BF16)
         turns[i].start()
     value = mm(mixed, columns(wo, y)) + columns(x_ref, y).astype(F32)
-    for turn in low_turns:
-        turn.wait()
-    low_sum = low_part[0] + low_came[0] + low_came[1] + low_came[2]
+    for i in range(3):
+        here = low_part.at[turned(y, 3 - i)]
+        send(here, here, y_sem.at[0, i], y_sem.at[1, i], y_mates[i]).wait()
+    low_sum = low_part[0] + low_part[1] + low_part[2] + low_part[3]
     lowmix_out[...] = low_sum.T.astype(BF16)
     value = value + mm(lowmix_out[...], columns(b_out, y))
     for turn in turns:
         turn.wait()
     value = value + came[0].astype(F32) + came[1].astype(F32) + came[2].astype(F32)
     hidden_out[...] = value
+    g_out[y] = (value * columns(gain_two, y)).astype(BF16)
+    turns = [send(g_out.at[y], g_out.at[y], y_sem.at[0, 9 + i], y_sem.at[1, 9 + i], y_mates[i]) for i in range(3)]
     square[...] = mm_nt(jnp.ones((8, COLS), F32), value * value, HIGH)
-    turns = [send(square, square_came.at[i], y_sem.at[0, 6 + i], y_sem.at[1, 6 + i], y_mates[i]) for i in range(3)]
-    for turn in turns:
+    square_turns = [
+        send(square, square_came.at[i], y_sem.at[0, 6 + i], y_sem.at[1, 6 + i], y_mates[i]) for i in range(3)
+    ]
+    for turn in square_turns + turns:
         turn.start()
-    for turn in turns:
+    for turn in square_turns:
         turn.wait()
     mean = (square[...] + square_came[0] + square_came[1] + square_came[2]) * (1.0 / 2048)
-    scale = lax.rsqrt(mean + EPS).T[:, 0:1]
-    r2_out[...] = scale
-    ns_out[y] = (hidden_out[...] * scale * columns(gain_two, y)).astype(BF16)
-    turns = [send(ns_out.at[y], ns_out.at[y], y_sem.at[0, 9 + i], y_sem.at[1, 9 + i], y_mates[i]) for i in range(3)]
-    for turn in turns:
-        turn.start()
+    r2_out[...] = lax.rsqrt(mean + EPS).T[:, 0:1]
     for i in range(3):
-        here = ns_out.at[turned(y, 3 - i)]
+        here = g_out.at[turned(y, 3 - i)]
         send(here, here, y_sem.at[0, 9 + i], y_sem.at[1, 9 + i], y_mates[i]).wait_recv()
     for turn in turns:
         turn.wait_send()
 
 
-def front(x, gain_one, gain_two, a_in, b_q, b_k, b_v, f_q, f_k, a_out, b_out, lengths, w_q, w_k, w_v, w_o):
+def front(*args):
     anywhere = pl.BlockSpec(memory_space=pl.ANY)
     vmem = pl.BlockSpec(memory_space=pltpu.VMEM)
     shapes = (
@@ -455,7 +453,7 @@
     return pl.pallas_call(
         front_kernel,
         out_shape=tuple(jax.ShapeDtypeStruct(*shape) for shape in shapes),
-        in_specs=[vmem] * 11 + [pl.BlockSpec(memory_space=pltpu.SMEM)] + [anywhere] * 4,
+        in_specs=[vmem] * 13 + [pl.BlockSpec(memory_space=pltpu.SMEM)] + [anywhere] * 4,
         out_specs=(vmem,) * len(shapes),
         scratch_shapes=[
             pltpu.VMEM((2048, 512), BF16),
@@ -469,12 +467,12 @@
             pltpu.VMEM((HEADS, ROWS, DIM), F32),
             pltpu.VMEM((ROWS, SPAN), F32),
             pltpu.VMEM((ROWS, SPAN), F32),
-            pltpu.SemaphoreType.DMA((2,)),
+            pltpu.VMEM((3, KEY_HEADS, STATE, 128), F32),
+            pltpu.SemaphoreType.DMA((4,)),
             pltpu.VMEM((3, ROWS, COLS), BF16),
             pltpu.VMEM((3, ROWS, COLS), BF16),
             pltpu.SemaphoreType.DMA((2, 12)),
-            pltpu.VMEM((1, 8, ROWS), F32),
-            pltpu.VMEM((3, 8, ROWS), F32),
+            pltpu.VMEM((4, 8, ROWS), F32),
             pltpu.VMEM((8, ROWS), F32),
             pltpu.VMEM((3, 8, ROWS), F32),
             *Scan.scratch((KEY_HEADS, STATE, 128)),
@@ -483,21 +481,25 @@
             collective_id=1, has_side_effects=True, vmem_limit_bytes=60 * 2**20
         ),
         name="front",
-    )(x, gain_one, gain_two, a_in, b_q, b_k, b_v, f_q, f_k, a_out, b_out, lengths, w_q, w_k, w_v, w_o)
-
-
-def ffn_kernel(ns, cot, normed, wg, wu, wd, y_out, gs_out, ffn_out, xt_out, gs_sum, ffn_sum):
+    )(*args)
+
+
+def ffn_kernel(g_in, r2, cot, normed, wg, wu, wd, y_out, gs_out, ffn_out, xt_out, dot_out, gs_sum, ffn_sum):
     j = pl.program_id(0)
     gate = jnp.zeros((ROWS, COLS), F32)
     up = jnp.zeros((ROWS, COLS), F32)
     for k in range(4):
         cut = slice(k * COLS, (k + 1) * COLS)
-        gate = gate + mm(ns[k], wg[cut])
-        up = up + mm(ns[k], wu[cut])
+        gate = gate + mm(g_in[k], wg[cut])
+        up = up + mm(g_in[k], wu[cut])
+    scale = r2[...]
+    gate = gate * scale
+    up = up * scale
     grad = mm_nt(cot[...], wd[...])
     sigmoid = jax.nn.sigmoid(gate)
     active = gate * sigmoid
     hidden = (active * up).astype(BF16)
+    grad = grad * scale
     grad_gate = (grad * up * sigmoid * (1.0 + gate * (1.0 - sigmoid))).astype(BF16)
     grad_up = (grad * active).astype(BF16)
     y_out[0, 0] = grad_gate
@@ -520,8 +522,15 @@
 
         @pl.when(j == 3)
         def _():
-            gs_out[k] = (gs_sum[k] + back).astype(BF16)
+            total = (gs_sum[k] + back) / scale
+            gs_out[k] = total.astype(BF16)
+            gs_sum[k] = total * g_in[k].astype(F32)
             ffn_out[k] = (ffn_sum[k] + forth).astype(BF16)
+
+    @pl.when(j == 3)
+    def _():
+        product = gs_sum[0] + gs_sum[1] + gs_sum[2] + gs_sum[3]
+        dot_out[...] = mm_nt(jnp.ones((8, COLS), F32), product, HIGH)
 
     def turn(m, block_of):
         for i in range(16):
@@ -531,7 +540,7 @@
 
     @pl.when(j == 0)
     def _():
-        turn(0, lambda i: ns[i // 4, :, (i % 4) * 128 : (i % 4 + 1) * 128])
+        turn(0, lambda i: g_in[i // 4, :, (i % 4) * 128 : (i % 4 + 1) * 128])
 
     @pl.when(j == 1)
     def _():
@@ -542,7 +551,7 @@
         turn(2, lambda i: normed[:, i * 128 : (i + 1) * 128])
 
 
-def ffn(ns, cot, normed, w_gate, w_up, w_down):
+def ffn(g_in, r2, cot, normed, w_gate, w_up, w_down):
     def whole(*shape):
         return pl.BlockSpec(shape, lambda j: (0,) * len(shape))
 
@@ -554,9 +563,11 @@
             jax.ShapeDtypeStruct((4, ROWS, COLS), BF16),
             jax.ShapeDtypeStruct((4, ROWS, COLS), BF16),
             jax.ShapeDtypeStruct((3, 2, 4, 4, 64, ROWS), BF16),
+            jax.ShapeDtypeStruct((8, ROWS), F32),
         ),
         in_specs=[
             whole(4, ROWS, COLS),
+            whole(ROWS, 1),
             whole(ROWS, 2048),
             whole(ROWS, 2048),
             pl.BlockSpec((2048, COLS), lambda j: (0, j)),
@@ -568,11 +579,12 @@
             whole(4, ROWS, COLS),
             whole(4, ROWS, COLS),
             whole(3, 2, 4, 4, 64, ROWS),
+            whole(8, ROWS),
         ),
         scratch_shapes=[pltpu.VMEM((4, ROWS, COLS), F32), pltpu.VMEM((4, ROWS, COLS), F32)],
         compiler_params=pltpu.CompilerParams(vmem_limit_bytes=60 * 2**20),
         name="ffn",
-    )(ns, cot, normed, w_gate, w_up, w_down)
+    )(g_in, r2, cot, normed, w_gate, w_up, w_down)
 
 
 def soft_back(soft, grad):
@@ -585,19 +597,19 @@
 
 
 def back_kernel(
-    hidden_in, r1, r2, gain_one, gain_two, mixed, low_mix, att, stat, state, q_in, kv, low,
-    f_q, f_k, a_in, a_out, b_out, b_q, b_k, b_v, lengths,
+    dot_two, hidden_in, r1, r2, gain_one, gain_two, mixed, low_mix, att, stat, state, q_in, kv, low,
+    f_q, f_k, a_q, a_k, a_v, a_out, b_out, b_q, b_k, b_v, lengths,
     gs_hbm, ffn_hbm, normed_hbm, x_hbm, cot_hbm, xt_hbm, y_hbm, w_q, w_k, w_v, w_o,
     out_block, out_inputs, out_ffn, out_att, out_pack,
-    wide_w, wk, wv, x_own, cot_own, gs_own, ffn_own, w_sem,
+    wide_w, wk, wv, x_all, cot_own, gs_own, ffn_own, w_sem,
     gs_came, ffn_came, gf_part, dot_part, dot_came, gb, gres, gsum, y_sem,
     xf, yf, sem_ffn, xa, ya, xgb, sem_att, pk, sem_pack,
-    near, far, qh, gh, pq, pkey, dext, dk, dv, gfq, gfk, ret, ret_came, ret_sem, glow, gkv, wide, gao, gbo,
-    ysum, sem_zx,
+    near, far, qh, gh, pq, pkey, dext, dk, dv, gfq, gfk, ret, ret_came, next_state, ret_sem, glow, gkv, wide, gao, gbo, down_ref,
+    first, gain_row, gain_rows_ref, px, px_came, pz, crown, sem_zx,
     *rest,
 ):
     scan = Scan(rest[0:5], True)
-    refs_big, refs_mid, refs_low = rest[5:12], rest[12:19], rest[19:26]
+    refs_big, refs_mid = rest[5:12], rest[12:19]
     z, x, c, y = spot()
     s = lax.axis_index("seq")
     following, leading = (lax.rem(s + 1, 32), y), (lax.rem(s + 31, 32), y)
@@ -614,7 +626,7 @@
         ]
 
     own_columns = pl.ds(pl.multiple_of(y * COLS, COLS), COLS)
-    gs_turns = to_mates(0, lambda i: gs_hbm.at[turned(y, 1 + i)], gs_came)
+    gs_turns = to_mates(3, lambda i: dot_two, dot_came) + to_mates(0, lambda i: gs_hbm.at[turned(y, 1 + i)], gs_came)
     for turn in gs_turns:
         turn.start()
     early = [
@@ -623,7 +635,7 @@
             (
                 (gs_hbm.at[y], gs_own),
                 (cot_hbm.at[:, own_columns], cot_own),
-                (x_hbm.at[:, own_columns], x_own),
+                (x_hbm, x_all),
                 (ffn_hbm.at[y], ffn_own),
                 (w_k, wk),
                 (w_v, wv),
@@ -688,15 +700,8 @@
     def finish_att(t, k, value):
         out_att[t] = value
 
-    def term_pack(t, k, dest, first, last):
-        return (pk[c, first:last, dest] + pk[2, first:last, dest]).reshape((last - first) * PACK, 128)
-
-    def finish_pack(t, k, value):
-        out_pack[c, z, x] = value
-
     big = Ring(refs_big, 64, product(xf, yf, lambda t: lax.div(t, 8)), finish_ffn)
     mid = Ring(refs_mid, 64, product(xa, ya, lambda t: t // 3), finish_att)
-    low_ring = Ring(refs_low, PACK, term_pack, finish_pack)
 
     for m in range(2):
         for copy in left_ffn(m):
@@ -715,31 +720,17 @@
         turn.wait()
     total = gs_own[...].astype(F32) + gs_came[0].astype(F32) + gs_came[1].astype(F32) + gs_came[2].astype(F32)
     gsum[...] = total
-    ones = jnp.ones((8, COLS), F32)
-
-    def mean_over(base, value):
-        dot_part[...] = mm_nt(ones, value, HIGH)
-        turns = to_mates(base, lambda i: dot_part, dot_came)
-        for turn in turns:
-            turn.start()
-        return turns
-
-    dot_turns = mean_over(3, total * columns(gain_two, y) * hidden_in[...])
-    write_masks(near, far, lengths)
-    for h in range(HEADS):
-        qh[h] = q_in[:, h * DIM : (h + 1) * DIM]
-    gain_rows_two = jnp.sum(total * hidden_in[...] * r2[...], axis=0, keepdims=True)
-    for turn in dot_turns:
-        turn.wait()
-
-    def mean_column():
-        return ((dot_part[...] + dot_came[0] + dot_came[1] + dot_came[2]) * (1.0 / 2048)).T[:, 0:1]
+    gain_rows = jnp.sum(total * hidden_in[...] * r2[...], axis=0, keepdims=True)
+    gain_rows_ref[...] = jnp.concatenate([gain_rows[:, i * 128 : (i + 1) * 128] for i in range(4)])
+
+    def mean_column(own):
+        return ((own + dot_came[0] + dot_came[1] + dot_came[2]) * (1.0 / 2048)).T[:, 0:1]
 
     scale = r2[...]
     residual = (
         cot_own[...].astype(F32)
         + scale * (gsum[...] * columns(gain_two, y))
-        - hidden_in[...] * (scale * scale * scale * mean_column())
+        - hidden_in[...] * (scale * scale * scale * mean_column(dot_two[...]))
     )
     gres[...] = residual
     gb[y] = residual.astype(BF16)
@@ -752,6 +743,10 @@
     for turn in ffn_turns:
         turn.start()
 
+    write_masks(near, far, lengths)
+    for h in range(HEADS):
+        qh[h] = q_in[:, h * DIM : (h + 1) * DIM]
+
     def features(h, carry):
         pq[h] = soft_pair(qh[h], f_q[h])
         return carry
@@ -759,10 +754,11 @@
     lax.fori_loop(0, HEADS, features, 0)
     for j in range(KEY_HEADS):
         pkey[j] = soft_pair(kv[j][:, :DIM], f_k[j])
+        pkey[KEY_HEADS + j] = jnp.zeros((SPAN, 128), F32)
     dk[...] = jnp.zeros(dk.shape, F32)
     dv[...] = jnp.zeros(dv.shape, F32)
     pk[...] = jnp.zeros(pk.shape, F32)
-    over_pairs(0, 1, big.merge)
+    over_pairs(0, 3, big.merge)
 
     for i in range(3):
         here = gb.at[turned(y, 3 - i)]
@@ -785,7 +781,8 @@
         gh[h] = rounded[:, h * DIM : (h + 1) * DIM]
     top, bottom = halves(grad_low)
     gao[...] = mm_tn(top, mixed[...]) + mm_tn(bottom, mixed[...])
-    gbo[...] = mm_tn(low_mix[...], gb[y])
+    for k in range(4):
+        gbo[:, k * COLS : (k + 1) * COLS] = mm_tn(low_mix[...], gb[k])
 
     lane = lax.broadcasted_iota(jnp.int32, (ROWS, DIM), 1)
     for h in range(HEADS):
@@ -850,105 +847,122 @@
         def _():
             scan.along_z()
 
-        @pl.when(h < 5)
+        @pl.when((h >= 1) & (h < 4))
         def _():
-            big.merge(2 * h + 2, 0)
-            big.merge(2 * h + 3, 1)
-
-        @pl.when(h >= 5)
+            big.merge(2 * h + 4, 0)
+            big.merge(2 * h + 5, 1)
+
+        @pl.when(h >= 6)
         def _():
-            big.cross(2 * h - 10, 0)
-            big.cross(2 * h - 9, 1)
+            big.cross(2 * h - 12, 0)
+            big.cross(2 * h - 11, 1)
 
         return carry
 
+    lax.fori_loop(0, HEADS, backward, 0)
+
     for j in range(KEY_HEADS):
-        pkey[KEY_HEADS + j] = jnp.zeros((SPAN, 128), F32)
-    lax.fori_loop(0, HEADS, backward, 0)
-
-    inside = middle(ROWS, -WINDOW, lengths)
-    suffix = scan.close()
-    for j in range(KEY_HEADS):
-        soft = pkey[j]
-        high, rest = halves(suffix[j])
-        rows = value_columns(kv[j, :ROWS])[:, :STATE]
-        grad_phi = pkey[KEY_HEADS + j]
-        carried = (mm(rows, high) + mm(rows, rest)) * inside
-        grad_phi = jnp.concatenate([grad_phi[:ROWS] + carried, grad_phi[ROWS:]], axis=0)
-        phi = soft[:ROWS].astype(BF16)
-        dv[j, :ROWS] = dv[j, :ROWS] + ((mm_nt(phi, high) + mm_nt(phi, rest)) * inside)[:, :DIM]
-        high, rest = halves(soft_back(soft, grad_phi))
-        dk[j] = dk[j] + mm_nt(high, f_k[j]) + mm_nt(rest, f_k[j])
-        keys = kv[j][:, :DIM]
-        gfk[j] = mm_tn(keys, high) + mm_tn(keys, rest)
-        ret[j] = jnp.concatenate([dk[j, :WINDOW], dv[j, :WINDOW]], axis=1)
-    back = send(ret, ret_came, ret_sem.at[0], ret_sem.at[1], leading)
-    back.start()
+        ret[j] = jnp.concatenate([dk[j, :WINDOW], dv[j, :WINDOW], pkey[KEY_HEADS + j, :WINDOW]], axis=1)
+    home = [
+        send(ret, ret_came, ret_sem.at[0], ret_sem.at[1], leading),
+        send(scan.own.at[0], next_state, ret_sem.at[2], ret_sem.at[3], leading),
+    ]
+    for copy in home:
+        copy.start()
     gq = jnp.concatenate([qh[h] for h in range(HEADS)], axis=1)
     for i in range(2):
         ya[i, 0:ROWS] = gq[:, i * ATT_WIDTH : (i + 1) * ATT_WIDTH]
         right_att(i).start()
-    for turn in ffn_turns:
-        turn.wait()
-    out_block[...] = (
-        hidden_in[...]
-        + ffn_own[...].astype(F32)
-        + ffn_came[0].astype(F32)
-        + ffn_came[1].astype(F32)
-        + ffn_came[2].astype(F32)
-    ).astype(BF16)
-    back.wait()
+    down_ref[...] = down_rows(a_q, a_k, a_v)
+    for load in load_q + load_n:
+        load.wait()
+    glow[:, :8] = mm_nt(gq, b_q[...])
+    for copy in left_att:
+        copy.wait()
+    for t in range(2):
+        right_att(t).wait()
+        mid.start(t, t % 2)
+    for k in range(4):
+        first[k] = mm_nt(gq, wide_w[k])
+
+    inside = middle(ROWS, 0, lengths)
+    suffix = scan.close(scan.pair[...] * (1.0 - c.astype(F32)))
+    for copy in home:
+        copy.wait()
+    joined = (s < 31).astype(F32)
+    late_row = lax.broadcasted_iota(jnp.int32, (ROWS, 128), 0) >= ROWS - WINDOW
     for j in range(KEY_HEADS):
-        dk[j, ROWS:] = dk[j, ROWS:] + ret_came[j][:, :DIM]
-        dv[j, ROWS:] = dv[j, ROWS:] + ret_came[j][:, DIM:]
+        soft = pkey[j, WINDOW:]
+        phi = soft.astype(BF16)
+        keys = kv[j, WINDOW:][:, :DIM]
+        rows = value_columns(kv[j, WINDOW:])[:, :STATE]
+        high, rest = halves(suffix[j])
+        high_next, rest_next = halves(suffix[j] - joined * next_state[j])
+        grad_phi = jnp.where(late_row, mm(rows, high_next) + mm(rows, rest_next), mm(rows, high) + mm(rows, rest))
+        grad_phi = grad_phi * inside + pkey[KEY_HEADS + j, WINDOW:]
+        grad_v = jnp.where(
+            late_row[:, :STATE], mm_nt(phi, high_next) + mm_nt(phi, rest_next), mm_nt(phi, high) + mm_nt(phi, rest)
+        )
+        grad_v = (grad_v * inside)[:, :DIM] + dv[j, WINDOW:]
+        last = ROWS - WINDOW
+        grad_phi = jnp.concatenate([grad_phi[:last], grad_phi[last:] + ret_came[j][:, 2 * DIM :]], axis=0)
+        high, rest = halves(soft_back(soft, grad_phi))
+        grad_k = dk[j, WINDOW:] + mm_nt(high, f_k[j]) + mm_nt(rest, f_k[j])
+        gfk[j] = mm_tn(keys, high) + mm_tn(keys, rest)
+        dk[j, WINDOW:] = jnp.concatenate([grad_k[:last], grad_k[last:] + ret_came[j][:, :DIM]], axis=0)
+        dv[j, WINDOW:] = jnp.concatenate([grad_v[:last], grad_v[last:] + ret_came[j][:, DIM : 2 * DIM]], axis=0)
     gk = jnp.concatenate([dk[j, WINDOW:] for j in range(KEY_HEADS)], axis=1).astype(BF16)
     gv = jnp.concatenate([dv[j, WINDOW:] for j in range(KEY_HEADS)], axis=1).astype(BF16)
     gkv[...] = jnp.concatenate([gk, gv], axis=1)
     ya[2, 0:ROWS] = gkv[...]
     right_att(2).start()
 
-    for load in load_q + load_n:
-        load.wait()
-    glow[...] = jnp.concatenate([mm_nt(gq, b_q[...]), mm_nt(gk, b_k[...]), mm_nt(gv, b_v[...])], axis=1)
+    glow[:, 8:16] = mm_nt(gk, b_k[...])
+    glow[:, 16:24] = mm_nt(gv, b_v[...])
     glow_high, glow_rest = halves(glow[...])
-
-    def partial_first(d):
+    gf_turns = to_mates(12, lambda i: gf_part.at[i], gs_came)
+    dot = jnp.zeros((ROWS, 1), F32)
+    for i in (1, 0, 2, 3):
+        d = turned(y, 1 + i)
         rows = pl.ds(pl.multiple_of(d * COLS, COLS), COLS)
-        down = a_in[rows, :]
-        return (
-            mm_nt(gq, wide_w[d])
+        down = columns(down_ref, d)
+        part = (
+            first[d]
             + mm_nt(gkv[:, :128], wk[rows, :])
             + mm_nt(gkv[:, 128:], wv[rows, :])
-            + mm_nt(glow_high, down)
-            + mm_nt(glow_rest, down)
+            + mm(glow_high, down)
+            + mm(glow_rest, down)
         )
-
-    gf_turns = to_mates(12, lambda i: gf_part.at[i], gs_came)
-    for i in (1, 0, 2):
-        gf_part[i] = partial_first(turned(y, 1 + i)).astype(BF16)
-        gf_turns[i].start()
-    gsum[...] = partial_first(y)
-    for copy in left_att:
-        copy.wait()
-    for t in range(3):
-        right_att(t).wait()
-        mid.start(t, t % 2)
+        if i < 3:
+            gf_part[i] = part.astype(BF16)
+            gf_turns[i].start()
+        else:
+            gsum[...] = part
+        part = part * columns(x_all, d).astype(F32)
+        dot = dot + jnp.sum(part * columns(gain_one, d), axis=1, keepdims=True)
+        gain_row[:, rows] = jnp.sum(part * r1[...], axis=0, keepdims=True)
+    dot_part[...] = jnp.broadcast_to(dot, (ROWS, 128)).T[:8]
+    dot_turns = to_mates(15, lambda i: dot_part, dot_came)
+    for turn in dot_turns:
+        turn.start()
 
     for k in range(4):
         wide[:, k * COLS : (k + 1) * COLS] = mm_tn(glow_high, gb[k]) + mm_tn(glow_rest, gb[k])
+
+    def place(d):
+        return d // 16, d // 4 % 4, d % 4
+
     for i in range(16):
+        cut = slice(i * 128, (i + 1) * 128)
         for half in range(2):
-            d = 2 * i + half
-            pk[d // 16, d // 4 % 4, d % 4, 0:12] = wide[12 * half : 12 * half + 12, i * 128 : (i + 1) * 128]
-    for i in range(4):
-        for half in range(2):
-            d = 2 * i + half
-            pk[lax.div(y, 2), lax.rem(y, 2) * 2 + d // 4, d % 4, 12:16] = gbo[
-                4 * half : 4 * half + 4, i * 128 : (i + 1) * 128
-            ]
+            d = place(2 * i + half)
+            pk[*d, 0:12] = wide[12 * half : 12 * half + 12, cut]
+            pk[*d, 13:16] = 0.25 * gbo[3 * half : 3 * half + 3, cut]
+        pk[*place(2 * i), 12:13] = gain_row[:, cut]
+        pk[*place(26 + i // 8), 16 + 2 * (i % 8) : 18 + 2 * (i % 8)] = gbo[6:8, cut]
 
     def low_half(d, value):
-        pk[d // 16, d // 4 % 4, d % 4, 16 : 16 + value.shape[0]] = value
+        pk[*place(d), 16 : 16 + value.shape[0]] = value
 
     for i in range(4):
         pair = jnp.concatenate([gfq[2 * i], gfq[2 * i + 1]], axis=1)
@@ -963,51 +977,13 @@
     for i in range(3):
         low_half(20 + i, jnp.concatenate([grad_b[:, 256 * i : 256 * i + 128], grad_b[:, 256 * i + 128 : 256 * i + 256]]))
     for i in range(2):
-        low_half(
-            23 + i, jnp.concatenate([gao[:, 256 * i : 256 * i + 128], gao[:, 256 * i + 128 : 256 * i + 256]])
-        )
-    for turn in gf_turns:
-        turn.wait()
-    total = gsum[...] + gs_came[0].astype(F32) + gs_came[1].astype(F32) + gs_came[2].astype(F32)
-    gsum[...] = total
-    inputs = x_own[...].astype(F32)
-    gain_rows_one = jnp.sum(total * inputs * r1[...], axis=0, keepdims=True)
-    low_half(
-        25,
-        jnp.concatenate([rows[:, i * 128 : (i + 1) * 128] for rows in (gain_rows_one, gain_rows_two) for i in range(4)]),
-    )
+        low_half(23 + i, jnp.concatenate([gao[:, 256 * i : 256 * i + 128], gao[:, 256 * i + 128 : 256 * i + 256]]))
+    low_half(25, gain_rows_ref[...])
     pack_far = send(pk.at[1 - c], pk.at[2], sem_pack.at[0], sem_pack.at[1], sibling)
     pack_far.start()
-    dot_turns = mean_over(15, total * columns(gain_one, y) * inputs)
+    right_att(2).wait()
+    mid.start(2, 0)
     pack_far.wait()
-    low_ring.start(0, 0)
-    for turn in dot_turns:
-        turn.wait()
-    scale = r1[...]
-    out_inputs[...] = (
-        gres[...]
-        + scale * (gsum[...] * columns(gain_one, y))
-        - x_own[...].astype(F32) * (scale * scale * scale * mean_column())
-    )
-    for t in (3, 4, 0, 1, 2):
-        mid.merge(t, t % 2)
-    low_ring.merge(0, 0)
-    over_pairs(3, 6, big.cross)
-    for t in (3, 4, 0, 1, 2):
-        mid.cross(t, t % 2)
-    low_ring.cross(0, 0)
-    over_pairs(0, 6, big.merge_cross)
-    for t in (3, 4, 0, 1, 2):
-        mid.merge_cross(t, t % 2)
-    low_ring.merge_cross(0, 0)
-    low_ring.end(0, 0)
-    crown = pl.ds(0, 16)
-    turns = to_mates(18, lambda i: out_pack.at[c, z, x, crown], ysum)
-    for turn in turns:
-        turn.start()
-    for turn in turns:
-        turn.wait()
-    out_pack[c, z, x, crown] = out_pack[c, z, x, crown] + ysum[0] + ysum[1] + ysum[2]
 
     def spread(base, piece, mates, back_piece):
         turns = [
@@ -1020,22 +996,68 @@
             for i, mate in enumerate(mates)
         ]
 
-    turns = spread(0, out_pack.at[c, z, x], scan.z_mates, lambda i: out_pack.at[c, turned(z, 3 - i), x])
+    def mine(dest):
+        return (pk[c, :, dest] + pk[2, :, dest]).astype(BF16)
+
+    x_turns = [send(px.at[i], px_came.at[i], sem_zx.at[0, i], sem_zx.at[1, i], scan.x_mates[i]) for i in range(3)]
+    for i in range(3):
+        px[i] = mine(turned(x, 1 + i))
+        x_turns[i].start()
+    own_pack = pk[c, :, x] + pk[2, :, x]
+    for t in (3, 4, 0, 1):
+        mid.merge(t, t % 2)
+    for turn in x_turns:
+        turn.wait()
+    own_pack = own_pack + px_came[0].astype(F32) + px_came[1].astype(F32) + px_came[2].astype(F32)
+    pz[z] = own_pack.astype(BF16)
+    z_turns = spread(3, pz.at[z], scan.z_mates, lambda i: pz.at[turned(z, 3 - i)])
+    mid.merge(2, 0)
+    over_pairs(2, 6, big.cross)
+    for turn in z_turns:
+        turn.wait()
+    own_pack = pz[0].astype(F32) + pz[1].astype(F32) + pz[2].astype(F32) + pz[3].astype(F32)
+    crown[y] = own_pack[:, :16]
+    y_turns = spread(10, crown.at[y], y_mates, lambda i: crown.at[turned(y, 3 - i)])
+    for t in (3, 4, 0, 1, 2):
+        mid.cross(t, t % 2)
+    for turn in y_turns:
+        turn.wait()
+    top = crown[0] + crown[1] + crown[2] + crown[3]
+    out_pack[c, :, x] = jnp.concatenate([top, own_pack[:, 16:]], axis=1).astype(BF16)
+
+    x_turns = spread(6, out_pack.at[c, :, x], scan.x_mates, lambda i: out_pack.at[c, :, turned(x, 3 - i)])
+    over_pairs(0, 6, big.merge_cross)
+    for t in (3, 4, 0, 1, 2):
+        mid.merge_cross(t, t % 2)
+    for turn in gf_turns + dot_turns:
+        turn.wait()
+    total = gsum[...] + gs_came[0].astype(F32) + gs_came[1].astype(F32) + gs_came[2].astype(F32)
+    scale = r1[...]
+    out_inputs[...] = (
+        gres[...]
+        + scale * (total * columns(gain_one, y))
+        - columns(x_all, y).astype(F32) * (scale * scale * scale * mean_column(dot_part[...]))
+    )
+    for turn in x_turns:
+        turn.wait()
+    last = spread(9, out_pack.at[c], [sibling], lambda i: out_pack.at[1 - c])
+    for turn in ffn_turns:
+        turn.wait()
+    out_block[...] = (
+        hidden_in[...]
+        + ffn_own[...].astype(F32)
+        + ffn_came[0].astype(F32)
+        + ffn_came[1].astype(F32)
+        + ffn_came[2].astype(F32)
+    ).astype(BF16)
     over_pairs(0, 6, big.end)
-    for turn in turns:
-        turn.wait()
-    turns = spread(3, out_pack.at[c, :, x], scan.x_mates, lambda i: out_pack.at[c, :, turned(x, 3 - i)])
     for t in (3, 4, 0, 1, 2):
         mid.end(t, t % 2)
-    for turn in turns:
+    for turn in last:
         turn.wait()
-    turns = spread(6, out_pack.at[c], [sibling], lambda i: out_pack.at[1 - c])
     over_pairs(0, 6, big.drain)
     for t in range(ATT_TILES):
         mid.drain(t, t % 2)
-    low_ring.drain(0, 0)
-    for turn in turns:
-        turn.wait()
 
 
 def back(args, weights):
@@ -1046,19 +1068,19 @@
         ((ROWS, COLS), F32),
         ((FFN_TILES, 64, FFN_WIDTH), F32),
         ((ATT_TILES, 64, ATT_WIDTH), F32),
-        ((2, 4, 4, PACK, 128), F32),
+        ((2, 4, 4, PACK, 128), BF16),
     )
     block = (ROWS, COLS)
     return pl.pallas_call(
         back_kernel,
         out_shape=tuple(jax.ShapeDtypeStruct(*shape) for shape in shapes),
-        in_specs=[vmem] * 21 + [pl.BlockSpec(memory_space=pltpu.SMEM)] + [anywhere] * 11,
+        in_specs=[vmem] * 24 + [pl.BlockSpec(memory_space=pltpu.SMEM)] + [anywhere] * 11,
         out_specs=(vmem,) * len(shapes),
         scratch_shapes=[
             pltpu.VMEM((4, 512, 512), BF16),
             pltpu.VMEM((2048, 128), BF16),
             pltpu.VMEM((2048, 128), BF16),
-            pltpu.VMEM(block, BF16),
+            pltpu.VMEM((ROWS, 2048), BF16),
             pltpu.VMEM(block, BF16),
             pltpu.VMEM(block, BF16),
             pltpu.VMEM(block, BF16),
@@ -1071,7 +1093,7 @@
             pltpu.VMEM((4, *block), BF16),
             pltpu.VMEM(block, F32),
             pltpu.VMEM(block, F32),
-            pltpu.SemaphoreType.DMA((2, 21)),
+            pltpu.SemaphoreType.DMA((2, 18)),
             pltpu.VMEM((2, 4, 4, 64, 512), BF16),
             pltpu.VMEM((FFN_TILES, 512, FFN_WIDTH), BF16),
             pltpu.SemaphoreType.DMA((3, 2 + FFN_TILES)),
@@ -1092,26 +1114,103 @@
             pltpu.VMEM((KEY_HEADS, SPAN, DIM), F32),
             pltpu.VMEM((HEADS, DIM, DIM), F32),
             pltpu.VMEM((KEY_HEADS, DIM, DIM), F32),
-            pltpu.VMEM((KEY_HEADS, WINDOW, 128), F32),
-            pltpu.VMEM((KEY_HEADS, WINDOW, 128), F32),
-            pltpu.SemaphoreType.DMA((2,)),
+            pltpu.VMEM((KEY_HEADS, WINDOW, 256), F32),
+            pltpu.VMEM((KEY_HEADS, WINDOW, 256), F32),
+            pltpu.VMEM((KEY_HEADS, STATE, 128), F32),
+            pltpu.SemaphoreType.DMA((4,)),
             pltpu.VMEM((ROWS, 24), F32),
             pltpu.VMEM((ROWS, 256), BF16),
             pltpu.VMEM((24, 2048), F32),
             pltpu.VMEM((8, COLS), F32),
-            pltpu.VMEM((8, COLS), F32),
-            pltpu.VMEM((3, 16, 128), F32),
-            pltpu.SemaphoreType.DMA((2, 7)),
+            pltpu.VMEM((8, 2048), F32),
+            pltpu.VMEM((24, 2048), BF16),
+            pltpu.VMEM((4, *block), F32),
+            pltpu.VMEM((1, 2048), F32),
+            pltpu.VMEM((4, 128), F32),
+            pltpu.VMEM((3, 4, PACK, 128), BF16),
+            pltpu.VMEM((3, 4, PACK, 128), BF16),
+            pltpu.VMEM((4, 4, PACK, 128), BF16),
+            pltpu.VMEM((4, 4, 16, 128), F32),
+            pltpu.SemaphoreType.DMA((2, 13)),
             *Scan.scratch((KEY_HEADS, STATE, 128)),
             *Ring.scratch(FFN_TILES, 64, FFN_WIDTH),
             *Ring.scratch(ATT_TILES, 64, ATT_WIDTH),
-            *Ring.scratch(1, PACK, 128),
         ],
         compiler_params=pltpu.CompilerParams(
             collective_id=2, has_side_effects=True, vmem_limit_bytes=63 * 2**20
         ),
         name="back",
     )(*args, *weights)
+
+
+def finish_kernel(
+    block, inputs, ffn_sums, att_sums, packed,
+    block_out, inputs_out, gain_one, w_q, a_q, b_q, w_k, a_k, b_k, w_v, a_v, b_v, f_q, f_k, w_o, a_o, b_o, gain_two,
+    w_gate, w_up, w_down,
+):
+    block_out[...] = block[...]
+    pack = packed[...].astype(F32)
+    inputs_out[...] = inputs[...]
+    for i in range(4):
+        cut = slice(i * FFN_WIDTH, (i + 1) * FFN_WIDTH)
+        w_gate[:, cut] = ffn_sums[i]
+        w_up[:, cut] = ffn_sums[4 + i]
+        w_down[:, cut] = ffn_sums[8 + i]
+    for i in range(2):
+        cut = slice(i * ATT_WIDTH, (i + 1) * ATT_WIDTH)
+        w_q[:, cut] = att_sums[i]
+        w_o[:, cut] = att_sums[3 + i]
+    w_k[...] = att_sums[2, :, :128]
+    w_v[...] = att_sums[2, :, 128:]
+    for i in range(16):
+        cut = slice(i * 128, (i + 1) * 128)
+        rows = jnp.concatenate([pack[2 * i, :12], pack[2 * i + 1, :12]], axis=0)
+        a_q[:, cut] = rows[:8]
+        a_k[:, cut] = rows[8:16]
+        a_v[:, cut] = rows[16:]
+        last = 16 + 2 * (i % 8)
+        b_o[:, cut] = jnp.concatenate(
+            [pack[2 * i, 13:16], pack[2 * i + 1, 13:16], pack[26 + i // 8, last : last + 2]], axis=0
+        )
+
+    def tile(i):
+        return pack[20 + i // 2, 16 + 8 * (i % 2) : 24 + 8 * (i % 2)]
+
+    for i in range(4):
+        cut = slice(i * 128, (i + 1) * 128)
+        for part in range(4):
+            rows = pack[4 * i + part, 16:]
+            f_q[2 * i, 16 * part : 16 * part + 16] = rows[:, :DIM]
+            f_q[2 * i + 1, 16 * part : 16 * part + 16] = rows[:, DIM:]
+        rows = pack[16 + i, 16:]
+        f_k[0, 16 * i : 16 * i + 16] = rows[:, :DIM]
+        f_k[1, 16 * i : 16 * i + 16] = rows[:, DIM:]
+        b_q[:, cut] = tile(i)
+        a_o[:, cut] = tile(6 + i)
+        gain_two[:, cut] = pack[25, 16 + i : 17 + i]
+        gain_one[:, cut] = packed[8 * lax.axis_index("head") + 2 * i].astype(F32)[12:13]
+    b_k[...] = tile(4)
+    b_v[...] = tile(5)
+
+
+def finish(block, inputs, ffn_sums, att_sums, pack):
+    vmem = pl.BlockSpec(memory_space=pltpu.VMEM)
+    shapes = (
+        (ROWS, COLS), (ROWS, COLS), (1, COLS), (64, COLS), (8, 2048), (8, COLS), (64, 128), (8, 2048), (8, 128),
+        (64, 128), (8, 2048), (8, 128), (HEADS, DIM, DIM), (KEY_HEADS, DIM, DIM), (64, COLS), (8, COLS), (8, 2048),
+        (1, COLS), (64, 2048), (64, 2048), (64, 2048),
+    )
+    outs = pl.pallas_call(
+        finish_kernel,
+        out_shape=tuple(jax.ShapeDtypeStruct(shape, F32 if i else BF16) for i, shape in enumerate(shapes)),
+        in_specs=[vmem] * 5,
+        out_specs=(vmem,) * len(shapes),
+        compiler_params=pltpu.CompilerParams(vmem_limit_bytes=32 * 2**20),
+        name="finish",
+    )(block, inputs, ffn_sums, att_sums, pack.reshape(32, 32, 128))
+    return tuple(
+        out[0] if i in (2, 17) else out.T if i in (4, 7, 10, 14, 15, 20) else out for i, out in enumerate(outs)
+    )
 
 
 def body(
@@ -1139,47 +1238,23 @@
     cotangent,
 ):
     gain_one, gain_two = gain_first[None], gain_second[None]
-    a_in = jnp.concatenate([a_query, a_key, a_value], axis=1)
+    a_in = (a_query.T, a_key.T, a_value.T)
     a_out = a_out.T
     projections = (w_query, key_projection_weight, value_projection_weight, w_out)
-    normed, low, queries, kv, state, att, stat, mixed, low_mix, hidden_in, ns, r2, r1 = front(
-        inputs, gain_one, gain_two, a_in, b_query, key_adapter_second, value_adapter_second,
+    normed, low, queries, kv, state, att, stat, mixed, low_mix, hidden_in, g, r2, r1 = front(
+        inputs, gain_one, gain_two, *a_in, b_query, key_adapter_second, value_adapter_second,
         feature_query, key_hedgehog_map, a_out, b_out, lengths, *projections,
     )
-    y_ffn, gs, ffn_sum, xt = ffn(ns, cotangent, normed, w_gate, w_up, w_down)
+    y_ffn, gs, ffn_sum, xt, dot_two = ffn(g, r2, cotangent, normed, w_gate, w_up, w_down)
     block_out, grad_inputs, out_ffn, out_att, out_pack = back(
         (
-            hidden_in, r1, r2, gain_one, gain_two, mixed, low_mix, att, stat, state, queries, kv, low,
-            feature_query, key_hedgehog_map, a_in, a_out, b_out, b_query, key_adapter_second,
+            dot_two, hidden_in, r1, r2, gain_one, gain_two, mixed, low_mix, att, stat, state, queries, kv, low,
+            feature_query, key_hedgehog_map, *a_in, a_out, b_out, b_query, key_adapter_second,
             value_adapter_second, lengths,
         ),
         (gs, ffn_sum, normed, inputs, cotangent, xt, y_ffn.reshape(FFN_TILES, ROWS, FFN_WIDTH), *projections),
     )
-    a_rows, b_out_sum, f_query, f_key, b_rows, a_out_sum, gain_one, gain_two = unpack_small(out_pack)
-    a_rows = a_rows.T
-    return (
-        block_out,
-        grad_inputs,
-        gain_one,
-        untile(out_att[:2]),
-        a_rows[:, :8],
-        b_rows[:, :512],
-        out_att[2, :, :128],
-        a_rows[:, 8:16],
-        b_rows[:, 512:640],
-        out_att[2, :, 128:],
-        a_rows[:, 16:],
-        b_rows[:, 640:],
-        f_query,
-        f_key,
-        untile(out_att[3:]).T,
-        a_out_sum.T,
-        b_out_sum,
-        gain_two,
-        untile(out_ffn[:4]),
-        untile(out_ffn[4:8]),
-        untile(out_ffn[8:]).T,
-    )
+    return finish(block_out, grad_inputs, out_ffn, out_att, out_pack)
 
 
 def solution(mesh):

time: 240 us -> 205 us (0.85)
  Pallas kernels: 218 us -> 199 us
  local copies, waits for them, and re-layouts: 18.7 us -> 5.31 us
    pallas_call x1, Pallas kernels: 129 us -> 112 us  [back(): pl.pallas_call(back_kernel, out_shape=tuple((jax.ShapeDtypeStruct(*shape)...]
    slice x8 -> x0, local copies, waits for them, and re-layouts: 6.6 us -> none  [the longest x1 1.32 us: unpack_small(): a_out = bottom[23:25].reshape(4, 8, 128).transpose(1, 0, 2).reshape(8, 512)]
    reshape x11 -> x0, local copies, waits for them, and re-layouts: 6.43 us -> none  [the longest x5 3.84 us: untile(): return tiles.transpose(1, 0, 2).reshape(tiles.shape[1], -1)]
    pallas_call x1, Pallas kernels: 63 us -> 57.8 us  [front(): pl.pallas_call(front_kernel, out_shape=tuple((jax.ShapeDtypeStruct(*shape...]
    unnamed x11 -> x10, local copies, waits for them, and re-layouts: 3.25 us -> 5.31 us
where the time goes in v3:
time: 205 us
  Pallas kernels  199 us (97%)
  local copies, waits for them, and re-layouts  5.31 us (3%)
    pallas_call x1, Pallas kernels, back(): pl.pallas_call(back_kernel, out_shape=tuple((jax.ShapeDtypeStruct(*shape)...  112 us
    pallas_call x1, Pallas kernels, front(): pl.pallas_call(front_kernel, out_shape=tuple((jax.ShapeDtypeStruct(*shape...  57.8 us
    pallas_call x1, Pallas kernels, ffn(): pl.pallas_call(ffn_kernel, grid=(4,), out_shape=(jax.ShapeDtypeStruct((3,...  27.1 us
    unnamed x10, local copies, waits for them, and re-layouts  5.31 us

profile of v3, /device:TPU:1, one launch (start us, length us, event | category | flops | bytes accessed | tf_op | source)
XLA Modules:
  0.0 204.9 jit_solution(16392821093519349186)
XLA Ops:
  0.7 57.8 %front.1 = (bf16[256,2048]{1,0:T(8,128)(2,1)}, bf16[256,24]{1,0:T(8,128)(2,1)}, bf16[256,512]{1,0:T(8,128)(2,1)}, bf16[2,320,128]{2,1,0:T(8,128)(2,1)}, f32[2,72...) custom-call(bf16[256,2048]{1,0:T(8,128)(2,1)} %x_hbm.1, ...), custom_call_target="tpu_custom_call" | custom-call | tf_op jit(solution)/shard_map/front/pallas_call | solution.py:453
  58.4 27.1 %ffn.1 = (bf16[3,4,256,512]{3,2,1,0:T(8,128)(2,1)}, bf16[4,256,512]{2,1,0:T(8,128)(2,1)}, bf16[4,256,512]{2,1,0:T(8,128)(2,1)}, bf16[3,2,4,4,64,256]{5,4,3,2,1,0:T(8,128)(2,1)}, f32[8,256]{1,0:T(8,128)}) custom-call(bf16[4,256,512]{2,1,0:T(8,128)(2,1)} %get-tuple-element.65.g_in, f32[256,1]{1,0:T(8,128)} %get-tuple-element.66.r2, bf16[256,2048]{1,0:T(8,128)(2,1)} %cot_hbm.1, ...), custom_call_target="tpu_custom_call" | custom-call | tf_op jit(solution)/shard_map/ffn/pallas_call | solution.py:558
  85.6 112.2 %back.1 = (bf16[256,512]{1,0:T(8,128)(2,1)}, f32[256,512]{1,0:T(8,128)}, f32[12,64,512]{2,1,0:T(8,128)}, f32[5,64,256]{2,1,0:T(8,128)}, bf16[2,4,4,32,128]{4,3,2,1,0:T(8,128)(2,1)}) custom-call(f32[8,256]{1,0:T(8,128)} %get-tuple-element.68.dot_two, f32[256,512]{1,0:T(8,128)} %get-tuple-element.69.hidden_in, f32[256,1]{1,0:T(8,128)} %get-tuple-element.70.r1, ...), custom_call_target="tpu_custom_call" | custom-call | tf_op jit(solution)/shard_map/back/pallas_call | solution.py:1074
  197.8 0.0 copy-start
  197.8 1.4 copy-done
  199.2 0.0 copy-start.1
  199.2 1.0 copy-done.1
  200.3 0.0 copy-start.2
  200.3 1.0 copy-done.2
  201.3 0.0 copy-start.3
  201.3 0.9 copy-done.3
  202.2 0.0 copy-start.4
  202.2 0.9 copy-done.4
  203.2 1.8 finish.1
Async XLA Ops:
  197.8 1.4 copy-start
  199.2 1.0 copy-start.1
  200.3 1.0 copy-start.2
  201.3 0.9 copy-start.3
  202.2 0.9 copy-start.4

commit v4 on v3

v4 whole, which is shorter than its diff:
```python
import jax
import jax.numpy as jnp
from jax import lax
from jax.experimental import pallas as pl
from jax.experimental.pallas import tpu as pltpu
from jax.sharding import PartitionSpec as P

MESH = pl.DeviceIdType.MESH
F32 = jnp.float32
BF16 = jnp.bfloat16


def spot():
    s = lax.axis_index("seq")
    y = lax.axis_index("head")
    return lax.div(s, 8), lax.rem(lax.div(s, 2), 4), lax.rem(s, 2), y


def at(z, x, c, y):
    return ((z * 4 + x) * 2 + c, y)


def turned(p, steps):
    return lax.rem(p + steps, 4)


def greet(partners):
    barrier = pltpu.get_barrier_semaphore()
    for partner in partners:
        pl.semaphore_signal(barrier, inc=1, device_id=partner, device_id_type=MESH)
    pl.semaphore_wait(barrier, len(partners))


def send(src, dst, ss, rs, device):
    return pltpu.make_async_remote_copy(
        src_ref=src, dst_ref=dst, send_sem=ss, recv_sem=rs, device_id=device, device_id_type=MESH
    )


def took(ref, sem):
    pltpu.make_async_copy(ref, ref, sem).wait()


class Ring:
    def __init__(self, refs, rows, pieces, term, finish):
        self.sb, self.ra, self.rf, self.ra3, self.rf3, self.ss, self.rs = refs
        self.rows, self.pieces, self.term, self.finish = rows, pieces, term, finish
        z, x, c, y = spot()
        self.axes = (
            (x, at(z, turned(x, 1), c, y), at(z, turned(x, 3), c, y)),
            (z, at(turned(z, 1), x, c, y), at(turned(z, 3), x, c, y)),
        )

    @staticmethod
    def scratch(count, pieces, rows, width):
        return [
            pltpu.VMEM((count, 2, pieces, 4 * rows, width), BF16),
            pltpu.VMEM((count, 2, pieces, 2 * rows, width), BF16),
            pltpu.VMEM((count, 2, pieces, 4 * rows, width), BF16),
            pltpu.VMEM((count, 2, pieces, rows // 2, width), BF16),
            pltpu.VMEM((count, 2, pieces, rows, width), BF16),
            pltpu.SemaphoreType.DMA((count, 4)),
            pltpu.SemaphoreType.DMA((count, 6)),
        ]

    def each(self, step):
        if self.pieces == 1:
            step(0)
        else:

            def one(p, carry):
                step(p)
                return carry

            lax.fori_loop(0, self.pieces, one, 0)

    def block(self, b, part):
        g = self.rows // 2
        if part is None:
            return pl.ds(pl.multiple_of(b * self.rows, self.rows), self.rows)
        return pl.ds(pl.multiple_of(b * self.rows + part * g, g), g)

    def copy(self, t, k, i):
        p, ahead, behind = self.axes[k]
        q, ahead3, behind3 = self.axes[1 - k]
        h, g = 2 * self.rows, self.rows // 2
        lo, hi, lo3, hi3 = pl.ds(0, h), pl.ds(h, h), pl.ds(0, g), pl.ds(g, g)
        sb, ra, rf, ra3, rf3, block = self.sb, self.ra, self.rf, self.ra3, self.rf3, self.block
        src, dst, device = (
            lambda: (sb.at[t, 0, :, lo], ra.at[t, 0], ahead),
            lambda: (sb.at[t, 0, :, hi], ra.at[t, 1], behind),
            lambda: (sb.at[t, 1, :, hi], rf.at[t, 0, :, hi], ahead),
            lambda: (sb.at[t, 1, :, lo], rf.at[t, 1, :, lo], behind),
            lambda: (ra.at[t, 0], rf.at[t, 0, :, lo], ahead),
            lambda: (ra.at[t, 1], rf.at[t, 1, :, hi], behind),
            lambda: (sb.at[t, 0, :, block(turned(q, 2), 0)], ra3.at[t, 0], ahead3),
            lambda: (sb.at[t, 0, :, block(turned(q, 2), 1)], ra3.at[t, 1], behind3),
            lambda: (sb.at[t, 0, :, block(turned(q, 1), 1)], rf3.at[t, 0, :, hi3], ahead3),
            lambda: (sb.at[t, 0, :, block(turned(q, 3), 0)], rf3.at[t, 1, :, lo3], behind3),
            lambda: (ra3.at[t, 0], rf3.at[t, 0, :, lo3], ahead3),
            lambda: (ra3.at[t, 1], rf3.at[t, 1, :, hi3], behind3),
        )[i]()
        here = (0, 0, 0, 0, 1, 1, 2, 2, 2, 2, 3, 3)[i]
        there = (0, 1, 2, 2, 2, 2, 3, 4, 5, 5, 5, 5)[i]
        return send(src, dst, self.ss.at[t, here], self.rs.at[t, there], device)

    def sent(self, t, group):
        took((self.sb, self.ra, self.rf3, self.ra3)[group].at[t], self.ss.at[t, group])

    def arrived(self, t, group):
        ref = (self.ra.at[t, 0], self.ra.at[t, 1], self.rf.at[t], self.ra3.at[t, 0], self.ra3.at[t, 1], self.rf3.at[t])
        took(ref[group], self.rs.at[t, group])

    def start(self, t, k):
        p = self.axes[k][0]
        h = 2 * self.rows

        def far(i):
            self.sb[t, 0, i] = self.term(t, i, k, turned(p, 2), 0, 4).astype(BF16)

        def near(i):
            self.sb[t, 1, i, h:] = self.term(t, i, k, turned(p, 1), 2, 4).astype(BF16)
            self.sb[t, 1, i, :h] = self.term(t, i, k, turned(p, 3), 0, 2).astype(BF16)

        self.each(far)
        self.copy(t, k, 0).start()
        self.copy(t, k, 1).start()
        self.each(near)
        self.copy(t, k, 2).start()
        self.copy(t, k, 3).start()

    def merge(self, t, k):
        p = self.axes[k][0]
        for way, dest, first in ((0, turned(p, 1), 0), (1, turned(p, 3), 2)):
            self.arrived(t, way)

            def one(i):
                mine = self.term(t, i, k, dest, first, first + 2)
                self.ra[t, way, i] = (mine + self.ra[t, way, i].astype(F32)).astype(BF16)

            self.each(one)
            self.copy(t, k, 4 + way).start()

    def cross(self, t, k):
        p = self.axes[k][0]
        self.sent(t, 0)
        self.arrived(t, 2)

        def one(i):
            own = self.term(t, i, k, p, 0, 4)
            self.sb[t, 0, i] = (own + self.rf[t, 0, i].astype(F32) + self.rf[t, 1, i].astype(F32)).astype(BF16)

        self.each(one)
        for i in (6, 7, 8, 9):
            self.copy(t, k, i).start()

    def merge_cross(self, t, k):
        q = self.axes[1 - k][0]
        for way, dest in ((0, turned(q, 1)), (1, turned(q, 3))):
            self.arrived(t, 3 + way)

            def one(i):
                mine = self.sb[t, 0, i, self.block(dest, way), :]
                self.ra3[t, way, i] = (mine.astype(F32) + self.ra3[t, way, i].astype(F32)).astype(BF16)

            self.each(one)
            self.copy(t, k, 10 + way).start()

    def end(self, t, k):
        q = self.axes[1 - k][0]
        self.arrived(t, 5)

        def one(i):
            mine = self.sb[t, 0, i, self.block(q, None), :].astype(F32)
            self.finish(t, i, k, mine + self.rf3[t, 0, i].astype(F32) + self.rf3[t, 1, i].astype(F32))

        self.each(one)

    def drain(self, t, k):
        for group in (1, 2, 3):
            self.sent(t, group)


FFN_TILES, FFN_PARTS, FFN_WIDTH = 4, 3, 512
ATT_TILES, ATT_WIDTH = 5, 256
PACK = 32


EPS = 1e-05
NEG = -1e30
HIGH = lax.Precision.HIGHEST
ROWS = 256
WINDOW = 64
SPAN = ROWS + WINDOW
COLS = 512
HEADS, KEY_HEADS, DIM = 8, 2, 64
STATE = 72


def mm(a, b):
    return jnp.dot(a, b, preferred_element_type=F32)


def mm_nt(a, b, precision=None):
    return lax.dot_general(a, b, (((1,), (1,)), ((), ())), precision=precision, preferred_element_type=F32)


def mm_tn(a, b, precision=None):
    return lax.dot_general(a, b, (((0,), (0,)), ((), ())), precision=precision, preferred_element_type=F32)


def halves(value):
    top = value.astype(BF16)
    return top, (value - top.astype(F32)).astype(BF16)


def down_rows(a_q, a_k, a_v):
    return jnp.concatenate([a[...].astype(F32) for a in (a_q, a_k, a_v)], axis=0).astype(BF16)


def soft_pair(rows, table):
    both = mm(rows, jnp.concatenate([table, -table], axis=1))
    left = lax.broadcasted_iota(jnp.int32, both.shape, 1) < DIM
    upper = jnp.max(jnp.where(left, both, NEG), axis=1, keepdims=True)
    lower = jnp.max(jnp.where(left, NEG, both), axis=1, keepdims=True)
    grown = jnp.exp(both - jnp.where(left, upper, lower))
    sum_left = jnp.sum(jnp.where(left, grown, 0.0), axis=1, keepdims=True)
    sum_right = jnp.sum(jnp.where(left, 0.0, grown), axis=1, keepdims=True)
    return grown / jnp.where(left, sum_left, sum_right)


def doc_at(positions, lengths):
    first = lengths[0]
    second = first + lengths[1]
    return (
        (positions >= 0).astype(jnp.int32)
        + (positions >= first).astype(jnp.int32)
        + (positions >= second).astype(jnp.int32)
    )


def write_mask(mask, lengths):
    base = lax.axis_index("seq") * ROWS
    row = lax.broadcasted_iota(jnp.int32, (ROWS, SPAN), 0) + base
    column = lax.broadcasted_iota(jnp.int32, (ROWS, SPAN), 1) + base - WINDOW
    same = doc_at(row, lengths) == doc_at(column, lengths)
    offset = row - column
    here = jnp.where(offset < WINDOW, 0.0, NEG)
    mask[...] = jnp.where(same & (offset >= 0), here, 2.0 * NEG)


def middle(count, first, lengths):
    base = lax.axis_index("seq") * ROWS + first
    position = lax.broadcasted_iota(jnp.int32, (count, 1), 0) + base
    return (doc_at(position, lengths) == 2).astype(F32)


def value_columns(kv):
    lane = lax.broadcasted_iota(jnp.int32, kv.shape, 1)
    v = jnp.concatenate([kv[:, DIM:], kv[:, :DIM]], axis=1)
    return jnp.where(lane < DIM, v, jnp.where(lane == DIM, 1.0, 0.0).astype(kv.dtype))


class Scan:
    def __init__(self, refs, reverse):
        self.own, self.pair, self.line, self.plane, self.sem = refs
        self.reverse = reverse
        z, x, c, y = spot()
        self.z, self.x, self.c = z, x, c
        self.sibling = at(z, x, 1 - c, y)
        self.x_mates = [at(z, turned(x, i), c, y) for i in (1, 2, 3)]
        self.z_mates = [at(turned(z, i), x, c, y) for i in (1, 2, 3)]

    @staticmethod
    def scratch(shape):
        return [
            pltpu.VMEM((3, *shape), F32),
            pltpu.VMEM(shape, F32),
            pltpu.VMEM((3, *shape), F32),
            pltpu.VMEM((3, *shape), F32),
            pltpu.SemaphoreType.DMA((2, 7)),
        ]

    def pair_copy(self):
        return send(self.own.at[0], self.pair, self.sem.at[0, 0], self.sem.at[1, 0], self.sibling)

    def line_copy(self, i):
        return send(self.own.at[1], self.line.at[i], self.sem.at[0, 1 + i], self.sem.at[1, 1 + i], self.x_mates[i])

    def plane_copy(self, i):
        return send(self.own.at[2], self.plane.at[i], self.sem.at[0, 4 + i], self.sem.at[1, 4 + i], self.z_mates[i])

    def counts(self, me, other):
        return ((other > me) if self.reverse else (other < me)).astype(F32)

    def open(self):
        self.pair_copy().start()

    def along_x(self):
        self.pair_copy().wait()
        self.own[1] = self.own[0] + self.pair[...]
        for i in range(3):
            self.line_copy(i).start()

    def along_z(self):
        for i in range(3):
            self.line_copy(i).wait()
        self.own[2] = self.own[1] + self.line[0] + self.line[1] + self.line[2]
        for i in range(3):
            self.plane_copy(i).start()

    def close(self, total):
        for i in range(3):
            self.plane_copy(i).wait()
        for i in range(3):
            total = total + self.line[i] * self.counts(self.x, turned(self.x, 3 - i))
        for i in range(3):
            total = total + self.plane[i] * self.counts(self.z, turned(self.z, 3 - i))
        return total


def front_kernel(
    x_ref, gain_one, gain_two, a_q, a_k, a_v, b_q, b_k, b_v, f_q, f_k, a_out, b_out, lengths, w_q, w_k, w_v, w_o, cot_hbm,
    normed_out, low_out, qh, kv_out, state_out, att_out, stat_out, mixed_out, lowmix_out, hidden_out, g_out, scales_out, xt_out,
    wq, wk, wv, wo, cot, w_sem, phq, phk, num, mask, q_rows, stat, brief, tail_sem,
    part, came, y_sem, low_part, square, square_came,
    *scan_refs,
):
    z, x, c, y = spot()
    s = lax.axis_index("seq")
    following, leading = (lax.rem(s + 1, 32), y), (lax.rem(s + 31, 32), y)
    y_mates = [at(z, x, c, turned(y, i)) for i in (1, 2, 3)]
    scan = Scan(scan_refs, False)
    greet([following, leading, scan.sibling] + scan.x_mates + scan.z_mates + y_mates)
    loads = [
        pltpu.make_async_copy(src, dst, w_sem.at[i])
        for i, (src, dst) in enumerate(((w_q, wq), (w_k, wk), (w_v, wv), (w_o, wo), (cot_hbm, cot)))
    ]
    for load in loads:
        load.start()
    for i in range(4):
        rows = pl.ds(64 * i, 64)
        value = x_ref[rows, :].astype(F32)
        scale = lax.rsqrt(jnp.mean(value * value, axis=1, keepdims=True) + EPS)
        scales_out[rows, 0:1] = scale
        normed_out[rows, :] = (value * scale * gain_one[...]).astype(BF16)
    write_mask(mask, lengths)
    low_out[...] = mm_nt(normed_out[...], down_rows(a_q, a_k, a_v)).astype(BF16)
    low = low_out[...]
    loads[1].wait()
    loads[2].wait()
    k = (mm(normed_out[...], wk[...]) + mm(low[:, 8:16], b_k[...])).astype(BF16)
    v = (mm(normed_out[...], wv[...]) + mm(low[:, 16:24], b_v[...])).astype(BF16)
    for j in range(KEY_HEADS):
        cut = slice(j * DIM, (j + 1) * DIM)
        kv_out[j, WINDOW:] = jnp.concatenate([k[:, cut], v[:, cut]], axis=1)
    tail = send(
        kv_out.at[:, pl.ds(ROWS, WINDOW)], kv_out.at[:, pl.ds(0, WINDOW)], tail_sem.at[0], tail_sem.at[1], following
    )
    tail.start()
    loads[0].wait()
    for i in range(2):
        cut = slice(i * 256, (i + 1) * 256)
        q_rows[:, cut] = (mm(normed_out[...], wq[:, cut]) + mm(low[:, :8], b_q[:, cut])).astype(BF16)
    for h in range(HEADS):
        qh[h] = q_rows[:, h * DIM : (h + 1) * DIM]
    inside = middle(ROWS, 0, lengths)
    for j in range(KEY_HEADS):
        phk[j, WINDOW:] = soft_pair(kv_out[j, WINDOW:][:, :DIM], f_k[j]).astype(BF16)
        counted = (phk[j, WINDOW:].astype(F32) * inside).astype(BF16)
        rows = value_columns(kv_out[j, WINDOW:])
        settled = mm_tn(rows[: ROWS - WINDOW], counted[: ROWS - WINDOW])[:STATE]
        brief[0, j] = settled
        scan.own[0, j] = settled + mm_tn(rows[ROWS - WINDOW :], counted[ROWS - WINDOW :])[:STATE]
    brief_turn = send(brief.at[0], brief.at[1], tail_sem.at[2], tail_sem.at[3], scan.sibling)
    brief_turn.start()
    scan.open()

    def features(h, carry):
        phq[h] = soft_pair(qh[h], f_q[h]).astype(BF16)
        return carry

    lax.fori_loop(0, 4, features, 0)
    scan.along_x()
    lax.fori_loop(4, HEADS, features, 0)
    tail.wait()
    inside = middle(WINDOW, -WINDOW, lengths)
    for j in range(KEY_HEADS):
        phk[j, :WINDOW] = soft_pair(kv_out[j, :WINDOW][:, :DIM], f_k[j]).astype(BF16)
        counted = (phk[j, :WINDOW].astype(F32) * inside).astype(BF16)
        brief[2, j] = mm_tn(value_columns(kv_out[j, :WINDOW]), counted)[:STATE]
    brief_turn.wait()

    def inner(h, carry):
        j = lax.div(h, 4)
        kv = kv_out[j]
        distant = mask[...] == NEG
        scores = mm_nt(qh[h], kv[:, :DIM]) * (DIM**-0.5) + mask[...]
        top = jnp.max(scores, axis=1, keepdims=True)
        weights = jnp.exp(scores - top)
        total = weights + jnp.where(distant, mm_nt(phq[h], phk[j]) * jnp.exp(-top), 0.0)
        high = total.astype(BF16)
        rest = jnp.where(distant, total - high.astype(F32), 0.0).astype(BF16)
        v = kv[:, DIM:]
        num[h] = mm(high, v) + mm(rest, v)
        stat[h, :, 0:1] = top
        stat[h, :, 1:2] = jnp.sum(total, axis=1, keepdims=True)
        return carry

    lax.fori_loop(0, 4, inner, 0)
    scan.along_z()
    lax.fori_loop(4, HEADS, inner, 0)
    second = c.astype(F32)
    state_out[...] = scan.close(brief[1] * second - brief[2] * (1.0 - second))
    mine = middle(ROWS, 0, lengths)
    for h in range(HEADS):
        top, rest = halves(state_out[h // 4])
        carried = mm_nt(phq[h], top) + mm_nt(phq[h], rest)
        gate = jnp.exp(-stat[h, :, 0:1]) * mine
        total = stat[h, :, 1:2] + gate * carried[:, DIM : DIM + 1]
        stat[h, :, 1:2] = total
        stat[h, :, 2:3] = gate
        cut = slice(h * DIM, (h + 1) * DIM)
        attended = (num[h] + gate * carried[:, :DIM]) / total
        att_out[:, cut] = attended
        mixed_out[:, cut] = attended.astype(BF16)
        stat_out[h] = stat[h].T
    mixed = mixed_out[...]
    low_part[y] = mm_nt(a_out[...], mixed)
    low_turns = [send(low_part.at[y], low_part.at[y], y_sem.at[0, i], y_sem.at[1, i], y_mates[i]) for i in range(3)]
    for turn in low_turns:
        turn.start()
    loads[3].wait()

    def columns(ref, d):
        return ref[:, pl.ds(pl.multiple_of(d * COLS, COLS), COLS)]

    turns = [send(part.at[i], came.at[i], y_sem.at[0, 3 + i], y_sem.at[1, 3 + i], y_mates[i]) for i in range(3)]
    for i in (1, 0, 2):
        part[i] = mm(mixed, columns(wo, turned(y, 1 + i))).astype(BF16)
        turns[i].start()
    value = mm(mixed, columns(wo, y)) + columns(x_ref, y).astype(F32)

    def by_owner(m, rows):
        for i in range(16):
            flat = rows[:, i * 128 : (i + 1) * 128].T
            xt_out[m, 0, i // 4, i % 4] = flat[:64]
            xt_out[m, 1, i // 4, i % 4] = flat[64:]

    by_owner(0, normed_out)
    for i in range(3):
        here = low_part.at[turned(y, 3 - i)]
        send(here, here, y_sem.at[0, i], y_sem.at[1, i], y_mates[i]).wait()
    low_sum = low_part[0] + low_part[1] + low_part[2] + low_part[3]
    lowmix_out[...] = low_sum.T.astype(BF16)
    value = value + mm(lowmix_out[...], columns(b_out, y))
    for turn in turns:
        turn.wait()
    value = value + came[0].astype(F32) + came[1].astype(F32) + came[2].astype(F32)
    hidden_out[...] = value
    g_out[y] = (value * columns(gain_two, y)).astype(BF16)
    turns = [send(g_out.at[y], g_out.at[y], y_sem.at[0, 9 + i], y_sem.at[1, 9 + i], y_mates[i]) for i in range(3)]
    square[...] = mm_nt(jnp.ones((8, COLS), F32), value * value, HIGH)
    square_turns = [
        send(square, square_came.at[i], y_sem.at[0, 6 + i], y_sem.at[1, 6 + i], y_mates[i]) for i in range(3)
    ]
    for turn in square_turns + turns:
        turn.start()
    loads[4].wait()
    by_owner(1, cot)
    for turn in square_turns:
        turn.wait()
    mean = (square[...] + square_came[0] + square_came[1] + square_came[2]) * (1.0 / 2048)
    scales_out[:, 1:2] = lax.rsqrt(mean + EPS).T[:, 0:1]
    for i in range(3):
        here = g_out.at[turned(y, 3 - i)]
        send(here, here, y_sem.at[0, 9 + i], y_sem.at[1, 9 + i], y_mates[i]).wait_recv()
    for turn in turns:
        turn.wait_send()


def front(*args):
    anywhere = pl.BlockSpec(memory_space=pl.ANY)
    vmem = pl.BlockSpec(memory_space=pltpu.VMEM)
    shapes = (
        ((ROWS, 2048), BF16),
        ((ROWS, 24), BF16),
        ((HEADS, ROWS, DIM), BF16),
        ((KEY_HEADS, SPAN, 128), BF16),
        ((KEY_HEADS, STATE, 128), F32),
        ((ROWS, 512), F32),
        ((HEADS, 8, ROWS), F32),
        ((ROWS, 512), BF16),
        ((ROWS, 8), BF16),
        ((ROWS, COLS), F32),
        ((4, ROWS, COLS), BF16),
        ((ROWS, 2), F32),
        ((2, 2, 4, 4, 64, ROWS), BF16),
    )
    return pl.pallas_call(
        front_kernel,
        out_shape=tuple(jax.ShapeDtypeStruct(*shape) for shape in shapes),
        in_specs=[vmem] * 13 + [pl.BlockSpec(memory_space=pltpu.SMEM)] + [anywhere] * 5,
        out_specs=(vmem,) * len(shapes),
        scratch_shapes=[
            pltpu.VMEM((2048, 512), BF16),
            pltpu.VMEM((2048, 128), BF16),
            pltpu.VMEM((2048, 128), BF16),
            pltpu.VMEM((512, 2048), BF16),
            pltpu.VMEM((ROWS, 2048), BF16),
            pltpu.SemaphoreType.DMA((5,)),
            pltpu.VMEM((HEADS, ROWS, 128), BF16),
            pltpu.VMEM((KEY_HEADS, SPAN, 128), BF16),
            pltpu.VMEM((HEADS, ROWS, DIM), F32),
            pltpu.VMEM((ROWS, SPAN), F32),
            pltpu.VMEM((ROWS, 512), BF16),
            pltpu.VMEM((HEADS, ROWS, 8), F32),
            pltpu.VMEM((3, KEY_HEADS, STATE, 128), F32),
            pltpu.SemaphoreType.DMA((4,)),
            pltpu.VMEM((3, ROWS, COLS), BF16),
            pltpu.VMEM((3, ROWS, COLS), BF16),
            pltpu.SemaphoreType.DMA((2, 12)),
            pltpu.VMEM((4, 8, ROWS), F32),
            pltpu.VMEM((8, ROWS), F32),
            pltpu.VMEM((3, 8, ROWS), F32),
            *Scan.scratch((KEY_HEADS, STATE, 128)),
        ],
        compiler_params=pltpu.CompilerParams(
            collective_id=1, has_side_effects=True, vmem_limit_bytes=60 * 2**20
        ),
        name="front",
    )(*args)


def soft_back(soft, grad):
    left = lax.broadcasted_iota(jnp.int32, soft.shape, 1) < DIM
    part = soft * grad
    sum_left = jnp.sum(jnp.where(left, part, 0.0), axis=1, keepdims=True)
    sum_right = jnp.sum(jnp.where(left, 0.0, part), axis=1, keepdims=True)
    both = part - soft * jnp.where(left, sum_left, sum_right)
    return both[:, :DIM] - both[:, DIM:]


def late_kernel(
    hidden_in, scales, gain_one, gain_two, mixed, low_mix, att, stat, state, qh, kv, low,
    f_q, f_k, a_q, a_k, a_v, a_out, b_out, b_q, b_k, b_v, lengths,
    g_hbm, normed_hbm, x_hbm, cot_hbm, xt_hbm, w_q, w_k, w_v, w_o, w_gate, w_up, w_down,
    out_block, out_inputs, out_ffn, out_att, out_pack, out_gain,
    wb, x_all, w_sem,
    gs_came, ffn_came, gf_part, dot_part, dot_came, gb, gres, gsum, y_sem,
    xf, yf, xs, sem_ffn, xa, ya, sem_att, pk, sem_pack,
    mask, gh, pq, pkey, dext, dkv, gfq, gfk, ret, ret_came, next_state, ret_sem, glow, gkv, wide, gao, gbo, down_ref,
    first, gain_row, gain_rows_ref, px, px_came, pz, crown, sem_zx, stage, sem_stage, gain_c, gain_x, gain_z, gain_y, sem_gain,
    *rest,
):
    scan = Scan(rest[0:5], True)
    refs_big, refs_mid = rest[5:12], rest[12:19]
    z, x, c, y = spot()
    s = lax.axis_index("seq")
    following, leading = (lax.rem(s + 1, 32), y), (lax.rem(s + 31, 32), y)
    y_mates = [at(z, x, c, turned(y, i)) for i in (1, 2, 3)]
    sibling = scan.sibling
    greet([following, leading, sibling] + scan.x_mates + scan.z_mates + y_mates)

    def columns(ref, d):
        return ref[:, pl.ds(pl.multiple_of(d * COLS, COLS), COLS)]

    def to_mates(base, pieces, slots):
        return [
            send(pieces(i), slots.at[i], y_sem.at[0, base + i], y_sem.at[1, base + i], y_mates[i]) for i in range(3)
        ]

    own_rows, far_rows = pl.ds(0, ROWS), pl.ds(ROWS, ROWS)

    def local(i, src, dst):
        return pltpu.make_async_copy(src, dst, w_sem.at[i])

    def turn_at(n):
        return turned(y, 1 + n)

    def part(n):
        return pl.ds(pl.multiple_of(n * COLS, COLS), COLS)

    def held(slot):
        local(slot, w_o.at[:, part(0)], wb.at[slot]).wait()

    def load_forward(u, slot):
        i = slot % 4
        src = (
            lambda: w_gate.at[part(i), part(u)],
            lambda: w_up.at[part(i), part(u)],
            lambda: w_down.at[part(u), part(i)],
        )[slot // 4]()
        local(slot, src, wb.at[slot]).start()

    def load_later(b):
        slot = b % 12
        if b < 32:
            src = (w_gate, w_up)[b % 8 // 4].at[part(turn_at(b // 8)), part(b % 4)]
        elif b < 48:
            src = w_down.at[part(b % 4), part(turn_at((b - 32) // 4))]
        elif b < 52:
            src = w_o.at[:, part(slot)]
        elif b < 56:
            src = w_q.at[part(slot - 4)]
        else:
            rows = part(slot - 8)
            local(slot, w_k.at[rows], wb.at[slot, :, pl.ds(0, 128)]).start()
            local(slot + 4, w_v.at[rows], wb.at[slot, :, pl.ds(128, 128)]).start()
            return
        local(slot, src, wb.at[slot]).start()

    def held_pair(slot):
        rows = part(slot - 8)
        local(slot, w_k.at[rows], wb.at[slot, :, pl.ds(0, 128)]).wait()
        local(slot + 4, w_v.at[rows], wb.at[slot, :, pl.ds(128, 128)]).wait()

    load_g = local(16, g_hbm, gb)
    load_cot = local(17, cot_hbm, x_all)
    load_x = local(18, x_hbm, x_all)
    load_n = [local(19 + i, normed_hbm.at[:, pl.ds(i * COLS, COLS)], gb.at[i]) for i in range(4)]
    load_g.start()
    for slot in range(12):
        load_forward(0, slot)
    load_cot.start()

    left_cot = [
        pltpu.make_async_copy(xt_hbm.at[1, c], xf.at[1, :, :, :, own_rows], w_sem.at[23]),
        send(xt_hbm.at[1, 1 - c], xf.at[1, :, :, :, far_rows], sem_ffn.at[0, 0], sem_ffn.at[1, 0], sibling),
    ]
    left_g = send(xs, xf.at[0, :, :, :, far_rows], sem_ffn.at[0, 1], sem_ffn.at[1, 1], sibling)

    def right_ffn(t):
        return send(yf.at[t, :, own_rows], yf.at[t, :, far_rows], sem_ffn.at[0, 2 + t], sem_ffn.at[1, 2 + t], sibling)

    left_att = [
        pltpu.make_async_copy(xt_hbm.at[0, c], xa.at[0, :, :, :, own_rows], w_sem.at[24]),
        send(xt_hbm.at[0, 1 - c], xa.at[0, :, :, :, far_rows], sem_att.at[0, 0], sem_att.at[1, 0], sibling),
    ]
    left_gb = send(xs, xa.at[1, :, :, :, far_rows], sem_att.at[0, 1], sem_att.at[1, 1], sibling)

    def right_att(t):
        return send(ya.at[t, own_rows], ya.at[t, far_rows], sem_att.at[0, 2 + t], sem_att.at[1, 2 + t], sibling)

    def by_owner(m, xd):
        for i in range(16):
            block = gb[i // 4, :, (i % 4) * 128 : (i % 4 + 1) * 128].T
            xd[m, i // 4, i % 4, :, 0:ROWS] = jnp.where(c == 0, block[:64], block[64:])
            xs[i // 4, i % 4] = jnp.where(c == 0, block[64:], block[:64])

    for copy in left_cot:
        copy.start()
    load_g.wait()
    by_owner(0, xf)
    left_g.start()

    def product(xd, right):
        def term(t, i, k, dest, first, last):
            m, yd = right(t, i)
            rows = xd[m, first:last, dest] if k == 0 else xd[m, dest, first:last]
            return mm(rows.reshape((last - first) * 64, 2 * ROWS), yd)

        return term

    def finish_ffn(t, i, k, value):
        stage[k, i] = value

    def write_ffn(t, k):
        return pltpu.make_async_copy(stage.at[k], out_ffn.at[:, t], sem_stage.at[k])

    def close_ffn(t):
        if t >= 2:
            write_ffn(t - 2, t % 2).wait()
        big.end(t, t % 2)
        write_ffn(t, t % 2).start()

    def finish_att(t, i, k, value):
        out_att[t] = value

    big = Ring(refs_big, 64, FFN_PARTS, product(xf, lambda t, i: (lax.div(i, 2), yf[t, i])), finish_ffn)
    mid = Ring(refs_mid, 64, 1, product(xa, lambda t, i: (t // 3, ya[t])), finish_att)

    def begin(u):
        right_ffn(u).wait()
        big.start(u, u % 2)

    def feed(u, carry):
        def through(first_slot, term):
            value = jnp.zeros((ROWS, COLS), F32)
            for i in range(4):
                slot = first_slot + i
                held(slot)
                value = value + term(i, slot)

                @pl.when(u < 3)
                def _():
                    load_forward(u + 1, slot)

                @pl.when(u == 3)
                def _():
                    load_later(slot)

            return value * scales[:, 1:2]

        gate = through(0, lambda i, slot: mm(gb[i], wb[slot]))
        up = through(4, lambda i, slot: mm(gb[i], wb[slot]))

        @pl.when(u == 0)
        def _():
            load_cot.wait()

        grad = through(8, lambda i, slot: mm_nt(x_all[:, i * COLS : (i + 1) * COLS], wb[slot]))
        sigmoid = jax.nn.sigmoid(gate)
        active = gate * sigmoid
        yf[u, 0, own_rows] = (grad * up * sigmoid * (1.0 + gate * (1.0 - sigmoid))).astype(BF16)
        yf[u, 1, own_rows] = (grad * active).astype(BF16)
        yf[u, 2, own_rows] = (active * up).astype(BF16)
        right_ffn(u).start()

        @pl.when(u == 1)
        def _():
            for copy in left_cot:
                copy.wait()
            left_g.wait()
            begin(0)

        @pl.when(u == 3)
        def _():
            begin(1)

        return carry

    lax.fori_loop(0, FFN_TILES, feed, 0)
    for copy in left_att:
        copy.start()
    inverse = 1.0 / scales[:, 1:2]
    gs_turns = to_mates(0, lambda i: gf_part.at[i], gs_came)
    dot = jnp.zeros((ROWS, 1), F32)
    for n in range(4):
        value = jnp.zeros((ROWS, COLS), F32)
        for b in range(8 * n, 8 * n + 8):
            held(b % 12)
            value = value + mm_nt(yf[b % 4, b % 8 // 4, 0:ROWS], wb[b % 12])
            load_later(b + 12)
        value = value * inverse
        dot = dot + jnp.sum(value * gb[turn_at(n)].astype(F32), axis=1, keepdims=True)
        if n < 3:
            gf_part[n] = value.astype(BF16)
            gs_turns[n].start()
        else:
            gsum[...] = value
    dot_part[...] = jnp.broadcast_to(dot, (ROWS, 128)).T[:8]
    gs_dots = to_mates(3, lambda i: dot_part, dot_came)
    for turn in gs_dots:
        turn.start()
    begin(2)

    for turn in gs_turns + gs_dots:
        turn.wait()
    total = gsum[...] + gs_came[0].astype(F32) + gs_came[1].astype(F32) + gs_came[2].astype(F32)
    gsum[...] = total
    gain_rows = jnp.sum(total * hidden_in[...] * scales[:, 1:2], axis=0, keepdims=True)
    gain_rows_ref[...] = jnp.concatenate([gain_rows[:, i * 128 : (i + 1) * 128] for i in range(4)])

    def mean_column(own):
        return ((own + dot_came[0] + dot_came[1] + dot_came[2]) * (1.0 / 2048)).T[:, 0:1]

    scale = scales[:, 1:2]
    residual = (
        columns(x_all, y).astype(F32)
        + scale * (gsum[...] * columns(gain_two, y))
        - hidden_in[...] * (scale * scale * scale * mean_column(dot_part[...]))
    )
    gres[...] = residual
    gb[y] = residual.astype(BF16)
    gb_turns = [
        send(gb.at[y], gb.at[y], y_sem.at[0, 6 + i], y_sem.at[1, 6 + i], y_mates[i]) for i in range(3)
    ]
    for turn in gb_turns:
        turn.start()
    load_x.start()

    ffn_turns = to_mates(9, lambda i: gf_part.at[i], ffn_came)
    for n in range(4):
        value = jnp.zeros((ROWS, COLS), F32)
        for b in range(32 + 4 * n, 36 + 4 * n):
            held(b % 12)
            value = value + mm(yf[b % 4, 2, 0:ROWS], wb[b % 12])
            load_later(b + 12)
        if n < 3:
            gf_part[n] = value.astype(BF16)
            ffn_turns[n].start()
        else:
            out_inputs[...] = value
    begin(3)
    write_mask(mask, lengths)
    def features(h, carry):
        pq[h] = soft_pair(qh[h], f_q[h])
        return carry

    lax.fori_loop(0, HEADS, features, 0)
    for j in range(KEY_HEADS):
        pkey[j] = soft_pair(kv[j][:, :DIM], f_k[j])
        pkey[KEY_HEADS + j] = jnp.zeros((SPAN, 128), F32)
    dkv[...] = jnp.zeros(dkv.shape, F32)
    pk[...] = jnp.zeros(pk.shape, F32)
    big.merge(0, 0)

    for i in range(3):
        here = gb.at[turned(y, 3 - i)]
        send(here, here, y_sem.at[0, 6 + i], y_sem.at[1, 6 + i], y_mates[i]).wait_recv()
    for slot in range(4):
        held(slot)
    grad_low = jnp.zeros((ROWS, 8), F32)
    grad_mixed = jnp.zeros((ROWS, COLS), F32)
    for k in range(4):
        cut = slice(k * COLS, (k + 1) * COLS)
        grad_low = grad_low + mm_nt(gb[k], b_out[:, cut])
        grad_mixed = grad_mixed + mm_nt(gb[k], wb[k])
    grad_mixed = grad_mixed + jnp.dot(
        grad_low, a_out[...].astype(F32), precision=HIGH, preferred_element_type=F32
    )
    rounded = grad_mixed.astype(BF16)
    for h in range(HEADS):
        gh[h] = rounded[:, h * DIM : (h + 1) * DIM]
    top, bottom = halves(grad_low)
    gao[...] = mm_tn(top, mixed[...]) + mm_tn(bottom, mixed[...])
    for k in range(4):
        gbo[:, k * COLS : (k + 1) * COLS] = mm_tn(low_mix[...], gb[k])

    lane = lax.broadcasted_iota(jnp.int32, (ROWS, DIM), 1)
    for h in range(HEADS):
        j = h // 4
        grad = gh[h].astype(F32)
        column = stat[h].T
        den = column[:, 1:2]
        inner = -jnp.sum(grad * att[:, h * DIM : (h + 1) * DIM], axis=1, keepdims=True) / den
        ext = jnp.concatenate([grad / den, jnp.where(lane == 0, inner, 0.0)], axis=1)
        dext[h] = ext
        top, bottom = halves(ext * column[:, 2:3])
        phi = pq[h].astype(BF16)
        piece = (mm_tn(top, phi) + mm_tn(bottom, phi))[:STATE]
        scan.own[0, j] = piece if h % 4 == 0 else scan.own[0, j] + piece
    scan.open()

    by_owner(1, xa)
    for turn in gb_turns:
        turn.wait_send()
    for load in load_n:
        load.start()
    left_gb.start()
    for t in (3, 4):
        ya[t, 0:ROWS] = mixed[:, (t - 3) * ATT_WIDTH : (t - 2) * ATT_WIDTH]
        right_att(t).start()
    scan.along_x()
    left_gb.wait()
    for t in (3, 4):
        right_att(t).wait()
        mid.start(t, t % 2)

    def backward(h, carry):
        j = lax.div(h, 4)
        keys, values = kv[j][:, :DIM], kv[j][:, DIM:]
        q, grad, ext = qh[h], gh[h], dext[h]
        column = stat[h].T
        top, den, gate = column[:, 0:1], column[:, 1:2], column[:, 2:3]
        distant = mask[...] == NEG
        soft = pq[h]
        phi, phi_key = soft.astype(BF16), pkey[j].astype(BF16)
        damping = jnp.where(distant, jnp.exp(-top), 0.0)
        weights = jnp.exp(mm_nt(q, keys) * (DIM**-0.5) + mask[...] - top)
        grad_weights = mm_nt(grad, values) / den + ext[:, DIM : DIM + 1]
        grad_scores = (weights * grad_weights).astype(BF16)
        grad_linear = (damping * grad_weights).astype(BF16)
        both = weights.astype(BF16).astype(F32) + mm_nt(phi, phi_key) * damping
        high, rest = halves(both / den)
        grad_q = mm(grad_scores, keys) * (DIM**-0.5)
        grad_k = mm_tn(grad_scores, q) * (DIM**-0.5)
        dkv[j] = dkv[j] + jnp.concatenate([grad_k, mm_tn(high, grad) + mm_tn(rest, grad)], axis=1)
        pkey[KEY_HEADS + j] = pkey[KEY_HEADS + j] + mm_tn(grad_linear, phi)
        carried = jnp.dot(
            (ext * gate)[:, :STATE], state[j], precision=HIGH, preferred_element_type=F32
        )
        grad_soft = mm(grad_linear, phi_key) + carried
        high, rest = halves(soft_back(soft, grad_soft))
        gh[h] = (grad_q + mm_nt(high, f_q[h]) + mm_nt(rest, f_q[h])).astype(BF16)
        gfq[h] = mm_tn(q, high) + mm_tn(q, rest)

        @pl.when(h == 1)
        def _():
            scan.along_z()

        @pl.when(h == 0)
        def _():
            big.merge(1, 1)

        @pl.when(h == 4)
        def _():
            big.merge(2, 0)

        @pl.when(h == 6)
        def _():
            big.cross(0, 0)

        @pl.when(h == 7)
        def _():
            big.merge(3, 1)

        return carry

    lax.fori_loop(0, HEADS, backward, 0)

    for j in range(KEY_HEADS):
        ret[j] = jnp.concatenate([dkv[j, :WINDOW], pkey[KEY_HEADS + j, :WINDOW]], axis=1)
    home = [
        send(ret, ret_came, ret_sem.at[0], ret_sem.at[1], leading),
        send(scan.own.at[0], next_state, ret_sem.at[2], ret_sem.at[3], leading),
    ]
    for copy in home:
        copy.start()
    gq = jnp.concatenate([gh[h] for h in range(HEADS)], axis=1)
    for i in range(2):
        ya[i, 0:ROWS] = gq[:, i * ATT_WIDTH : (i + 1) * ATT_WIDTH]
        right_att(i).start()
    down_ref[...] = down_rows(a_q, a_k, a_v)
    for slot in range(4, 8):
        held(slot)
    for slot in range(8, 12):
        held_pair(slot)
    for load in load_n + [load_x]:
        load.wait()
    glow[:, :8] = mm_nt(gq, b_q[...])
    for copy in left_att:
        copy.wait()
    for t in range(2):
        right_att(t).wait()
        mid.start(t, t % 2)
    for k in range(4):
        first[k] = mm_nt(gq, wb[4 + k])

    inside = middle(ROWS, 0, lengths)
    suffix = scan.close(scan.pair[...] * (1.0 - c.astype(F32)))
    for copy in home:
        copy.wait()
    joined = (s < 31).astype(F32)
    late_row = lax.broadcasted_iota(jnp.int32, (ROWS, 128), 0) >= ROWS - WINDOW
    for j in range(KEY_HEADS):
        soft = pkey[j, WINDOW:]
        phi = soft.astype(BF16)
        keys = kv[j, WINDOW:][:, :DIM]
        rows = value_columns(kv[j, WINDOW:])[:, :STATE]
        high, rest = halves(suffix[j])
        high_next, rest_next = halves(suffix[j] - joined * next_state[j])
        grad_phi = jnp.where(late_row, mm(rows, high_next) + mm(rows, rest_next), mm(rows, high) + mm(rows, rest))
        grad_phi = grad_phi * inside + pkey[KEY_HEADS + j, WINDOW:]
        grad_v = jnp.where(
            late_row[:, :STATE], mm_nt(phi, high_next) + mm_nt(phi, rest_next), mm_nt(phi, high) + mm_nt(phi, rest)
        )
        grad_v = (grad_v * inside)[:, :DIM]
        last = ROWS - WINDOW
        grad_phi = jnp.concatenate([grad_phi[:last], grad_phi[last:] + ret_came[j][:, 2 * DIM :]], axis=0)
        high, rest = halves(soft_back(soft, grad_phi))
        grad_k = mm_nt(high, f_k[j]) + mm_nt(rest, f_k[j])
        gfk[j] = mm_tn(keys, high) + mm_tn(keys, rest)
        dkv[j, WINDOW:] = dkv[j, WINDOW:] + jnp.concatenate([grad_k, grad_v], axis=1)
        dkv[j, ROWS:] = dkv[j, ROWS:] + ret_came[j][:, : 2 * DIM]
    gk = jnp.concatenate([dkv[j, WINDOW:][:, :DIM] for j in range(KEY_HEADS)], axis=1).astype(BF16)
    gv = jnp.concatenate([dkv[j, WINDOW:][:, DIM:] for j in range(KEY_HEADS)], axis=1).astype(BF16)
    gkv[...] = jnp.concatenate([gk, gv], axis=1)
    ya[2, 0:ROWS] = gkv[...]
    right_att(2).start()

    glow[:, 8:16] = mm_nt(gk, b_k[...])
    glow[:, 16:24] = mm_nt(gv, b_v[...])
    glow_high, glow_rest = halves(glow[...])
    for k in range(4):
        wide[:, k * COLS : (k + 1) * COLS] = mm_tn(glow_high, gb[k]) + mm_tn(glow_rest, gb[k])

    def place(d):
        return d // 16, d // 4 % 4, d % 4

    for i in range(16):
        cut = slice(i * 128, (i + 1) * 128)
        for half in range(2):
            d = place(2 * i + half)
            pk[*d, 0:12] = wide[12 * half : 12 * half + 12, cut]
            pk[*d, 13:16] = 0.25 * gbo[3 * half : 3 * half + 3, cut]
        pk[*place(26 + i // 8), 16 + 2 * (i % 8) : 18 + 2 * (i % 8)] = gbo[6:8, cut]

    def low_half(d, value):
        pk[*place(d), 16 : 16 + value.shape[0]] = value

    for i in range(4):
        pair = jnp.concatenate([gfq[2 * i], gfq[2 * i + 1]], axis=1)
        for part in range(4):
            low_half(4 * i + part, pair[16 * part : 16 * part + 16])
    pair = jnp.concatenate([gfk[0], gfk[1]], axis=1)
    for part in range(4):
        low_half(16 + part, pair[16 * part : 16 * part + 16])
    grad_b = jnp.concatenate(
        [mm_tn(low[:, :8], gq), mm_tn(low[:, 8:16], gkv[:, :128]), mm_tn(low[:, 16:24], gkv[:, 128:])], axis=1
    )
    for i in range(3):
        low_half(20 + i, jnp.concatenate([grad_b[:, 256 * i : 256 * i + 128], grad_b[:, 256 * i + 128 : 256 * i + 256]]))
    for i in range(2):
        low_half(23 + i, jnp.concatenate([gao[:, 256 * i : 256 * i + 128], gao[:, 256 * i + 128 : 256 * i + 256]]))
    low_half(25, gain_rows_ref[...])
    pack_far = send(pk.at[1 - c], pk.at[2], sem_pack.at[0], sem_pack.at[1], sibling)
    pack_far.start()

    for turn in ffn_turns:
        turn.wait()
    out_block[...] = (
        hidden_in[...]
        + out_inputs[...]
        + ffn_came[0].astype(F32)
        + ffn_came[1].astype(F32)
        + ffn_came[2].astype(F32)
    ).astype(BF16)
    gf_turns = to_mates(12, lambda i: gf_part.at[i], gs_came)

    def partial_first(d, dot):
        rows = pl.ds(pl.multiple_of(d * COLS, COLS), COLS)
        down = columns(down_ref, d)
        part = first[d] + mm_nt(gkv[...], wb[8 + d, :, 0:256]) + mm(glow_high, down) + mm(glow_rest, down)
        shaped = part * columns(x_all, d).astype(F32)
        gain_row[:, rows] = jnp.sum(shaped * scales[:, 0:1], axis=0, keepdims=True)
        return part, dot + jnp.sum(shaped * columns(gain_one, d), axis=1, keepdims=True)

    def spread(sems, base, piece, mates, back_piece):
        turns = [send(piece, piece, sems.at[0, base + i], sems.at[1, base + i], mate) for i, mate in enumerate(mates)]
        for turn in turns:
            turn.start()
        return [
            send(back_piece(i), back_piece(i), sems.at[0, base + i], sems.at[1, base + i], mate)
            for i, mate in enumerate(mates)
        ]

    def settle(turns):
        for turn in turns:
            turn.wait()

    dot = jnp.zeros((ROWS, 1), F32)
    for i in (1, 0):
        chunk, dot = partial_first(turned(y, 1 + i), dot)
        gf_part[i] = chunk.astype(BF16)
        gf_turns[i].start()

    pack_far.wait()
    x_turns = [send(px.at[i], px_came.at[i], sem_zx.at[0, i], sem_zx.at[1, i], scan.x_mates[i]) for i in range(3)]
    for i in range(3):
        dest = turned(x, 1 + i)
        px[i] = (pk[c, :, dest] + pk[2, :, dest]).astype(BF16)
        x_turns[i].start()
    chunk, dot = partial_first(turned(y, 3), dot)
    gf_part[2] = chunk.astype(BF16)
    gf_turns[2].start()
    chunk, dot = partial_first(y, dot)
    gsum[...] = chunk
    dot_part[...] = jnp.broadcast_to(dot, (ROWS, 128)).T[:8]
    dot_turns = to_mates(15, lambda i: dot_part, dot_came)
    for turn in dot_turns:
        turn.start()
    for i in range(16):
        gain_c[c, i : i + 1] = gain_row[:, i * 128 : (i + 1) * 128]
    gain_turns = spread(sem_gain, 0, gain_c.at[c], [sibling], lambda i: gain_c.at[1 - c])
    own_pack = pk[c, :, x] + pk[2, :, x]
    right_att(2).wait()
    mid.start(2, 0)
    settle(x_turns)
    own_pack = own_pack + px_came[0].astype(F32) + px_came[1].astype(F32) + px_came[2].astype(F32)
    pz[z] = own_pack.astype(BF16)
    z_turns = spread(sem_zx, 3, pz.at[z], scan.z_mates, lambda i: pz.at[turned(z, 3 - i)])
    settle(gain_turns)
    gain_x[x] = gain_c[0] + gain_c[1]
    gain_turns = spread(sem_gain, 1, gain_x.at[x], scan.x_mates, lambda i: gain_x.at[turned(x, 3 - i)])
    for t in (3, 4, 0, 1):
        mid.merge(t, t % 2)
    settle(z_turns)
    own_pack = pz[0].astype(F32) + pz[1].astype(F32) + pz[2].astype(F32) + pz[3].astype(F32)
    crown[y] = own_pack[:, :16]
    y_turns = spread(sem_zx, 10, crown.at[y], y_mates, lambda i: crown.at[turned(y, 3 - i)])
    settle(gain_turns)
    gain_z[z] = gain_x[0] + gain_x[1] + gain_x[2] + gain_x[3]
    gain_turns = spread(sem_gain, 4, gain_z.at[z], scan.z_mates, lambda i: gain_z.at[turned(z, 3 - i)])
    big.cross(1, 1)
    mid.merge(2, 0)
    settle(y_turns)
    top = crown[0] + crown[1] + crown[2] + crown[3]
    out_pack[c, :, x] = jnp.concatenate([top, own_pack[:, 16:]], axis=1).astype(BF16)
    x_turns = spread(sem_zx, 6, out_pack.at[c, :, x], scan.x_mates, lambda i: out_pack.at[c, :, turned(x, 3 - i)])
    settle(gain_turns)
    gain_y[y] = gain_z[0] + gain_z[1] + gain_z[2] + gain_z[3]
    gain_turns = spread(sem_gain, 7, gain_y.at[y], y_mates, lambda i: gain_y.at[turned(y, 3 - i)])
    big.cross(2, 0)
    for t in (3, 4, 0, 1, 2):
        mid.cross(t, t % 2)
    settle(gf_turns + dot_turns)
    total = gsum[...] + gs_came[0].astype(F32) + gs_came[1].astype(F32) + gs_came[2].astype(F32)
    scale = scales[:, 0:1]
    out_inputs[...] = (
        gres[...]
        + scale * (total * columns(gain_one, y))
        - columns(x_all, y).astype(F32) * (scale * scale * scale * mean_column(dot_part[...]))
    )
    settle(x_turns)
    last = spread(sem_zx, 9, out_pack.at[c], [sibling], lambda i: out_pack.at[1 - c])
    settle(gain_turns)
    out_gain[...] = gain_y[0] + gain_y[1] + gain_y[2] + gain_y[3]
    big.cross(3, 1)
    for t in range(FFN_TILES):
        big.merge_cross(t, t % 2)
    for t in (3, 4, 0, 1, 2):
        mid.merge_cross(t, t % 2)
    for t in range(FFN_TILES):
        close_ffn(t)
    for t in (3, 4, 0, 1, 2):
        mid.end(t, t % 2)
    settle(last)
    for i in range(2):
        write_ffn(FFN_TILES - 2 + i, i).wait()
    for t in range(FFN_TILES):
        big.drain(t, t % 2)
    for t in range(ATT_TILES):
        mid.drain(t, t % 2)


def late(args, weights):
    anywhere = pl.BlockSpec(memory_space=pl.ANY)
    vmem = pl.BlockSpec(memory_space=pltpu.VMEM)
    shapes = (
        ((ROWS, COLS), BF16),
        ((ROWS, COLS), F32),
        ((FFN_PARTS, FFN_TILES, 64, FFN_WIDTH), F32),
        ((ATT_TILES, 64, ATT_WIDTH), F32),
        ((2, 4, 4, PACK, 128), BF16),
        ((16, 128), F32),
    )
    block = (ROWS, COLS)
    return pl.pallas_call(
        late_kernel,
        out_shape=tuple(jax.ShapeDtypeStruct(*shape) for shape in shapes),
        in_specs=[vmem] * 22 + [pl.BlockSpec(memory_space=pltpu.SMEM)] + [anywhere] * 12,
        out_specs=(vmem, vmem, anywhere, vmem, vmem, vmem),
        scratch_shapes=[
            pltpu.VMEM((12, COLS, COLS), BF16),
            pltpu.VMEM((ROWS, 2048), BF16),
            pltpu.SemaphoreType.DMA((25,)),
            pltpu.VMEM((3, *block), BF16),
            pltpu.VMEM((3, *block), BF16),
            pltpu.VMEM((3, *block), BF16),
            pltpu.VMEM((8, ROWS), F32),
            pltpu.VMEM((3, 8, ROWS), F32),
            pltpu.VMEM((4, *block), BF16),
            pltpu.VMEM(block, F32),
            pltpu.VMEM(block, F32),
            pltpu.SemaphoreType.DMA((2, 18)),
            pltpu.VMEM((2, 4, 4, 64, 512), BF16),
            pltpu.VMEM((FFN_TILES, FFN_PARTS, 512, FFN_WIDTH), BF16),
            pltpu.VMEM((4, 4, 64, ROWS), BF16),
            pltpu.SemaphoreType.DMA((2, 2 + FFN_TILES)),
            pltpu.VMEM((2, 4, 4, 64, 512), BF16),
            pltpu.VMEM((ATT_TILES, 512, ATT_WIDTH), BF16),
            pltpu.SemaphoreType.DMA((2, 2 + ATT_TILES)),
            pltpu.VMEM((3, 4, 4, PACK, 128), F32),
            pltpu.SemaphoreType.DMA((2,)),
            pltpu.VMEM((ROWS, SPAN), F32),
            pltpu.VMEM((HEADS, ROWS, DIM), BF16),
            pltpu.VMEM((HEADS, ROWS, 128), F32),
            pltpu.VMEM((2 * KEY_HEADS, SPAN, 128), F32),
            pltpu.VMEM((HEADS, ROWS, 128), F32),
            pltpu.VMEM((KEY_HEADS, SPAN, 128), F32),
            pltpu.VMEM((HEADS, DIM, DIM), F32),
            pltpu.VMEM((KEY_HEADS, DIM, DIM), F32),
            pltpu.VMEM((KEY_HEADS, WINDOW, 256), F32),
            pltpu.VMEM((KEY_HEADS, WINDOW, 256), F32),
            pltpu.VMEM((KEY_HEADS, STATE, 128), F32),
            pltpu.SemaphoreType.DMA((4,)),
            pltpu.VMEM((ROWS, 24), F32),
            pltpu.VMEM((ROWS, 256), BF16),
            pltpu.VMEM((24, 2048), F32),
            pltpu.VMEM((8, COLS), F32),
            pltpu.VMEM((8, 2048), F32),
            pltpu.VMEM((24, 2048), BF16),
            pltpu.VMEM((4, *block), F32),
            pltpu.VMEM((1, 2048), F32),
            pltpu.VMEM((4, 128), F32),
            pltpu.VMEM((3, 4, PACK, 128), BF16),
            pltpu.VMEM((3, 4, PACK, 128), BF16),
            pltpu.VMEM((4, 4, PACK, 128), BF16),
            pltpu.VMEM((4, 4, 16, 128), F32),
            pltpu.SemaphoreType.DMA((2, 13)),
            pltpu.VMEM((2, FFN_PARTS, 64, FFN_WIDTH), F32),
            pltpu.SemaphoreType.DMA((2,)),
            pltpu.VMEM((2, 16, 128), F32),
            pltpu.VMEM((4, 16, 128), F32),
            pltpu.VMEM((4, 16, 128), F32),
            pltpu.VMEM((4, 16, 128), F32),
            pltpu.SemaphoreType.DMA((2, 10)),
            *Scan.scratch((KEY_HEADS, STATE, 128)),
            *Ring.scratch(FFN_TILES, FFN_PARTS, 64, FFN_WIDTH),
            *Ring.scratch(ATT_TILES, 1, 64, ATT_WIDTH),
        ],
        compiler_params=pltpu.CompilerParams(
            collective_id=2, has_side_effects=True, vmem_limit_bytes=63 * 2**20 + 2**19
        ),
        name="late",
    )(*args, *weights)


def finish_kernel(
    block, inputs, ffn_sums, att_sums, packed, gains,
    block_out, inputs_out, gain_one, w_q, a_q, b_q, w_k, a_k, b_k, w_v, a_v, b_v, f_q, f_k, w_o, a_o, b_o, gain_two,
    w_gate, w_up, w_down,
):
    block_out[...] = block[...]
    pack = packed[...].astype(F32)
    inputs_out[...] = inputs[...]
    for i in range(4):
        cut = slice(i * FFN_WIDTH, (i + 1) * FFN_WIDTH)
        w_gate[:, cut] = ffn_sums[0, i]
        w_up[:, cut] = ffn_sums[1, i]
        w_down[:, cut] = ffn_sums[2, i]
    for i in range(2):
        cut = slice(i * ATT_WIDTH, (i + 1) * ATT_WIDTH)
        w_q[:, cut] = att_sums[i]
        w_o[:, cut] = att_sums[3 + i]
    w_k[...] = att_sums[2, :, :128]
    w_v[...] = att_sums[2, :, 128:]
    for i in range(16):
        cut = slice(i * 128, (i + 1) * 128)
        rows = jnp.concatenate([pack[2 * i, :12], pack[2 * i + 1, :12]], axis=0)
        a_q[:, cut] = rows[:8]
        a_k[:, cut] = rows[8:16]
        a_v[:, cut] = rows[16:]
        last = 16 + 2 * (i % 8)
        b_o[:, cut] = jnp.concatenate(
            [pack[2 * i, 13:16], pack[2 * i + 1, 13:16], pack[26 + i // 8, last : last + 2]], axis=0
        )

    def tile(i):
        return pack[20 + i // 2, 16 + 8 * (i % 2) : 24 + 8 * (i % 2)]

    for i in range(4):
        cut = slice(i * 128, (i + 1) * 128)
        for part in range(4):
            rows = pack[4 * i + part, 16:]
            f_q[2 * i, 16 * part : 16 * part + 16] = rows[:, :DIM]
            f_q[2 * i + 1, 16 * part : 16 * part + 16] = rows[:, DIM:]
        rows = pack[16 + i, 16:]
        f_k[0, 16 * i : 16 * i + 16] = rows[:, :DIM]
        f_k[1, 16 * i : 16 * i + 16] = rows[:, DIM:]
        b_q[:, cut] = tile(i)
        a_o[:, cut] = tile(6 + i)
        gain_two[:, cut] = pack[25, 16 + i : 17 + i]
        gain_one[:, cut] = gains[pl.ds(4 * lax.axis_index("head") + i, 1), :]
    b_k[...] = tile(4)
    b_v[...] = tile(5)


def finish(block, inputs, ffn_sums, att_sums, pack, gains):
    vmem = pl.BlockSpec(memory_space=pltpu.VMEM)
    shapes = (
        (ROWS, COLS), (ROWS, COLS), (1, COLS), (64, COLS), (8, 2048), (8, COLS), (64, 128), (8, 2048), (8, 128),
        (64, 128), (8, 2048), (8, 128), (HEADS, DIM, DIM), (KEY_HEADS, DIM, DIM), (64, COLS), (8, COLS), (8, 2048),
        (1, COLS), (64, 2048), (64, 2048), (64, 2048),
    )
    outs = pl.pallas_call(
        finish_kernel,
        out_shape=tuple(jax.ShapeDtypeStruct(shape, F32 if i else BF16) for i, shape in enumerate(shapes)),
        in_specs=[vmem] * 6,
        out_specs=(vmem,) * len(shapes),
        compiler_params=pltpu.CompilerParams(vmem_limit_bytes=32 * 2**20),
        name="finish",
    )(block, inputs, ffn_sums, att_sums, pack.reshape(32, 32, 128), gains)
    return tuple(
        out[0] if i in (2, 17) else out.T if i in (4, 7, 10, 14, 15, 20) else out for i, out in enumerate(outs)
    )


def body(
    inputs,
    gain_first,
    w_query,
    a_query,
    b_query,
    key_projection_weight,
    a_key,
    key_adapter_second,
    value_projection_weight,
    a_value,
    value_adapter_second,
    feature_query,
    key_hedgehog_map,
    w_out,
    a_out,
    b_out,
    gain_second,
    w_gate,
    w_up,
    w_down,
    lengths,
    cotangent,
):
    gain_one, gain_two = gain_first[None], gain_second[None]
    a_in = (a_query.T, a_key.T, a_value.T)
    a_out = a_out.T
    projections = (w_query, key_projection_weight, value_projection_weight, w_out)
    normed, low, queries, kv, state, att, stat, mixed, low_mix, hidden_in, g, scales, xt = front(
        inputs, gain_one, gain_two, *a_in, b_query, key_adapter_second, value_adapter_second,
        feature_query, key_hedgehog_map, a_out, b_out, lengths, *projections, cotangent,
    )
    block_out, grad_inputs, out_ffn, out_att, out_pack, out_gain = late(
        (
            hidden_in, scales, gain_one, gain_two, mixed, low_mix, att, stat, state, queries, kv, low,
            feature_query, key_hedgehog_map, *a_in, a_out, b_out, b_query, key_adapter_second,
            value_adapter_second, lengths,
        ),
        (g, normed, inputs, cotangent, xt, *projections, w_gate, w_up, w_down),
    )
    return finish(block_out, grad_inputs, out_ffn, out_att, out_pack, out_gain)


def solution(mesh):
    return jax.shard_map(
        body,
        mesh=mesh,
        in_specs=(
            P("seq", None),
            P(),
            P(None, "head"),
            P(),
            P(None, "head"),
            P(None, "head"),
            P(),
            P(None, "head"),
            P(None, "head"),
            P(),
            P(None, "head"),
            P("head", None, None),
            P("head", None, None),
            P("head", None),
            P("head", None),
            P(),
            P(),
            P(None, "head"),
            P(None, "head"),
            P("head", None),
            P(),
            P("seq", None),
        ),
        out_specs=(
            P("seq", "head"),
            P("seq", "head"),
            P("head"),
            P("seq", "head"),
            P(),
            P(None, "head"),
            P("seq", "head"),
            P(),
            P(None, "head"),
            P("seq", "head"),
            P(),
            P(None, "head"),
            P("head", None, None),
            P("head", None, None),
            P("head", "seq"),
            P("head", None),
            P(),
            P("head"),
            P("seq", "head"),
            P("seq", "head"),
            P("head", "seq"),
        ),
        check_vma=False,
    )
```

time: 205 us -> 193 us (0.941)
  Pallas kernels: 199 us -> 186 us
    pallas_call x2 -> x1, Pallas kernels: 139 us -> 126 us  [late(): pl.pallas_call(late_kernel, out_shape=tuple((jax.ShapeDtypeStruct(*shape)...]
    unnamed x10 -> x12, local copies, waits for them, and re-layouts: 5.31 us -> 6.01 us
where the time goes in v4:
time: 193 us
  Pallas kernels  186 us (96%)
  local copies, waits for them, and re-layouts  6.01 us (3%)
    pallas_call x1, Pallas kernels, late(): pl.pallas_call(late_kernel, out_shape=tuple((jax.ShapeDtypeStruct(*shape)...  126 us
    pallas_call x1, Pallas kernels, front(): pl.pallas_call(front_kernel, out_shape=tuple((jax.ShapeDtypeStruct(*shape...  58.3 us
    unnamed x12, local copies, waits for them, and re-layouts  6.01 us

profile of v4, /device:TPU:1, one launch (start us, length us, event | category | flops | bytes accessed | tf_op | source)
XLA Modules:
  0.0 192.8 jit_solution(3833361460784469117)
XLA Ops:
  0.7 58.3 %front.1 = (bf16[256,2048]{1,0:T(8,128)(2,1)}, bf16[256,24]{1,0:T(8,128)(2,1)}, bf16[8,256,64]{2,1,0:T(8,128)(2,1)}, bf16[2,320,128]{2,1,0:T(8,128)(2,1)}, f32[2...) custom-call(bf16[256,2048]{1,0:T(8,128)(2,1)} %x_hbm.1, ...), custom_call_target="tpu_custom_call" | custom-call | tf_op jit(solution)/shard_map/front/pallas_call | solution.py:500
  58.9 126.1 %late.1 = (bf16[256,512]{1,0:T(8,128)(2,1)}, f32[256,512]{1,0:T(8,128)}, f32[3,4,64,512]{3,2,1,0:T(8,128)}, f32[5,64,256]{2,1,0:T(8,128)}, bf16[2,4,4,32,128]{4,3,2,1,0:T(8,128)(2,1)}, /*index=5*/f32[16,128]{1,0:T(8,128)}) custom-call(f32[256,512]{1,0:T(8,128)} %get-tuple-element.61.hidden_in, f32[256,2]{1,0:T(8,128)} %get-tuple-element.62.scales, ...), custom_call_target="tpu_custom_call" | custom-call | tf_op jit(solution)/shard_map/late/pallas_call | solution.py:1140
  185.0 0.0 copy-start
  185.0 1.4 copy-done
  186.4 0.0 copy-start.1
  186.4 1.0 copy-done.1
  187.5 0.0 copy-start.2
  187.5 1.0 copy-done.2
  188.4 0.0 copy-start.3
  188.4 0.9 copy-done.3
  189.4 0.0 copy-start.4
  189.4 0.9 copy-done.4
  190.3 0.0 copy-start.5
  190.3 0.7 copy-done.5
  191.0 1.8 finish.1
Async XLA Ops:
  185.0 1.4 copy-start
  186.4 1.0 copy-start.1
  187.5 1.0 copy-start.2
  188.4 0.9 copy-start.3
  189.4 0.9 copy-start.4
  190.3 0.7 copy-start.5

commit v5 on v4

--- a/solution.py
+++ b/solution.py
@@ -28,7 +28,10 @@
     barrier = pltpu.get_barrier_semaphore()
     for partner in partners:
         pl.semaphore_signal(barrier, inc=1, device_id=partner, device_id_type=MESH)
-    pl.semaphore_wait(barrier, len(partners))
+
+
+def greeted(partners):
+    pl.semaphore_wait(pltpu.get_barrier_semaphore(), len(partners))
 
 
 def send(src, dst, ss, rs, device):
@@ -114,31 +117,31 @@
     def start(self, t, k):
         p = self.axes[k][0]
         h = 2 * self.rows
-
-        def far(i):
-            self.sb[t, 0, i] = self.term(t, i, k, turned(p, 2), 0, 4).astype(BF16)
-
-        def near(i):
-            self.sb[t, 1, i, h:] = self.term(t, i, k, turned(p, 1), 2, 4).astype(BF16)
-            self.sb[t, 1, i, :h] = self.term(t, i, k, turned(p, 3), 0, 2).astype(BF16)
-
-        self.each(far)
-        self.copy(t, k, 0).start()
-        self.copy(t, k, 1).start()
-        self.each(near)
-        self.copy(t, k, 2).start()
-        self.copy(t, k, 3).start()
+        pieces = ((turned(p, 2), 0, 4), (turned(p, 3), 0, 2), (turned(p, 1), 2, 4))
+
+        def one(i):
+            value = self.term(t, i, k, *pieces).astype(BF16)
+            self.sb[t, 0, i] = value[: 2 * h]
+            self.sb[t, 1, i] = value[2 * h :]
+
+        self.each(one)
+        for i in range(4):
+            self.copy(t, k, i).start()
 
     def merge(self, t, k):
         p = self.axes[k][0]
-        for way, dest, first in ((0, turned(p, 1), 0), (1, turned(p, 3), 2)):
+        h = 2 * self.rows
+        for way in range(2):
             self.arrived(t, way)
 
-            def one(i):
-                mine = self.term(t, i, k, dest, first, first + 2)
-                self.ra[t, way, i] = (mine + self.ra[t, way, i].astype(F32)).astype(BF16)
-
-            self.each(one)
+        def one(i):
+            mine = self.term(t, i, k, (turned(p, 1), 0, 2), (turned(p, 3), 2, 4))
+            for way in range(2):
+                part = mine[way * h : (way + 1) * h]
+                self.ra[t, way, i] = (part + self.ra[t, way, i].astype(F32)).astype(BF16)
+
+        self.each(one)
+        for way in range(2):
             self.copy(t, k, 4 + way).start()
 
     def cross(self, t, k):
@@ -147,7 +150,7 @@
         self.arrived(t, 2)
 
         def one(i):
-            own = self.term(t, i, k, p, 0, 4)
+            own = self.term(t, i, k, (p, 0, 4))
             self.sb[t, 0, i] = (own + self.rf[t, 0, i].astype(F32) + self.rf[t, 1, i].astype(F32)).astype(BF16)
 
         self.each(one)
@@ -181,7 +184,83 @@
             self.sent(t, group)
 
 
-FFN_TILES, FFN_PARTS, FFN_WIDTH = 4, 3, 512
+LO, HI = pl.ds(0, 128), pl.ds(128, 128)
+
+
+class Line:
+    def __init__(self, part, came, sems, base):
+        z, x, c, y = spot()
+        ahead, behind = at(z, x, c, turned(y, 1)), at(z, x, c, turned(y, 3))
+        self.part, self.came = part, came
+        ways = (
+            (part.at[1, LO], came.at[2, LO], ahead),
+            (part.at[1, HI], came.at[2, HI], behind),
+            (part.at[0, HI], came.at[0, HI], ahead),
+            (part.at[2, LO], came.at[1, LO], behind),
+            (came.at[2, LO], came.at[0, LO], ahead),
+            (came.at[2, HI], came.at[1, HI], behind),
+        )
+        self.copies = [send(src, dst, sems.at[0, base + i], sems.at[1, base + i], to) for i, (src, dst, to) in enumerate(ways)]
+
+    def start(self, *which):
+        for i in which:
+            self.copies[i].start()
+
+    def merge(self):
+        for i, piece, rows in ((0, 0, LO), (1, 2, HI)):
+            self.copies[i].wait_recv()
+            self.came[2, rows] = (self.came[2, rows].astype(F32) + self.part[piece, rows].astype(F32)).astype(BF16)
+            self.copies[4 + i].start()
+
+    def total(self, own):
+        for copy in self.copies[2:]:
+            copy.wait_recv()
+        for copy in self.copies:
+            copy.wait_send()
+        return own + self.came[0].astype(F32) + self.came[1].astype(F32)
+
+
+class Share:
+    def __init__(self, ref, sems, base):
+        z, x, c, y = spot()
+        ahead, behind = at(z, x, c, turned(y, 1)), at(z, x, c, turned(y, 3))
+        next_y, last_y, far_y = turned(y, 1), turned(y, 3), turned(y, 2)
+        out = (
+            (ref.at[y, LO], ahead),
+            (ref.at[y, HI], behind),
+            (ref.at[y, HI], ahead),
+            (ref.at[y, LO], behind),
+            (ref.at[last_y, LO], ahead),
+            (ref.at[next_y, HI], behind),
+        )
+        into = (
+            ref.at[last_y, LO],
+            ref.at[next_y, HI],
+            ref.at[last_y, HI],
+            ref.at[next_y, LO],
+            ref.at[far_y, LO],
+            ref.at[far_y, HI],
+        )
+        self.copies = [send(src, src, sems.at[0, base + i], sems.at[1, base + i], to) for i, (src, to) in enumerate(out)]
+        self.arrivals = [send(dst, dst, sems.at[0, base + i], sems.at[1, base + i], ahead) for i, dst in enumerate(into)]
+
+    def start(self):
+        for copy in self.copies[:4]:
+            copy.start()
+
+    def pass_on(self):
+        for i in range(2):
+            self.arrivals[i].wait_recv()
+            self.copies[4 + i].start()
+
+    def finish(self):
+        for arrival in self.arrivals[2:]:
+            arrival.wait_recv()
+        for copy in self.copies:
+            copy.wait_send()
+
+
+FFN_TILES, FFN_PARTS, FFN_WIDTH, FFN_HALF = 4, 3, 512, 256
 ATT_TILES, ATT_WIDTH = 5, 256
 PACK = 32
 
@@ -226,7 +305,7 @@
     grown = jnp.exp(both - jnp.where(left, upper, lower))
     sum_left = jnp.sum(jnp.where(left, grown, 0.0), axis=1, keepdims=True)
     sum_right = jnp.sum(jnp.where(left, 0.0, grown), axis=1, keepdims=True)
-    return grown / jnp.where(left, sum_left, sum_right)
+    return grown * jnp.where(left, 1.0 / sum_left, 1.0 / sum_right)
 
 
 def doc_at(positions, lengths):
@@ -331,7 +410,8 @@
     following, leading = (lax.rem(s + 1, 32), y), (lax.rem(s + 31, 32), y)
     y_mates = [at(z, x, c, turned(y, i)) for i in (1, 2, 3)]
     scan = Scan(scan_refs, False)
-    greet([following, leading, scan.sibling] + scan.x_mates + scan.z_mates + y_mates)
+    partners = [following, leading, scan.sibling] + scan.x_mates + scan.z_mates + y_mates
+    greet(partners)
     loads = [
         pltpu.make_async_copy(src, dst, w_sem.at[i])
         for i, (src, dst) in enumerate(((w_q, wq), (w_k, wk), (w_v, wv), (w_o, wo), (cot_hbm, cot)))
@@ -357,6 +437,7 @@
     tail = send(
         kv_out.at[:, pl.ds(ROWS, WINDOW)], kv_out.at[:, pl.ds(0, WINDOW)], tail_sem.at[0], tail_sem.at[1], following
     )
+    greeted(partners)
     tail.start()
     loads[0].wait()
     for i in range(2):
@@ -421,7 +502,7 @@
         stat[h, :, 1:2] = total
         stat[h, :, 2:3] = gate
         cut = slice(h * DIM, (h + 1) * DIM)
-        attended = (num[h] + gate * carried[:, :DIM]) / total
+        attended = (num[h] + gate * carried[:, :DIM]) * (1.0 / total)
         att_out[:, cut] = attended
         mixed_out[:, cut] = attended.astype(BF16)
         stat_out[h] = stat[h].T
@@ -435,10 +516,10 @@
     def columns(ref, d):
         return ref[:, pl.ds(pl.multiple_of(d * COLS, COLS), COLS)]
 
-    turns = [send(part.at[i], came.at[i], y_sem.at[0, 3 + i], y_sem.at[1, 3 + i], y_mates[i]) for i in range(3)]
-    for i in (1, 0, 2):
+    line = Line(part, came, y_sem, 3)
+    for i, which in ((1, (0, 1)), (0, (2,)), (2, (3,))):
         part[i] = mm(mixed, columns(wo, turned(y, 1 + i))).astype(BF16)
-        turns[i].start()
+        line.start(*which)
     value = mm(mixed, columns(wo, y)) + columns(x_ref, y).astype(F32)
 
     def by_owner(m, rows):
@@ -454,29 +535,26 @@
     low_sum = low_part[0] + low_part[1] + low_part[2] + low_part[3]
     lowmix_out[...] = low_sum.T.astype(BF16)
     value = value + mm(lowmix_out[...], columns(b_out, y))
-    for turn in turns:
-        turn.wait()
-    value = value + came[0].astype(F32) + came[1].astype(F32) + came[2].astype(F32)
+    line.merge()
+    loads[4].wait()
+    by_owner(1, cot)
+    value = line.total(value)
     hidden_out[...] = value
     g_out[y] = (value * columns(gain_two, y)).astype(BF16)
-    turns = [send(g_out.at[y], g_out.at[y], y_sem.at[0, 9 + i], y_sem.at[1, 9 + i], y_mates[i]) for i in range(3)]
+    share = Share(g_out, y_sem, 12)
     square[...] = mm_nt(jnp.ones((8, COLS), F32), value * value, HIGH)
     square_turns = [
-        send(square, square_came.at[i], y_sem.at[0, 6 + i], y_sem.at[1, 6 + i], y_mates[i]) for i in range(3)
+        send(square, square_came.at[i], y_sem.at[0, 9 + i], y_sem.at[1, 9 + i], y_mates[i]) for i in range(3)
     ]
-    for turn in square_turns + turns:
+    for turn in square_turns:
         turn.start()
-    loads[4].wait()
-    by_owner(1, cot)
+    share.start()
     for turn in square_turns:
         turn.wait()
     mean = (square[...] + square_came[0] + square_came[1] + square_came[2]) * (1.0 / 2048)
     scales_out[:, 1:2] = lax.rsqrt(mean + EPS).T[:, 0:1]
-    for i in range(3):
-        here = g_out.at[turned(y, 3 - i)]
-        send(here, here, y_sem.at[0, 9 + i], y_sem.at[1, 9 + i], y_mates[i]).wait_recv()
-    for turn in turns:
-        turn.wait_send()
+    share.pass_on()
+    share.finish()
 
 
 def front(*args):
@@ -519,7 +597,7 @@
             pltpu.SemaphoreType.DMA((4,)),
             pltpu.VMEM((3, ROWS, COLS), BF16),
             pltpu.VMEM((3, ROWS, COLS), BF16),
-            pltpu.SemaphoreType.DMA((2, 12)),
+            pltpu.SemaphoreType.DMA((2, 18)),
             pltpu.VMEM((4, 8, ROWS), F32),
             pltpu.VMEM((8, ROWS), F32),
             pltpu.VMEM((3, 8, ROWS), F32),
@@ -560,7 +638,8 @@
     following, leading = (lax.rem(s + 1, 32), y), (lax.rem(s + 31, 32), y)
     y_mates = [at(z, x, c, turned(y, i)) for i in (1, 2, 3)]
     sibling = scan.sibling
-    greet([following, leading, sibling] + scan.x_mates + scan.z_mates + y_mates)
+    partners = [following, leading, sibling] + scan.x_mates + scan.z_mates + y_mates
+    greet(partners)
 
     def columns(ref, d):
         return ref[:, pl.ds(pl.multiple_of(d * COLS, COLS), COLS)]
@@ -576,7 +655,7 @@
         return pltpu.make_async_copy(src, dst, w_sem.at[i])
 
     def turn_at(n):
-        return turned(y, 1 + n)
+        return turned(y, (2, 1, 3, 0)[n])
 
     def part(n):
         return pl.ds(pl.multiple_of(n * COLS, COLS), COLS)
@@ -648,41 +727,51 @@
             xd[m, i // 4, i % 4, :, 0:ROWS] = jnp.where(c == 0, block[:64], block[64:])
             xs[i // 4, i % 4] = jnp.where(c == 0, block[64:], block[:64])
 
-    for copy in left_cot:
-        copy.start()
     load_g.wait()
     by_owner(0, xf)
-    left_g.start()
+    greeted(partners)
+    for copy in left_cot + [left_g]:
+        copy.start()
 
     def product(xd, right):
-        def term(t, i, k, dest, first, last):
-            m, yd = right(t, i)
-            rows = xd[m, first:last, dest] if k == 0 else xd[m, dest, first:last]
-            return mm(rows.reshape((last - first) * 64, 2 * ROWS), yd)
+        def term(t, i, k, *pieces):
+            m, yd = right(t, i, k)
+            rows = []
+            for dest, first, last in pieces:
+                piece = xd[m, first:last, dest] if k == 0 else xd[m, dest, first:last]
+                rows.append(piece.reshape((last - first) * 64, 2 * ROWS))
+            return mm(jnp.concatenate(rows, axis=0), yd)
 
         return term
 
+    def half_of(k):
+        return slice(k * FFN_HALF, (k + 1) * FFN_HALF)
+
     def finish_ffn(t, i, k, value):
-        stage[k, i] = value
-
-    def write_ffn(t, k):
-        return pltpu.make_async_copy(stage.at[k], out_ffn.at[:, t], sem_stage.at[k])
-
-    def close_ffn(t):
-        if t >= 2:
-            write_ffn(t - 2, t % 2).wait()
-        big.end(t, t % 2)
-        write_ffn(t, t % 2).start()
+        stage[t // 2 % 2, i, :, half_of(k)] = value
+
+    def write_ffn(u):
+        return pltpu.make_async_copy(stage.at[u % 2], out_ffn.at[:, u], sem_stage.at[u % 2])
+
+    def sides(step, u):
+        step(2 * u, 0)
+        step(2 * u + 1, 1)
+
+    def close_ffn(u):
+        if u >= 2:
+            write_ffn(u - 2).wait()
+        sides(big.end, u)
+        write_ffn(u).start()
 
     def finish_att(t, i, k, value):
         out_att[t] = value
 
-    big = Ring(refs_big, 64, FFN_PARTS, product(xf, lambda t, i: (lax.div(i, 2), yf[t, i])), finish_ffn)
-    mid = Ring(refs_mid, 64, 1, product(xa, lambda t, i: (t // 3, ya[t])), finish_att)
+    big = Ring(refs_big, 64, FFN_PARTS, product(xf, lambda t, i, k: (lax.div(i, 2), yf[t // 2, i, :, half_of(k)])), finish_ffn)
+    mid = Ring(refs_mid, 64, 1, product(xa, lambda t, i, k: (t // 3, ya[t])), finish_att)
 
     def begin(u):
         right_ffn(u).wait()
-        big.start(u, u % 2)
+        sides(big.start, u)
 
     def feed(u, carry):
         def through(first_slot, term):
@@ -724,9 +813,13 @@
             left_g.wait()
             begin(0)
 
+        @pl.when(u == 2)
+        def _():
+            begin(1)
+
         @pl.when(u == 3)
         def _():
-            begin(1)
+            begin(2)
 
         return carry
 
@@ -734,7 +827,7 @@
     for copy in left_att:
         copy.start()
     inverse = 1.0 / scales[:, 1:2]
-    gs_turns = to_mates(0, lambda i: gf_part.at[i], gs_came)
+    gs_line = Line(gf_part, gs_came, y_sem, 0)
     dot = jnp.zeros((ROWS, 1), F32)
     for n in range(4):
         value = jnp.zeros((ROWS, COLS), F32)
@@ -745,19 +838,21 @@
         value = value * inverse
         dot = dot + jnp.sum(value * gb[turn_at(n)].astype(F32), axis=1, keepdims=True)
         if n < 3:
-            gf_part[n] = value.astype(BF16)
-            gs_turns[n].start()
+            gf_part[(1, 0, 2)[n]] = value.astype(BF16)
+            gs_line.start(*((0, 1), (2,), (3,))[n])
         else:
             gsum[...] = value
     dot_part[...] = jnp.broadcast_to(dot, (ROWS, 128)).T[:8]
-    gs_dots = to_mates(3, lambda i: dot_part, dot_came)
+    gs_dots = to_mates(6, lambda i: dot_part, dot_came)
     for turn in gs_dots:
         turn.start()
-    begin(2)
-
-    for turn in gs_turns + gs_dots:
+    gs_line.merge()
+    begin(3)
+    sides(big.merge, 0)
+
+    for turn in gs_dots:
         turn.wait()
-    total = gsum[...] + gs_came[0].astype(F32) + gs_came[1].astype(F32) + gs_came[2].astype(F32)
+    total = gs_line.total(gsum[...])
     gsum[...] = total
     gain_rows = jnp.sum(total * hidden_in[...] * scales[:, 1:2], axis=0, keepdims=True)
     gain_rows_ref[...] = jnp.concatenate([gain_rows[:, i * 128 : (i + 1) * 128] for i in range(4)])
@@ -773,14 +868,11 @@
     )
     gres[...] = residual
     gb[y] = residual.astype(BF16)
-    gb_turns = [
-        send(gb.at[y], gb.at[y], y_sem.at[0, 6 + i], y_sem.at[1, 6 + i], y_mates[i]) for i in range(3)
-    ]
-    for turn in gb_turns:
-        turn.start()
+    gb_share = Share(gb, y_sem, 9)
+    gb_share.start()
     load_x.start()
 
-    ffn_turns = to_mates(9, lambda i: gf_part.at[i], ffn_came)
+    ffn_turns = to_mates(15, lambda i: gf_part.at[i], ffn_came)
     for n in range(4):
         value = jnp.zeros((ROWS, COLS), F32)
         for b in range(32 + 4 * n, 36 + 4 * n):
@@ -788,11 +880,11 @@
             value = value + mm(yf[b % 4, 2, 0:ROWS], wb[b % 12])
             load_later(b + 12)
         if n < 3:
-            gf_part[n] = value.astype(BF16)
-            ffn_turns[n].start()
+            gf_part[(1, 0, 2)[n]] = value.astype(BF16)
         else:
             out_inputs[...] = value
-    begin(3)
+    gb_share.pass_on()
+    sides(big.merge, 1)
     write_mask(mask, lengths)
     def features(h, carry):
         pq[h] = soft_pair(qh[h], f_q[h])
@@ -804,11 +896,11 @@
         pkey[KEY_HEADS + j] = jnp.zeros((SPAN, 128), F32)
     dkv[...] = jnp.zeros(dkv.shape, F32)
     pk[...] = jnp.zeros(pk.shape, F32)
-    big.merge(0, 0)
-
-    for i in range(3):
-        here = gb.at[turned(y, 3 - i)]
-        send(here, here, y_sem.at[0, 6 + i], y_sem.at[1, 6 + i], y_mates[i]).wait_recv()
+    sides(big.merge, 2)
+
+    gb_share.finish()
+    for turn in ffn_turns:
+        turn.start()
     for slot in range(4):
         held(slot)
     grad_low = jnp.zeros((ROWS, 8), F32)
@@ -833,9 +925,9 @@
         j = h // 4
         grad = gh[h].astype(F32)
         column = stat[h].T
-        den = column[:, 1:2]
-        inner = -jnp.sum(grad * att[:, h * DIM : (h + 1) * DIM], axis=1, keepdims=True) / den
-        ext = jnp.concatenate([grad / den, jnp.where(lane == 0, inner, 0.0)], axis=1)
+        inverse = 1.0 / column[:, 1:2]
+        inner = -jnp.sum(grad * att[:, h * DIM : (h + 1) * DIM], axis=1, keepdims=True) * inverse
+        ext = jnp.concatenate([grad * inverse, jnp.where(lane == 0, inner, 0.0)], axis=1)
         dext[h] = ext
         top, bottom = halves(ext * column[:, 2:3])
         phi = pq[h].astype(BF16)
@@ -844,8 +936,6 @@
     scan.open()
 
     by_owner(1, xa)
-    for turn in gb_turns:
-        turn.wait_send()
     for load in load_n:
         load.start()
     left_gb.start()
@@ -863,20 +953,20 @@
         keys, values = kv[j][:, :DIM], kv[j][:, DIM:]
         q, grad, ext = qh[h], gh[h], dext[h]
         column = stat[h].T
-        top, den, gate = column[:, 0:1], column[:, 1:2], column[:, 2:3]
+        top, inverse, gate = column[:, 0:1], 1.0 / column[:, 1:2], column[:, 2:3]
         distant = mask[...] == NEG
         soft = pq[h]
         phi, phi_key = soft.astype(BF16), pkey[j].astype(BF16)
         damping = jnp.where(distant, jnp.exp(-top), 0.0)
         weights = jnp.exp(mm_nt(q, keys) * (DIM**-0.5) + mask[...] - top)
-        grad_weights = mm_nt(grad, values) / den + ext[:, DIM : DIM + 1]
+        grad_weights = mm_nt(grad, values) * inverse + ext[:, DIM : DIM + 1]
         grad_scores = (weights * grad_weights).astype(BF16)
         grad_linear = (damping * grad_weights).astype(BF16)
         both = weights.astype(BF16).astype(F32) + mm_nt(phi, phi_key) * damping
-        high, rest = halves(both / den)
+        held_weights = (both * inverse).astype(BF16)
         grad_q = mm(grad_scores, keys) * (DIM**-0.5)
         grad_k = mm_tn(grad_scores, q) * (DIM**-0.5)
-        dkv[j] = dkv[j] + jnp.concatenate([grad_k, mm_tn(high, grad) + mm_tn(rest, grad)], axis=1)
+        dkv[j] = dkv[j] + jnp.concatenate([grad_k, mm_tn(held_weights, grad)], axis=1)
         pkey[KEY_HEADS + j] = pkey[KEY_HEADS + j] + mm_tn(grad_linear, phi)
         carried = jnp.dot(
             (ext * gate)[:, :STATE], state[j], precision=HIGH, preferred_element_type=F32
@@ -890,21 +980,21 @@
         def _():
             scan.along_z()
 
-        @pl.when(h == 0)
+        @pl.when(h == 2)
         def _():
-            big.merge(1, 1)
-
-        @pl.when(h == 4)
+            sides(big.cross, 0)
+
+        @pl.when(h == 3)
         def _():
-            big.merge(2, 0)
-
-        @pl.when(h == 6)
+            sides(big.merge, 3)
+
+        @pl.when(h == 5)
         def _():
-            big.cross(0, 0)
+            sides(big.cross, 1)
 
         @pl.when(h == 7)
         def _():
-            big.merge(3, 1)
+            sides(big.cross, 2)
 
         return carry
 
@@ -1017,7 +1107,7 @@
         + ffn_came[1].astype(F32)
         + ffn_came[2].astype(F32)
     ).astype(BF16)
-    gf_turns = to_mates(12, lambda i: gf_part.at[i], gs_came)
+    gf_line = Line(gf_part, gs_came, y_sem, 18)
 
     def partial_first(d, dot):
         rows = pl.ds(pl.multiple_of(d * COLS, COLS), COLS)
@@ -1044,7 +1134,7 @@
     for i in (1, 0):
         chunk, dot = partial_first(turned(y, 1 + i), dot)
         gf_part[i] = chunk.astype(BF16)
-        gf_turns[i].start()
+        gf_line.start(*((2,), (0, 1))[i])
 
     pack_far.wait()
     x_turns = [send(px.at[i], px_came.at[i], sem_zx.at[0, i], sem_zx.at[1, i], scan.x_mates[i]) for i in range(3)]
@@ -1054,11 +1144,11 @@
         x_turns[i].start()
     chunk, dot = partial_first(turned(y, 3), dot)
     gf_part[2] = chunk.astype(BF16)
-    gf_turns[2].start()
+    gf_line.start(3)
     chunk, dot = partial_first(y, dot)
     gsum[...] = chunk
     dot_part[...] = jnp.broadcast_to(dot, (ROWS, 128)).T[:8]
-    dot_turns = to_mates(15, lambda i: dot_part, dot_came)
+    dot_turns = to_mates(24, lambda i: dot_part, dot_came)
     for turn in dot_turns:
         turn.start()
     for i in range(16):
@@ -1067,6 +1157,7 @@
     own_pack = pk[c, :, x] + pk[2, :, x]
     right_att(2).wait()
     mid.start(2, 0)
+    gf_line.merge()
     settle(x_turns)
     own_pack = own_pack + px_came[0].astype(F32) + px_came[1].astype(F32) + px_came[2].astype(F32)
     pz[z] = own_pack.astype(BF16)
@@ -1083,7 +1174,7 @@
     settle(gain_turns)
     gain_z[z] = gain_x[0] + gain_x[1] + gain_x[2] + gain_x[3]
     gain_turns = spread(sem_gain, 4, gain_z.at[z], scan.z_mates, lambda i: gain_z.at[turned(z, 3 - i)])
-    big.cross(1, 1)
+    sides(big.cross, 3)
     mid.merge(2, 0)
     settle(y_turns)
     top = crown[0] + crown[1] + crown[2] + crown[3]
@@ -1092,11 +1183,13 @@
     settle(gain_turns)
     gain_y[y] = gain_z[0] + gain_z[1] + gain_z[2] + gain_z[3]
     gain_turns = spread(sem_gain, 7, gain_y.at[y], y_mates, lambda i: gain_y.at[turned(y, 3 - i)])
-    big.cross(2, 0)
     for t in (3, 4, 0, 1, 2):
         mid.cross(t, t % 2)
-    settle(gf_turns + dot_turns)
-    total = gsum[...] + gs_came[0].astype(F32) + gs_came[1].astype(F32) + gs_came[2].astype(F32)
+    sides(big.merge_cross, 0)
+    sides(big.merge_cross, 1)
+    sides(big.merge_cross, 2)
+    settle(dot_turns)
+    total = gf_line.total(gsum[...])
     scale = scales[:, 0:1]
     out_inputs[...] = (
         gres[...]
@@ -1107,20 +1200,18 @@
     last = spread(sem_zx, 9, out_pack.at[c], [sibling], lambda i: out_pack.at[1 - c])
     settle(gain_turns)
     out_gain[...] = gain_y[0] + gain_y[1] + gain_y[2] + gain_y[3]
-    big.cross(3, 1)
-    for t in range(FFN_TILES):
-        big.merge_cross(t, t % 2)
     for t in (3, 4, 0, 1, 2):
         mid.merge_cross(t, t % 2)
+    sides(big.merge_cross, 3)
     for t in range(FFN_TILES):
         close_ffn(t)
     for t in (3, 4, 0, 1, 2):
         mid.end(t, t % 2)
     settle(last)
-    for i in range(2):
-        write_ffn(FFN_TILES - 2 + i, i).wait()
-    for t in range(FFN_TILES):
-        big.drain(t, t % 2)
+    write_ffn(2).wait()
+    write_ffn(3).wait()
+    for u in range(FFN_TILES):
+        sides(big.drain, u)
     for t in range(ATT_TILES):
         mid.drain(t, t % 2)
 
@@ -1154,7 +1245,7 @@
             pltpu.VMEM((4, *block), BF16),
             pltpu.VMEM(block, F32),
             pltpu.VMEM(block, F32),
-            pltpu.SemaphoreType.DMA((2, 18)),
+            pltpu.SemaphoreType.DMA((2, 27)),
             pltpu.VMEM((2, 4, 4, 64, 512), BF16),
             pltpu.VMEM((FFN_TILES, FFN_PARTS, 512, FFN_WIDTH), BF16),
             pltpu.VMEM((4, 4, 64, ROWS), BF16),
@@ -1198,7 +1289,7 @@
             pltpu.VMEM((4, 16, 128), F32),
             pltpu.SemaphoreType.DMA((2, 10)),
             *Scan.scratch((KEY_HEADS, STATE, 128)),
-            *Ring.scratch(FFN_TILES, FFN_PARTS, 64, FFN_WIDTH),
+            *Ring.scratch(2 * FFN_TILES, FFN_PARTS, 64, FFN_HALF),
             *Ring.scratch(ATT_TILES, 1, 64, ATT_WIDTH),
         ],
         compiler_params=pltpu.CompilerParams(
@@ -1270,7 +1361,7 @@
         out_shape=tuple(jax.ShapeDtypeStruct(shape, F32 if i else BF16) for i, shape in enumerate(shapes)),
         in_specs=[vmem] * 6,
         out_specs=(vmem,) * len(shapes),
-        compiler_params=pltpu.CompilerParams(vmem_limit_bytes=32 * 2**20),
+        compiler_params=pltpu.CompilerParams(vmem_limit_bytes=63 * 2**20),
         name="finish",
     )(block, inputs, ffn_sums, att_sums, pack.reshape(32, 32, 128), gains)
     return tuple(

time: 193 us -> 177 us (0.917); the launches traced: 193 us -> 174 us
  Pallas kernels: 186 us -> 173 us
  local copies, waits for them, and re-layouts: 6.01 us -> 0 us
    pallas_call x1, Pallas kernels: 58.3 us -> 46.7 us  [front(): pl.pallas_call(front_kernel, out_shape=tuple((jax.ShapeDtypeStruct(*shape...]
    unnamed x12 -> x0, local copies, waits for them, and re-layouts: 6.01 us -> none
    pallas_call x1, Pallas kernels: 126 us -> 123 us  [late(): pl.pallas_call(late_kernel, out_shape=tuple((jax.ShapeDtypeStruct(*shape)...]
where the time goes in v5:
time: 177 us; the launch traced here: 174 us
  Pallas kernels  173 us (98%)
    pallas_call x1, Pallas kernels, late(): pl.pallas_call(late_kernel, out_shape=tuple((jax.ShapeDtypeStruct(*shape)...  123 us
    pallas_call x1, Pallas kernels, front(): pl.pallas_call(front_kernel, out_shape=tuple((jax.ShapeDtypeStruct(*shape...  46.7 us
    pallas_call x1, Pallas kernels, finish(): pl.pallas_call(finish_kernel, out_shape=tuple((jax.ShapeDtypeStruct(shape...  3.55 us

profile of v5, /device:TPU:1, one launch (start us, length us, event | category | flops | bytes accessed | tf_op | source)
XLA Modules:
  0.0 174.4 jit_solution(13468935166223068394)
XLA Ops:
  0.7 46.7 %front.1 = (bf16[256,2048]{1,0:T(8,128)(2,1)}, bf16[256,24]{1,0:T(8,128)(2,1)}, bf16[8,256,64]{2,1,0:T(8,128)(2,1)}, bf16[2,320,128]{2,1,0:T(8,128)(2,1)}, f32[2...) custom-call(bf16[256,2048]{1,0:T(8,128)(2,1)} %x_hbm.1, ...), custom_call_target="tpu_custom_call" | custom-call | tf_op jit(solution)/shard_map/front/pallas_call | solution.py:578
  47.4 123.1 %late.1 = (bf16[256,512]{1,0:T(8,128)(2,1)}, f32[256,512]{1,0:T(8,128)}, f32[3,4,64,512]{3,2,1,0:T(8,128)}, f32[5,64,256]{2,1,0:T(8,128)}, bf16[2,4,4,32,128]{4,3,2,1,0:T(8,128)(2,1)}, /*index=5*/f32[16,128]{1,0:T(8,128)}) custom-call(f32[256,512]{1,0:T(8,128)} %get-tuple-element.61.hidden_in, f32[256,2]{1,0:T(8,128)} %get-tuple-element.62.scales, ...), custom_call_target="tpu_custom_call" | custom-call | tf_op jit(solution)/shard_map/late/pallas_call | solution.py:1231
  170.5 3.6 %finish.1 = (bf16[256,512]{1,0:T(8,128)(2,1)}, f32[256,512]{1,0:T(8,128)}, f32[1,512]{1,0:T(1,128)}, f32[64,512]{1,0:T(8,128)}, f32[8,2048]{1,0:T(8,128)}, /*ind...) custom-call(bf16[256,512]{1,0:T(8,128)(2,1)} %get-tuple-element.74.b, ...), custom_call_target="tpu_custom_call" | custom-call | tf_op jit(solution)/shard_map/finish/pallas_call | solution.py:1359

commit v6 on v5

--- a/solution.py
+++ b/solution.py
@@ -457,13 +457,14 @@
     brief_turn.start()
     scan.open()
 
-    def features(h, carry):
-        phq[h] = soft_pair(qh[h], f_q[h]).astype(BF16)
+    def features(i, carry):
+        phq[i] = soft_pair(qh[i], f_q[i]).astype(BF16)
+        phq[i + 4] = soft_pair(qh[i + 4], f_q[i + 4]).astype(BF16)
         return carry
 
-    lax.fori_loop(0, 4, features, 0)
+    lax.fori_loop(0, 2, features, 0)
     scan.along_x()
-    lax.fori_loop(4, HEADS, features, 0)
+    lax.fori_loop(2, 4, features, 0)
     tail.wait()
     inside = middle(WINDOW, -WINDOW, lengths)
     for j in range(KEY_HEADS):
@@ -472,8 +473,7 @@
         brief[2, j] = mm_tn(value_columns(kv_out[j, :WINDOW]), counted)[:STATE]
     brief_turn.wait()
 
-    def inner(h, carry):
-        j = lax.div(h, 4)
+    def one_head(h, j):
         kv = kv_out[j]
         distant = mask[...] == NEG
         scores = mm_nt(qh[h], kv[:, :DIM]) * (DIM**-0.5) + mask[...]
@@ -486,11 +486,15 @@
         num[h] = mm(high, v) + mm(rest, v)
         stat[h, :, 0:1] = top
         stat[h, :, 1:2] = jnp.sum(total, axis=1, keepdims=True)
+
+    def inner(i, carry):
+        one_head(i, 0)
+        one_head(i + 4, 1)
         return carry
 
-    lax.fori_loop(0, 4, inner, 0)
+    lax.fori_loop(0, 2, inner, 0)
     scan.along_z()
-    lax.fori_loop(4, HEADS, inner, 0)
+    lax.fori_loop(2, 4, inner, 0)
     second = c.astype(F32)
     state_out[...] = scan.close(brief[1] * second - brief[2] * (1.0 - second))
     mine = middle(ROWS, 0, lengths)
@@ -886,11 +890,12 @@
     gb_share.pass_on()
     sides(big.merge, 1)
     write_mask(mask, lengths)
-    def features(h, carry):
-        pq[h] = soft_pair(qh[h], f_q[h])
+    def features(i, carry):
+        pq[i] = soft_pair(qh[i], f_q[i])
+        pq[i + 4] = soft_pair(qh[i + 4], f_q[i + 4])
         return carry
 
-    lax.fori_loop(0, HEADS, features, 0)
+    lax.fori_loop(0, 4, features, 0)
     for j in range(KEY_HEADS):
         pkey[j] = soft_pair(kv[j][:, :DIM], f_k[j])
         pkey[KEY_HEADS + j] = jnp.zeros((SPAN, 128), F32)
@@ -948,14 +953,13 @@
         right_att(t).wait()
         mid.start(t, t % 2)
 
-    def backward(h, carry):
-        j = lax.div(h, 4)
+    sides(big.merge, 3)
+
+    def one_head(h, j, q, grad, ext, row_stat, soft):
         keys, values = kv[j][:, :DIM], kv[j][:, DIM:]
-        q, grad, ext = qh[h], gh[h], dext[h]
-        column = stat[h].T
+        column = row_stat.T
         top, inverse, gate = column[:, 0:1], 1.0 / column[:, 1:2], column[:, 2:3]
         distant = mask[...] == NEG
-        soft = pq[h]
         phi, phi_key = soft.astype(BF16), pkey[j].astype(BF16)
         damping = jnp.where(distant, jnp.exp(-top), 0.0)
         weights = jnp.exp(mm_nt(q, keys) * (DIM**-0.5) + mask[...] - top)
@@ -966,39 +970,45 @@
         held_weights = (both * inverse).astype(BF16)
         grad_q = mm(grad_scores, keys) * (DIM**-0.5)
         grad_k = mm_tn(grad_scores, q) * (DIM**-0.5)
-        dkv[j] = dkv[j] + jnp.concatenate([grad_k, mm_tn(held_weights, grad)], axis=1)
-        pkey[KEY_HEADS + j] = pkey[KEY_HEADS + j] + mm_tn(grad_linear, phi)
+        grad_kv = jnp.concatenate([grad_k, mm_tn(held_weights, grad)], axis=1)
+        grad_phi_key = mm_tn(grad_linear, phi)
         carried = jnp.dot(
             (ext * gate)[:, :STATE], state[j], precision=HIGH, preferred_element_type=F32
         )
         grad_soft = mm(grad_linear, phi_key) + carried
         high, rest = halves(soft_back(soft, grad_soft))
-        gh[h] = (grad_q + mm_nt(high, f_q[h]) + mm_nt(rest, f_q[h])).astype(BF16)
-        gfq[h] = mm_tn(q, high) + mm_tn(q, rest)
-
-        @pl.when(h == 1)
+        grad_q = (grad_q + mm_nt(high, f_q[h]) + mm_nt(rest, f_q[h])).astype(BF16)
+        return grad_q, mm_tn(q, high) + mm_tn(q, rest), grad_kv, grad_phi_key
+
+    def backward(i, carry):
+        heads = (i, i + 4)
+        loaded = [(qh[h], gh[h], dext[h], stat[h], pq[h]) for h in heads]
+        results = [one_head(h, j, *loaded[j]) for j, h in enumerate(heads)]
+        for j, h in enumerate(heads):
+            gh[h], gfq[h] = results[j][:2]
+            dkv[j] = dkv[j] + results[j][2]
+            pkey[KEY_HEADS + j] = pkey[KEY_HEADS + j] + results[j][3]
+
+        @pl.when(i == 0)
         def _():
             scan.along_z()
-
-        @pl.when(h == 2)
-        def _():
             sides(big.cross, 0)
 
-        @pl.when(h == 3)
-        def _():
-            sides(big.merge, 3)
-
-        @pl.when(h == 5)
+        @pl.when(i == 1)
         def _():
             sides(big.cross, 1)
 
-        @pl.when(h == 7)
+        @pl.when(i == 2)
         def _():
             sides(big.cross, 2)
 
+        @pl.when(i == 3)
+        def _():
+            sides(big.cross, 3)
+
         return carry
 
-    lax.fori_loop(0, HEADS, backward, 0)
+    lax.fori_loop(0, 4, backward, 0)
 
     for j in range(KEY_HEADS):
         ret[j] = jnp.concatenate([dkv[j, :WINDOW], pkey[KEY_HEADS + j, :WINDOW]], axis=1)
@@ -1027,6 +1037,9 @@
         mid.start(t, t % 2)
     for k in range(4):
         first[k] = mm_nt(gq, wb[4 + k])
+
+    sides(big.merge_cross, 0)
+    sides(big.merge_cross, 1)
 
     inside = middle(ROWS, 0, lengths)
     suffix = scan.close(scan.pair[...] * (1.0 - c.astype(F32)))
@@ -1174,7 +1187,6 @@
     settle(gain_turns)
     gain_z[z] = gain_x[0] + gain_x[1] + gain_x[2] + gain_x[3]
     gain_turns = spread(sem_gain, 4, gain_z.at[z], scan.z_mates, lambda i: gain_z.at[turned(z, 3 - i)])
-    sides(big.cross, 3)
     mid.merge(2, 0)
     settle(y_turns)
     top = crown[0] + crown[1] + crown[2] + crown[3]
@@ -1185,8 +1197,6 @@
     gain_turns = spread(sem_gain, 7, gain_y.at[y], y_mates, lambda i: gain_y.at[turned(y, 3 - i)])
     for t in (3, 4, 0, 1, 2):
         mid.cross(t, t % 2)
-    sides(big.merge_cross, 0)
-    sides(big.merge_cross, 1)
     sides(big.merge_cross, 2)
     settle(dot_turns)
     total = gf_line.total(gsum[...])

time: 177 us -> 174 us (0.983)
  the two profiles are of different devices: /device:TPU:1 before, /device:TPU:0 now
where the time goes in v6:
time: 174 us; the launch traced here: 170 us
  Pallas kernels  169 us (97%)
    pallas_call x1, Pallas kernels, late(): pl.pallas_call(late_kernel, out_shape=tuple((jax.ShapeDtypeStruct(*shape)...  116 us
    pallas_call x1, Pallas kernels, front(): pl.pallas_call(front_kernel, out_shape=tuple((jax.ShapeDtypeStruct(*shape...  49.9 us
    pallas_call x1, Pallas kernels, finish(): pl.pallas_call(finish_kernel, out_shape=tuple((jax.ShapeDtypeStruct(shape...  3.55 us

profile of v6, /device:TPU:0, one launch (start us, length us, event | category | flops | bytes accessed | tf_op | source)
XLA Modules:
  0.0 170.4 jit_solution(16846011634953824585)
XLA Ops:
  0.7 49.9 %front.1 = (bf16[256,2048]{1,0:T(8,128)(2,1)}, bf16[256,24]{1,0:T(8,128)(2,1)}, bf16[8,256,64]{2,1,0:T(8,128)(2,1)}, bf16[2,320,128]{2,1,0:T(8,128)(2,1)}, f32[2...) custom-call(bf16[256,2048]{1,0:T(8,128)(2,1)} %x_hbm.1, ...), custom_call_target="tpu_custom_call" | custom-call | tf_op jit(solution)/shard_map/front/pallas_call | solution.py:582
  50.6 116.0 %late.1 = (bf16[256,512]{1,0:T(8,128)(2,1)}, f32[256,512]{1,0:T(8,128)}, f32[3,4,64,512]{3,2,1,0:T(8,128)}, f32[5,64,256]{2,1,0:T(8,128)}, bf16[2,4,4,32,128]{4,3,2,1,0:T(8,128)(2,1)}, /*index=5*/f32[16,128]{1,0:T(8,128)}) custom-call(f32[256,512]{1,0:T(8,128)} %get-tuple-element.61.hidden_in, f32[256,2]{1,0:T(8,128)} %get-tuple-element.62.scales, ...), custom_call_target="tpu_custom_call" | custom-call | tf_op jit(solution)/shard_map/late/pallas_call | solution.py:1241
  166.6 3.6 %finish.1 = (bf16[256,512]{1,0:T(8,128)(2,1)}, f32[256,512]{1,0:T(8,128)}, f32[1,512]{1,0:T(1,128)}, f32[64,512]{1,0:T(8,128)}, f32[8,2048]{1,0:T(8,128)}, /*ind...) custom-call(bf16[256,512]{1,0:T(8,128)(2,1)} %get-tuple-element.74.b, ...), custom_call_target="tpu_custom_call" | custom-call | tf_op jit(solution)/shard_map/finish/pallas_call | solution.py:1369
